TPU v7x, 32 devices: a whole 2x2x4 slice. The times are simulated.
32 devices in a mesh: pipe: 4 (over z), row: 4 (over y, x), col: 2 (over core).
Axes of the slice: x: 2, y: 2, z: 4, core: 2. Of those that a mesh axis runs over, the one named last changes fastest.
Arguments:
- saved_in: bfloat16 [4, 32, 32, 2048], P('pipe', 'row', 'col'), may hold values from -400 to 400
- cotangent: bfloat16 [4, 32, 32, 2048], P('pipe', 'row', 'col'), may hold values from -6 to 6
- section_gains: float32 [4, 5, 2048], P('pipe'), may hold values from -8 to 8
Outputs:
- next_grad: bfloat16 [4, 32, 32, 2048], P('pipe', 'row', 'col')
All inputs are finite; a program needn't handle non-finite values.
Results may differ from a plain program's by a relative error of at most 0.0028.
The roundings to bfloat16 on the way count: a program that leaves them out, or rounds other values in their place, can miss the bound.
Values may be sent and summed in bfloat16 or wider, within the bound.
No kernel may reach another device: no remote copies, remote signals or barrier semaphores. Data moves between devices by JAX's collectives and lax.ppermute only.
A program may use at most 64 MiB of HBM per device.

v0:
```python
import functools
import math

import jax
import jax.numpy as jnp
from jax import lax
from jax.experimental import pallas as pl
from jax.experimental.pallas import tpu as pltpu
from jax.sharding import PartitionSpec as P

HEADS = 16
HEAD_DIM = 128
TILE = 8
SPAN = 5


NEGATIVE = -1e30
EPSILON = 1e-06


def passed_along(block, axis, distance):
    devices = range(lax.axis_size(axis))
    route = [(i - distance, i) for i in devices if i - distance in devices]
    return lax.ppermute(block, axis, route)


def to_tiles(image):
    lead = image.shape[:-3]
    height, width, channels = image.shape[-3:]
    count = len(lead)
    image = image.reshape(lead + (height // TILE, TILE, width // TILE, TILE, channels))
    order = tuple(range(count)) + (count, count + 2, count + 1, count + 3, count + 4)
    return image.transpose(order).reshape(
        lead + (height // TILE, width // TILE, TILE * TILE, channels)
    )


def from_tiles(tiled):
    tile_rows, tile_cols, area, channels = tiled.shape
    tiled = tiled.reshape(tile_rows, tile_cols, TILE, TILE, channels)
    return tiled.transpose(0, 2, 1, 3, 4).reshape(tile_rows * TILE, tile_cols * TILE, channels)


def windows(extended, tile_rows, tile_cols):
    return jnp.concatenate(
        [
            extended[row_off : row_off + tile_rows, col_off : col_off + tile_cols]
            for row_off in range(SPAN)
            for col_off in range(SPAN)
        ],
        axis=2,
    )


def key_valid(base_row, base_col, tile_rows, tile_cols, all_rows, all_cols):
    reach_tiles = SPAN // 2
    offsets = jnp.arange(SPAN, dtype=jnp.int32) - reach_tiles
    row_ids = base_row + jnp.arange(tile_rows, dtype=jnp.int32)[:, None] + offsets[None, :]
    col_ids = base_col + jnp.arange(tile_cols, dtype=jnp.int32)[:, None] + offsets[None, :]
    row_ok = (row_ids >= 0) & (row_ids < all_rows)
    col_ok = (col_ids >= 0) & (col_ids < all_cols)
    allowed = row_ok[:, None, :, None] & col_ok[None, :, None, :]
    return jnp.repeat(allowed.reshape(tile_rows, tile_cols, SPAN * SPAN), TILE * TILE, axis=2)


def project(normed, scales, factor):
    return (normed.astype(jnp.float32) * (scales * factor)).astype(jnp.bfloat16)


def normalize(image, scales):
    x_float = image.astype(jnp.float32)
    inverse = lax.rsqrt(jnp.mean(x_float * x_float, axis=-1, keepdims=True) + EPSILON)
    return (x_float, inverse, (x_float * inverse * scales).astype(jnp.bfloat16))


def widen(array, dim, reach, move):
    own = array.shape[dim]
    need = -(-reach // own)
    above = []
    below = []
    for step_by in range(need, 0, -1):
        lower_end = max(-step_by * own, -reach)
        upper_end = -(step_by - 1) * own
        piece = array
        above.append(move(piece, step_by))
    for step_by in range(1, need + 1):
        length = min((step_by + 1) * own, own + reach) - step_by * own
        piece = array
        below.append(move(piece, -step_by))
    return jnp.concatenate(above + [array] + below, axis=dim)


def halo_per_device(saved_in, cotangent, section_gains):
    scales = section_gains[0]
    reach_tiles = SPAN // 2
    reach_cells = TILE * reach_tiles
    factor = 1.0 / math.sqrt(HEAD_DIM)
    tile_rows = saved_in.shape[1] // TILE
    tile_cols = saved_in.shape[2] // TILE
    allowed = key_valid(
        lax.axis_index("row") * tile_rows,
        lax.axis_index("col") * tile_cols,
        tile_rows,
        tile_cols,
        tile_rows * lax.axis_size("row"),
        tile_cols * lax.axis_size("col"),
    )
    saved_float, saved_inverse, saved_normed = normalize(saved_in[0], scales[0])
    upstream_image = cotangent[0].astype(jnp.float32)
    grad_image = (upstream_image * scales[4]).astype(jnp.bfloat16)
    paired = jnp.stack([saved_normed, grad_image])

    def move_cols(piece, step_by):
        return passed_along(piece, "col", step_by)

    def move_rows(piece, step_by):
        return passed_along(piece, "row", step_by)

    paired_wide = widen(widen(paired, 2, reach_cells, move_cols), 1, reach_cells, move_rows)
    paired_ext = to_tiles(paired_wide)
    normed_ext = paired_ext[0]
    grad_ext = paired_ext[1]
    normed_tiles = to_tiles(saved_normed)
    grad_tiles = to_tiles(grad_image)
    stat_shape = (HEADS, tile_rows, tile_cols, TILE * TILE)

    def own_head(head, carry):
        dnormed, log_all, delta_all = carry
        start = head * HEAD_DIM

        def part(array):
            return lax.dynamic_slice_in_dim(array, start, HEAD_DIM, array.ndim - 1)

        queries = project(part(normed_tiles), part(scales[1]), factor)
        key_win = windows(project(part(normed_ext), part(scales[2]), 1.0), tile_rows, tile_cols)
        value_win = windows(project(part(normed_ext), part(scales[3]), 1.0), tile_rows, tile_cols)
        scores = jnp.einsum("ijqc,ijkc->ijqk", queries, key_win, preferred_element_type=jnp.float32)
        scores = jnp.where(allowed[:, :, None, :], scores, NEGATIVE)
        row_max = jnp.max(scores, axis=-1, keepdims=True)
        log_total = row_max + jnp.log(jnp.sum(jnp.exp(scores - row_max), axis=-1, keepdims=True))
        weights = jnp.exp(scores - log_total)
        rounded = weights.astype(jnp.bfloat16)
        output = jnp.einsum(
            "ijqk,ijkc->ijqc", rounded, value_win, preferred_element_type=jnp.float32
        )
        grads = part(grad_tiles)
        delta_sum = jnp.sum(grads.astype(jnp.float32) * output, axis=-1)
        prob_grad = jnp.einsum(
            "ijqc,ijkc->ijqk", grads, value_win, preferred_element_type=jnp.float32
        )
        dscore = (weights * (prob_grad - delta_sum[..., None])).astype(jnp.bfloat16)
        dquery = jnp.einsum("ijqk,ijkc->ijqc", dscore, key_win, preferred_element_type=jnp.float32)
        dnormed = lax.dynamic_update_slice_in_dim(
            dnormed, dquery * (part(scales[1]) * factor), start, 3
        )
        log_all = log_all.at[head].set(log_total[..., 0])
        delta_all = delta_all.at[head].set(delta_sum)
        return (dnormed, log_all, delta_all)

    dnormed, log_all, delta_all = lax.fori_loop(
        0,
        HEADS,
        own_head,
        (
            jnp.zeros(normed_tiles.shape, jnp.float32),
            jnp.zeros(stat_shape, jnp.float32),
            jnp.zeros(stat_shape, jnp.float32),
        ),
    )
    stat_tiles = jnp.concatenate([log_all, delta_all], axis=0).transpose(1, 2, 3, 0)

    def stat_cols(piece, step_by):
        return passed_along(piece, "col", step_by)

    def stat_rows(piece, step_by):
        return passed_along(piece, "row", step_by)

    stat_wide = widen(
        widen(from_tiles(stat_tiles), 1, reach_cells, stat_cols), 0, reach_cells, stat_rows
    )
    stat_win = windows(to_tiles(stat_wide), tile_rows, tile_cols)

    def far_head(head, dnormed):
        start = head * HEAD_DIM

        def part(array):
            return lax.dynamic_slice_in_dim(array, start, HEAD_DIM, array.ndim - 1)

        query_win = windows(
            project(part(normed_ext), part(scales[1]), factor), tile_rows, tile_cols
        )
        grad_win = windows(part(grad_ext), tile_rows, tile_cols)
        own_keys = project(part(normed_tiles), part(scales[2]), 1.0)
        own_values = project(part(normed_tiles), part(scales[3]), 1.0)
        far_log = lax.dynamic_index_in_dim(stat_win, head, 3, keepdims=False)
        far_delta = lax.dynamic_index_in_dim(stat_win, HEADS + head, 3, keepdims=False)
        scores = jnp.einsum(
            "ijqc,ijkc->ijqk", query_win, own_keys, preferred_element_type=jnp.float32
        )
        weights = jnp.exp(jnp.where(allowed[..., None], scores - far_log[..., None], NEGATIVE))
        prob_grad = jnp.einsum(
            "ijqc,ijkc->ijqk", grad_win, own_values, preferred_element_type=jnp.float32
        )
        dscore = (weights * (prob_grad - far_delta[..., None])).astype(jnp.bfloat16)
        key_grad = jnp.einsum(
            "ijqk,ijqc->ijkc", dscore, query_win, preferred_element_type=jnp.float32
        )
        dvalue = jnp.einsum(
            "ijqk,ijqc->ijkc",
            weights.astype(jnp.bfloat16),
            grad_win,
            preferred_element_type=jnp.float32,
        )
        terms = key_grad * part(scales[2]) + dvalue * part(scales[3])
        return lax.dynamic_update_slice_in_dim(dnormed, part(dnormed) + terms, start, 3)

    dnormed = lax.fori_loop(0, HEADS, far_head, dnormed)
    scaled = scales[0] * dnormed
    x_tiles = to_tiles(saved_float)
    inv_tiles = to_tiles(saved_inverse)
    upstream = to_tiles(upstream_image)
    image_grad = (
        upstream
        + inv_tiles * scaled
        - x_tiles
        * (inv_tiles * inv_tiles * inv_tiles)
        * jnp.mean(x_tiles * scaled, axis=-1, keepdims=True)
    )
    sent_back = passed_along(from_tiles(image_grad.astype(jnp.bfloat16)), "pipe", -1)
    return sent_back[None]


PIECES = 16


def crossing(sizes, row_step, col_step):
    rows, cols = sizes
    return [
        (row * cols + col, (row ^ row_step) * cols + (col ^ col_step))
        for row in range(rows)
        for col in range(cols)
    ]


def crossing_back(sizes, row_step):
    pipes, rows, cols = sizes
    return [
        (
            (pipe * rows + row) * cols + col,
            ((pipe - 1) % pipes * rows + (row ^ row_step)) * cols + col,
        )
        for pipe in range(pipes)
        for row in range(rows)
        for col in range(cols)
    ]


def row_to_column(row):
    return jnp.broadcast_to(row, (row.shape[1], row.shape[1])).T


def inverse_columns(pieces):
    pieces = pieces.astype(jnp.float32)
    return row_to_column(pieces[0:1] + pieces[1:2] + pieces[2:3])


def pack_kernel(rows, heads, x_hbm, c_hbm, *refs):
    outs = refs[: heads * 2]
    x_ref, c_ref, x_sem, c_sem = refs[heads * 2 :]
    tokens, channels = x_ref.shape
    row = lax.axis_index("row")
    col = lax.axis_index("col")
    parts = x_sem.shape[0]
    wide = channels // parts

    def fetch(source, target, sems, part):
        lanes = pl.ds(part * wide, wide)
        return pltpu.make_async_copy(source.at[:, lanes], target.at[:, lanes], sems.at[part])

    fetches = [fetch(x_hbm, x_ref, x_sem, part) for part in range(parts)]
    fetches += [fetch(c_hbm, c_ref, c_sem, part) for part in range(parts)]
    for copy in fetches:
        copy.start()
    squares = None
    for lane in range(0, channels, HEAD_DIM):
        if lane % wide == 0:
            fetches[lane // wide].wait()
        part = x_ref[:, lane : lane + HEAD_DIM].astype(jnp.float32)
        part = part * part
        squares = part if squares is None else squares + part
    for copy in fetches[parts:]:
        copy.wait()
    total = jnp.sum(squares.T, axis=0, keepdims=True)
    inverse = lax.rsqrt(total / channels + EPSILON)
    high = inverse.astype(jnp.bfloat16).astype(jnp.float32)
    mid = (inverse - high).astype(jnp.bfloat16).astype(jnp.float32)
    low = inverse - high - mid
    place = lax.broadcasted_iota(jnp.int32, (PIECES, tokens), 0)
    pieces = jnp.where(place == 0, high, jnp.where(place == 1, mid, jnp.where(place == 2, low, 0.0)))
    pieces = pieces.astype(jnp.bfloat16)
    for head in range(heads):
        for step in range(rows):
            for slot in range(2):
                first = ((row ^ step) * 2 + (col ^ slot)) * heads + head
                lanes = pl.ds(pl.multiple_of(first * HEAD_DIM, HEAD_DIM), HEAD_DIM)
                out = outs[head * 2 + slot]
                out[step, 0:tokens, :] = x_ref[:, lanes]
                out[step, tokens : 2 * tokens, :] = c_ref[:, lanes]
                if head == 0:
                    out[step, 2 * tokens :, :] = pieces


def attention_kernel(rows, heads, head, g_ref, *refs):
    held = rows + 1
    arrays, inverses = refs[0:held], refs[held : 2 * held]
    before_ref, keep_ref, give_ref, sums_ref = refs[2 * held : 2 * held + 4]
    q_s, k_s, kt_s, v_s, d_s, p_s, ds_s, s_s, dp_s, dk_s, dv_s, dq_s = refs[2 * held + 4 :]
    tokens = keep_ref.shape[1] // rows
    row = lax.axis_index("row")
    col = lax.axis_index("col")
    lanes = pl.ds(pl.multiple_of(((row * 2 + col) * heads + head) * HEAD_DIM, HEAD_DIM), HEAD_DIM)
    gn, gq, gk, gv, go = (g_ref[i : i + 1, lanes] for i in range(5))
    gq = gq * (1.0 / math.sqrt(HEAD_DIM))
    square = 2 * tokens
    pattern = (tokens // (2 * TILE), 2, TILE, tokens)
    query_right = (lax.broadcasted_iota(jnp.int32, pattern[1:], 2) // TILE) % 2
    key_right = lax.broadcasted_iota(jnp.int32, pattern[1:], 0)
    no_cap = float(jnp.finfo(jnp.float32).max)
    left_keys = jnp.where((key_right == 0) & (query_right == 1), NEGATIVE, no_cap)
    right_keys = jnp.where((key_right == 1) & (query_right == 0), NEGATIVE, no_cap)

    def capped(s, cap):
        return jnp.minimum(s.reshape(pattern), cap[None]).reshape(tokens, tokens)

    def block(step, slot):
        number, index = (slot, 0) if step == 0 else (step + 1, slot)
        ref = arrays[number]
        place = pl.multiple_of(((row ^ step) * 2 + (col ^ slot)) * tokens, tokens)
        x = ref[index, 0:tokens, :].astype(jnp.float32)
        c = ref[index, tokens : 2 * tokens, :].astype(jnp.float32)
        inverse = inverse_columns(inverses[number][index, 2 * tokens :, :])
        return pl.ds(place, tokens), x, c, inverse

    blocks = [(step, slot) for step in range(rows) for slot in range(2)]
    for step, slot in blocks:
        here, x, c, inverse = block(step, slot)
        normed = (x * inverse * gn).astype(jnp.bfloat16).astype(jnp.float32)
        q_s[here, :] = (normed * gq).astype(jnp.bfloat16)
        key = (normed * gk).astype(jnp.bfloat16)
        k_s[here, :] = key
        kt_s[:, here] = key.astype(jnp.float32).T.astype(jnp.bfloat16)
        v_s[here, :] = (normed * gv).astype(jnp.bfloat16)
        d_s[here, :] = (c * go).astype(jnp.bfloat16)

    contract_last = (((1,), (1,)), ((), ()))
    reach = SPAN // 2
    spans = []
    for at in range(rows):
        near = [r for r in range(rows) if abs(r - at) <= reach]
        spans.append((near[0] * square, (near[-1] + 1) * square))

    def own(at):
        return slice(at * square, (at + 1) * square)

    def cells(at):
        return [slice(start, start + square) for start in range(*spans[at], square)]

    def fold(combine, parts):
        total = parts[0]
        for part in parts[1:]:
            total = combine(total, part)
        return total

    def products(at, tops):
        buffer = at % 2
        q, d = q_s[own(at), :], d_s[own(at), :]
        left, right = [], []
        for cell in cells(at):
            s = lax.dot_general(k_s[cell, :], q, contract_last, preferred_element_type=jnp.float32)
            upper = slice(cell.start, cell.start + tokens)
            lower = slice(cell.start + tokens, cell.stop)
            upper_left, upper_right = s[0:tokens, 0:tokens], capped(s[0:tokens, tokens:], left_keys)
            lower_left, lower_right = capped(s[tokens:, 0:tokens], right_keys), s[tokens:, tokens:]
            s_s[buffer, upper, 0:tokens] = upper_left
            s_s[buffer, upper, tokens:] = upper_right
            s_s[buffer, lower, 0:tokens] = lower_left
            s_s[buffer, lower, tokens:] = lower_right
            left.append(jnp.max(jnp.maximum(upper_left, lower_left), axis=0, keepdims=True))
            right.append(jnp.max(jnp.maximum(upper_right, lower_right), axis=0, keepdims=True))
            yield
            dp_s[buffer, cell, :] = lax.dot_general(
                v_s[cell, :], d, contract_last, preferred_element_type=jnp.float32
            )
            yield
        tops[at] = jnp.concatenate([fold(jnp.maximum, left), fold(jnp.maximum, right)], axis=1)

    def softmax(at, tops):
        buffer = at % 2
        top = tops[at]
        sums = []
        for cell in cells(at):
            e = jnp.exp(s_s[buffer, cell, :] - top)
            s_s[buffer, cell, :] = e
            sums.append(jnp.sum(e, axis=0, keepdims=True))
            yield
        scale = 1.0 / fold(jnp.add, sums)
        sums = []
        for cell in cells(at):
            p = s_s[buffer, cell, :] * scale
            pb = p.astype(jnp.bfloat16)
            p_s[cell, own(at)] = pb
            sums.append(jnp.sum(pb.astype(jnp.float32) * dp_s[buffer, cell, :], axis=0, keepdims=True))
            yield
        delta = fold(jnp.add, sums)
        for cell in cells(at):
            p = s_s[buffer, cell, :] * scale
            ds_s[cell, own(at)] = (p * (dp_s[buffer, cell, :] - delta)).astype(jnp.bfloat16)
            yield

    def query_side(at):
        span = slice(*spans[at])
        dq = jnp.dot(kt_s[:, span], ds_s[span, own(at)], preferred_element_type=jnp.float32)
        yield
        dq_s[own(at), :] = dq.T
        yield

    def key_side(first, last):
        for at in range(rows):
            low, high = max(spans[at][0], first * square), min(spans[at][1], last * square)
            if low >= high:
                continue
            span = slice(low, high)
            dk = jnp.dot(ds_s[own(at), span], q_s[span, :], preferred_element_type=jnp.float32)
            fresh = low == spans[at][0]
            dk_s[own(at), :] = dk if fresh else dk_s[own(at), :] + dk
            yield
            dv = jnp.dot(p_s[own(at), span], d_s[span, :], preferred_element_type=jnp.float32)
            dv_s[own(at), :] = dv if fresh else dv_s[own(at), :] + dv
            yield

    def together(*works):
        works = list(works)
        while works:
            works = [work for work in works if next(work, works) is not works]


    def all_queries():
        dq = jnp.dot(kt_s[...], ds_s[...], preferred_element_type=jnp.float32)
        yield
        dq_s[...] = dq.T
        yield

    for at in range(rows):
        for other in range(rows):
            if abs(at - other) > reach:
                ds_s[own(at), own(other)] = jnp.zeros((square, square), jnp.bfloat16)
    tops = {}
    together(products(0, tops))
    for at in range(rows):
        works = [softmax(at, tops)]
        if at + 1 < rows:
            works.append(products(at + 1, tops))
        if at > 0:
            works += [key_side(at - 1, at)]
        together(*works)
    together(key_side(rows - 1, rows), all_queries())
    for step, slot in blocks:
        here, x, c, inverse = block(step, slot)
        scaled = gn * (dq_s[here, :] * gq + dk_s[here, :] * gk + dv_s[here, :] * gv)
        out = (keep_ref, give_ref)[slot]
        out[0, step * tokens : (step + 1) * tokens, :] = c + inverse * scaled
        out[1, step * tokens : (step + 1) * tokens, :] = x * (inverse * inverse * inverse)
        part = jnp.sum((x * scaled).T, axis=0, keepdims=True)
        index = slot * rows + step
        if head > 0:
            part = part + before_ref[index : index + 1, :]
        sums_ref[index : index + 1, :] = part


def finish_kernel(rows, heads, channels, *refs):
    parts = refs[0 : 2 * heads]
    sums = refs[2 * heads : 2 * heads + rows]
    outs = refs[2 * heads + rows :]
    tokens = outs[0].shape[0]
    col = lax.axis_index("col")
    for step in range(rows):
        total = sums[0][step : step + 1, :]
        for other in range(1, rows):
            total = total + sums[other][step ^ other : (step ^ other) + 1, :]
        mean = row_to_column(total / channels)
        here = slice(step * tokens, (step + 1) * tokens)
        for slot in range(2):
            for head in range(heads):
                part = parts[slot * heads + head]
                grad = part[0, here, :] - part[1, here, :] * mean
                start = pl.multiple_of(((col ^ slot) * heads + head) * HEAD_DIM, HEAD_DIM)
                outs[step][:, pl.ds(start, HEAD_DIM)] = grad.astype(jnp.bfloat16)


def collect_kernel(rows, *refs):
    out_ref = refs[rows]
    width = refs[0].shape[1]
    row = lax.axis_index("row")
    last = lax.axis_index("pipe") == lax.axis_size("pipe") - 1
    for step in range(rows):
        start = pl.multiple_of((row ^ step) * width, width)
        part = refs[step][...]
        out_ref[:, pl.ds(start, width)] = jnp.where(last, jnp.zeros_like(part), part)


def local_call(kernel, out_shape, scratch_shapes=(), in_specs=None):
    placed = {} if in_specs is None else {"in_specs": in_specs}
    return pl.pallas_call(
        kernel,
        out_shape=out_shape,
        **placed,
        scratch_shapes=scratch_shapes,
        compiler_params=pltpu.CompilerParams(vmem_limit_bytes=24 * 1024 * 1024),
    )


def near(arrays):
    return [pltpu.with_memory_space_constraint(array, pltpu.VMEM) for array in arrays]


def split_heads_per_device(saved_in, cotangent, section_gains):
    pipes, rows, cols = (lax.axis_size(name) for name in ("pipe", "row", "col"))
    channels = saved_in.shape[-1]
    tokens = saved_in.shape[1] * saved_in.shape[2]
    heads = channels // HEAD_DIM // (rows * cols)
    plane = ("row", "col")
    sizes = (rows, cols)
    bf, f32 = jnp.bfloat16, jnp.float32
    x = saved_in.reshape(tokens, channels)
    c = cotangent.reshape(tokens, channels)
    gains = section_gains[0]
    packets = []
    for head in range(heads):
        packets += [pltpu.VMEM((rows, 2 * tokens + (PIECES if head == 0 else 0), HEAD_DIM), bf)] * 2
    far = pl.BlockSpec(memory_space=pltpu.HBM)
    staged = [pltpu.VMEM((tokens, channels), bf)] * 2 + [pltpu.SemaphoreType.DMA((4,))] * 2
    packed = local_call(functools.partial(pack_kernel, rows, heads), packets, staged, [far, far])(
        pltpu.with_memory_space_constraint(x, pltpu.HBM), pltpu.with_memory_space_constraint(c, pltpu.HBM)
    )
    passed = [lax.ppermute(packed[2 * head + 1], plane, crossing(sizes, 0, 1)) for head in range(heads)]
    arrays = []
    for head in range(heads):
        own, other = packed[2 * head], passed[head]
        held = [own, other]
        packets = [jnp.stack([own[step], other[step]]) for step in range(1, rows)]
        if head > 0:
            packets, arrays[head - 1][2] = lax.optimization_barrier((packets, arrays[head - 1][2]))
        for step in range(1, rows):
            held.append(lax.ppermute(packets[step - 1], plane, crossing(sizes, step, 0)))
        arrays.append(held)
    count = rows * cols * tokens
    square = 2 * tokens
    scratch = [
        pltpu.VMEM((count, HEAD_DIM), bf),
        pltpu.VMEM((count, HEAD_DIM), bf),
        pltpu.VMEM((HEAD_DIM, count), bf),
        pltpu.VMEM((count, HEAD_DIM), bf),
        pltpu.VMEM((count, HEAD_DIM), bf),
        pltpu.VMEM((count, count), bf),
        pltpu.VMEM((count, count), bf),
        pltpu.VMEM((2, count, square), f32),
        pltpu.VMEM((2, count, square), f32),
        pltpu.VMEM((count, HEAD_DIM), f32),
        pltpu.VMEM((count, HEAD_DIM), f32),
        pltpu.VMEM((count, HEAD_DIM), f32),
    ]
    part = pltpu.VMEM((2, rows * tokens, HEAD_DIM), f32)
    sums_shape = pltpu.VMEM((2 * rows, tokens), f32)
    sums = jnp.zeros((2 * rows, tokens), f32)
    keep, give = [], []
    for head in range(heads):
        kept, given, sums = local_call(
            functools.partial(attention_kernel, rows, heads, head), [part, part, sums_shape], scratch
        )(gains, *near(arrays[head]), *near(arrays[0]), *near([sums]))
        keep.append(kept)
        give.append(given)
    own = sums[0:rows] + lax.ppermute(sums[rows:], plane, crossing(sizes, 0, 1))
    give, own = lax.optimization_barrier((give, own))
    got = [lax.ppermute(given, plane, crossing(sizes, 0, 1)) for given in give]
    totals = [own]
    for step in range(1, rows):
        totals.append(lax.ppermute(own, plane, crossing(sizes, step, 0)))
    piece = pltpu.VMEM((tokens, 2 * heads * HEAD_DIM), bf)
    grads = local_call(functools.partial(finish_kernel, rows, heads, channels), [piece] * rows)(
        *near(keep + got + totals)
    )
    sent = [
        lax.ppermute(grads[step], ("pipe",) + plane, crossing_back((pipes, rows, cols), step))
        for step in range(rows)
    ]
    out = local_call(
        functools.partial(collect_kernel, rows), jax.ShapeDtypeStruct((tokens, channels), bf)
    )(*near(sent))
    return out.reshape(saved_in.shape)


def per_device(saved_in, cotangent, section_gains):
    rows, cols = lax.axis_size("row"), lax.axis_size("col")
    block_fits = saved_in.shape[1] == TILE and saved_in.shape[2] == 2 * TILE
    devices_fit = cols == 2 and rows & (rows - 1) == 0 and HEADS % (rows * cols) == 0
    plan = split_heads_per_device if block_fits and devices_fit else halo_per_device
    return plan(saved_in, cotangent, section_gains)


def solution(mesh):
    return jax.shard_map(
        per_device,
        mesh=mesh,
        in_specs=(
            P("pipe", "row", "col", None),
            P("pipe", "row", "col", None),
            P("pipe", None, None),
        ),
        out_specs=P("pipe", "row", "col", None),
        check_vma=False,
    )
```

profile of v0, /device:TPU:0, one launch (start us, length us, event | category | flops | bytes accessed | tf_op | source)
XLA Modules:
  0.0 49.6 jit_solution(17937648193762291078)
XLA Ops:
  0.0 1.6 %shard_map.37 = (bf16[4,272,128]{2,1,0:T(8,128)(2,1)S(1)}, bf16[4,272,128]{2,1,0:T(8,128)(2,1)S(1)}, bf16[4,256,128]{2,1,0:T(8,128)(2,1)S(1)}, bf16[4,256,128]{2,1,0:T(8,128)(2,1)S(1)}) custom-call(bf16[128,2048]{1,0:T(8,128)(2,1)} %bitcast.8, bf16[128,2048]{1,0:T(8,128)(2,1)} %bitcast.9), custom_call_target="tpu_custom_call" | custom-call | tf_op jit(solution)/shard_map/pallas_call | solution.py:542
  1.6 0.5 %collective-permute-start.1 = (bf16[4,256,128]{2,1,0:T(8,128)(2,1)S(1)}, bf16[4,256,128]{2,1,0:T(8,128)(2,1)S(1)}, u32[]{:S(2)}, u32[]{:S(2)}) collective-permute-start(bf16[4,256,128]{2,1,0:T(8,128)(2,1)S(1)} %get-tuple-element.29), channel_id=1, source_target_pairs={{0,1},{1,0},{2,3},{3,2},{4,5},{5,4},{6,7},{7,6},{8,9},{9,8},{10,11... | collective-permute-start | bytes 786440 | tf_op jit(solution)/shard_map/ppermute | solution.py:545
  2.2 0.1 collective-permute-start
  2.3 1.0 %collective-permute-done.1.refs_1_ = bf16[4,256,128]{2,1,0:T(8,128)(2,1)S(1)} collective-permute-done((bf16[4,256,128]{2,1,0:T(8,128)(2,1)S(1)}, bf16[4,256,128]{2,1,0:T(8,128)(2,1)S(1)}, u32[]{:S(2)}, u32[]{:S(2)}) %collective-permute-start.1) | collective-permute-done | bytes 262176 | tf_op jit(solution)/shard_map/ppermute | solution.py:545
  3.4 0.3 collective-permute-done.refs_1_.refs_6_
  3.8 2.9 %collective-permute-start.2 = (bf16[2,272,128]{2,1,0:T(8,128)(2,1)S(1)}, bf16[2,272,128]{2,1,0:T(8,128)(2,1)S(1)}, u32[]{:S(2)}, u32[]{:S(2)}) collective-permute-start(bf16[2,272,128]{2,1,0:T(8,128)(2,1)S(1)} %pad_maximum_fusion), channel_id=1, source_target_pairs={{0,2},{1,3},{2,0},{3,1},{4,6},{5,7},{6,4},{7,5},{8,10},{9,11},{10,... | collective-permute-start | bytes 417800 | tf_op jit(solution)/shard_map/ppermute | solution.py:554
  6.7 1.6 %collective-permute-start.3 = (bf16[2,272,128]{2,1,0:T(8,128)(2,1)S(1)}, bf16[2,272,128]{2,1,0:T(8,128)(2,1)S(1)}, u32[]{:S(2)}, u32[]{:S(2)}) collective-permute-start(bf16[2,272,128]{2,1,0:T(8,128)(2,1)S(1)} %pad_maximum_fusion.1), channel_id=1, source_target_pairs={{0,4},{1,5},{2,6},{3,7},{4,0},{5,1},{6,2},{7,3},{8,12},{9,13},{10,... | collective-permute-start | bytes 417800 | tf_op jit(solution)/shard_map/ppermute | solution.py:554
  8.3 0.1 collective-permute-start.4
  8.4 0.0 copy-start
  8.4 2.3 %collective-permute-done.2.refs_2_.refs_7_ = bf16[2,272,128]{2,1,0:T(8,128)(2,1)S(1)} collective-permute-done((bf16[2,272,128]{2,1,0:T(8,128)(2,1)S(1)}, bf16[2,272,128]{2,1,0:T(8,128)(2,1)S(1)}, u32[]{:S(2)}, u32[]{:S(2)}) %collective-permute-start.2) | collective-permute-done | bytes 139296 | tf_op jit(solution)/shard_map/ppermute | solution.py:554
  10.8 2.4 %collective-permute-start.5 = (bf16[2,256,128]{2,1,0:T(8,128)(2,1)S(1)}, bf16[2,256,128]{2,1,0:T(8,128)(2,1)S(1)}, u32[]{:S(2)}, u32[]{:S(2)}) collective-permute-start(bf16[2,256,128]{2,1,0:T(8,128)(2,1)S(1)} %get-tuple-element.32), channel_id=1, source_target_pairs={{0,2},{1,3},{2,0},{3,1},{4,6},{5,7},{6,4},{7,5},{8,10},{9,11},{10,... | collective-permute-start | bytes 393224 | tf_op jit(solution)/shard_map/ppermute | solution.py:554
  13.2 1.5 %collective-permute-start.6 = (bf16[2,256,128]{2,1,0:T(8,128)(2,1)S(1)}, bf16[2,256,128]{2,1,0:T(8,128)(2,1)S(1)}, u32[]{:S(2)}, u32[]{:S(2)}) collective-permute-start(bf16[2,256,128]{2,1,0:T(8,128)(2,1)S(1)} %get-tuple-element.33), channel_id=1, source_target_pairs={{0,4},{1,5},{2,6},{3,7},{4,0},{5,1},{6,2},{7,3},{8,12},{9,13},{10,... | collective-permute-start | bytes 393224 | tf_op jit(solution)/shard_map/ppermute | solution.py:554
  14.7 0.0 collective-permute-start.7
  14.7 0.0 copy-done
  14.7 0.6 %collective-permute-done.3.refs_3_.refs_8_ = bf16[2,272,128]{2,1,0:T(8,128)(2,1)S(1)} collective-permute-done((bf16[2,272,128]{2,1,0:T(8,128)(2,1)S(1)}, bf16[2,272,128]{2,1,0:T(8,128)(2,1)S(1)}, u32[]{:S(2)}, u32[]{:S(2)}) %collective-permute-start.3) | collective-permute-done | bytes 139296 | tf_op jit(solution)/shard_map/ppermute | solution.py:554
  15.4 0.6 %collective-permute-done.4.refs_4_.refs_9_ = bf16[2,272,128]{2,1,0:T(8,128)(2,1)S(1)} collective-permute-done((bf16[2,272,128]{2,1,0:T(8,128)(2,1)S(1)}, bf16[2,272,128]{2,1,0:T(8,128)(2,1)S(1)}, u32[]{:S(2)}, u32[]{:S(2)}) %collective-permute-start.4) | collective-permute-done | bytes 139296 | tf_op jit(solution)/shard_map/ppermute | solution.py:554
  15.9 4.5 %shard_map.38 = (f32[2,512,128]{2,1,0:T(8,128)S(1)}, f32[2,512,128]{2,1,0:T(8,128)S(1)}, f32[8,128]{1,0:T(8,128)S(1)}) custom-call(f32[5,2048]{1,0:T(8,128)S(1)} %bitcast.6, bf16[4,272,128]{2,1,0:T(8,128)(2,1)S(1)} %get-tuple-element.26.refs_0_.refs_5_, bf16[4,272,128]{2,1,0:T(8,128)(2,1)S(1)} %collective-permute-done.refs_1_.refs_6_, ...), custom_call_target="tpu_custom_call" | custom-call | tf_op jit(solution)/shard_map/pallas_call | solution.py:577
  20.4 0.0 collective-permute-done.5.refs_2_
  20.4 0.5 %collective-permute-done.6.refs_3_ = bf16[2,256,128]{2,1,0:T(8,128)(2,1)S(1)} collective-permute-done((bf16[2,256,128]{2,1,0:T(8,128)(2,1)S(1)}, bf16[2,256,128]{2,1,0:T(8,128)(2,1)S(1)}, u32[]{:S(2)}, u32[]{:S(2)}) %collective-permute-start.6) | collective-permute-done | bytes 131104 | tf_op jit(solution)/shard_map/ppermute | solution.py:554
  20.9 0.0 collective-permute-done.7.refs_4_
  20.9 4.5 %shard_map.39 = (f32[2,512,128]{2,1,0:T(8,128)S(1)}, f32[2,512,128]{2,1,0:T(8,128)S(1)}, f32[8,128]{1,0:T(8,128)S(1)}) custom-call(f32[5,2048]{1,0:T(8,128)S(1)} %bitcast.7, bf16[4,256,128]{2,1,0:T(8,128)(2,1)S(1)} %get-tuple-element.28.refs_0_, bf16[4,256,128]{2,1,0:T(8,128)(2,1)S(1)} %collective-permute-done.1.refs_1_, ...), custom_call_target="tpu_custom_call" | custom-call | tf_op jit(solution)/shard_map/pallas_call | solution.py:577
  25.4 0.1 collective-permute-start.8
  25.5 1.1 %collective-permute-done.8 = f32[4,128]{1,0:T(4,128)S(1)} collective-permute-done((f32[4,128]{1,0:T(4,128)S(1)}, f32[4,128]{1,0:T(4,128)S(1)}, u32[]{:S(2)}, u32[]{:S(2)}) %collective-permute-start.8) | collective-permute-done | bytes 2080 | tf_op jit(solution)/shard_map/ppermute | solution.py:582
  26.7 0.2 collective-permute-start.9
  26.8 0.3 collective-permute-start.10
  27.2 1.4 %collective-permute-start.13 = (f32[4,128]{1,0:T(4,128)S(1)}, f32[4,128]{1,0:T(4,128)S(1)}, u32[]{:S(2)}, u32[]{:S(2)}) collective-permute-start(f32[4,128]{1,0:T(4,128)S(1)} %slice_add_fusion.refs_4_), channel_id=1, source_target_pairs={{0,6},{1,7},{2,4},{3,5},{4,2},{5,3},{6,0},{7,1},{8,14},{9,15},{10,... | collective-permute-start | bytes 6152 | tf_op jit(solution)/shard_map/ppermute | solution.py:587
  28.5 1.1 %collective-permute-start.12 = (f32[4,128]{1,0:T(4,128)S(1)}, f32[4,128]{1,0:T(4,128)S(1)}, u32[]{:S(2)}, u32[]{:S(2)}) collective-permute-start(f32[4,128]{1,0:T(4,128)S(1)} %slice_add_fusion.refs_4_), channel_id=1, source_target_pairs={{0,4},{1,5},{2,6},{3,7},{4,0},{5,1},{6,2},{7,3},{8,12},{9,13},{10,... | collective-permute-start | bytes 6152 | tf_op jit(solution)/shard_map/ppermute | solution.py:587
  29.7 1.0 %collective-permute-start.11 = (f32[4,128]{1,0:T(4,128)S(1)}, f32[4,128]{1,0:T(4,128)S(1)}, u32[]{:S(2)}, u32[]{:S(2)}) collective-permute-start(f32[4,128]{1,0:T(4,128)S(1)} %slice_add_fusion.refs_4_), channel_id=1, source_target_pairs={{0,2},{1,3},{2,0},{3,1},{4,6},{5,7},{6,4},{7,5},{8,10},{9,11},{10,... | collective-permute-start | bytes 6152 | tf_op jit(solution)/shard_map/ppermute | solution.py:587
  30.7 1.0 %collective-permute-done.13.refs_7_ = f32[4,128]{1,0:T(4,128)S(1)} collective-permute-done((f32[4,128]{1,0:T(4,128)S(1)}, f32[4,128]{1,0:T(4,128)S(1)}, u32[]{:S(2)}, u32[]{:S(2)}) %collective-permute-start.13) | collective-permute-done | bytes 2080 | tf_op jit(solution)/shard_map/ppermute | solution.py:587
  31.7 0.5 collective-permute-done.12.refs_6_
  32.1 1.1 %collective-permute-done.11.refs_5_ = f32[4,128]{1,0:T(4,128)S(1)} collective-permute-done((f32[4,128]{1,0:T(4,128)S(1)}, f32[4,128]{1,0:T(4,128)S(1)}, u32[]{:S(2)}, u32[]{:S(2)}) %collective-permute-start.11) | collective-permute-done | bytes 2080 | tf_op jit(solution)/shard_map/ppermute | solution.py:587
  33.2 0.0 collective-permute-done.9.refs_2_
  33.3 0.0 collective-permute-done.10.refs_3_
  33.3 0.2 shard_map.40
  33.5 3.7 %collective-permute-start.14 = (bf16[128,512]{1,0:T(8,128)(2,1)S(1)}, bf16[128,512]{1,0:T(8,128)(2,1)S(1)}, u32[]{:S(2)}, u32[]{:S(2)}) collective-permute-start(bf16[128,512]{1,0:T(8,128)(2,1)S(1)} %get-tuple-element.43), channel_id=1, source_target_pairs={{0,24},{1,25},{2,26},{3,27},{4,28},{5,29},{6,30},{7,31},{8,0},{9,1... | collective-permute-start | bytes 393224 | tf_op jit(solution)/shard_map/ppermute | solution.py:593
  37.2 0.9 %collective-permute-start.15 = (bf16[128,512]{1,0:T(8,128)(2,1)S(1)}, bf16[128,512]{1,0:T(8,128)(2,1)S(1)}, u32[]{:S(2)}, u32[]{:S(2)}) collective-permute-start(bf16[128,512]{1,0:T(8,128)(2,1)S(1)} %get-tuple-element.44), channel_id=1, source_target_pairs={{0,26},{1,27},{2,24},{3,25},{4,30},{5,31},{6,28},{7,29},{8,2},{9,3... | collective-permute-start | bytes 393224 | tf_op jit(solution)/shard_map/ppermute | solution.py:593
  38.0 1.3 %collective-permute-start.16 = (bf16[128,512]{1,0:T(8,128)(2,1)S(1)}, bf16[128,512]{1,0:T(8,128)(2,1)S(1)}, u32[]{:S(2)}, u32[]{:S(2)}) collective-permute-start(bf16[128,512]{1,0:T(8,128)(2,1)S(1)} %get-tuple-element.45), channel_id=1, source_target_pairs={{0,28},{1,29},{2,30},{3,31},{4,24},{5,25},{6,26},{7,27},{8,4},{9,5... | collective-permute-start | bytes 393224 | tf_op jit(solution)/shard_map/ppermute | solution.py:593
  39.3 1.0 %collective-permute-start.17 = (bf16[128,512]{1,0:T(8,128)(2,1)S(1)}, bf16[128,512]{1,0:T(8,128)(2,1)S(1)}, u32[]{:S(2)}, u32[]{:S(2)}) collective-permute-start(bf16[128,512]{1,0:T(8,128)(2,1)S(1)} %get-tuple-element.46), channel_id=1, source_target_pairs={{0,30},{1,31},{2,28},{3,29},{4,26},{5,27},{6,24},{7,25},{8,6},{9,7... | collective-permute-start | bytes 393224 | tf_op jit(solution)/shard_map/ppermute | solution.py:593
  40.3 0.8 %collective-permute-done.14.refs_0_ = bf16[128,512]{1,0:T(8,128)(2,1)S(1)} collective-permute-done((bf16[128,512]{1,0:T(8,128)(2,1)S(1)}, bf16[128,512]{1,0:T(8,128)(2,1)S(1)}, u32[]{:S(2)}, u32[]{:S(2)}) %collective-permute-start.14) | collective-permute-done | bytes 131104 | tf_op jit(solution)/shard_map/ppermute | solution.py:593
  41.1 3.4 %collective-permute-done.15.refs_1_ = bf16[128,512]{1,0:T(8,128)(2,1)S(1)} collective-permute-done((bf16[128,512]{1,0:T(8,128)(2,1)S(1)}, bf16[128,512]{1,0:T(8,128)(2,1)S(1)}, u32[]{:S(2)}, u32[]{:S(2)}) %collective-permute-start.15) | collective-permute-done | bytes 131104 | tf_op jit(solution)/shard_map/ppermute | solution.py:593
  44.5 2.6 %collective-permute-done.16.refs_2_ = bf16[128,512]{1,0:T(8,128)(2,1)S(1)} collective-permute-done((bf16[128,512]{1,0:T(8,128)(2,1)S(1)}, bf16[128,512]{1,0:T(8,128)(2,1)S(1)}, u32[]{:S(2)}, u32[]{:S(2)}) %collective-permute-start.16) | collective-permute-done | bytes 131104 | tf_op jit(solution)/shard_map/ppermute | solution.py:593
  47.1 1.7 %collective-permute-done.17.refs_3_ = bf16[128,512]{1,0:T(8,128)(2,1)S(1)} collective-permute-done((bf16[128,512]{1,0:T(8,128)(2,1)S(1)}, bf16[128,512]{1,0:T(8,128)(2,1)S(1)}, u32[]{:S(2)}, u32[]{:S(2)}) %collective-permute-start.17) | collective-permute-done | bytes 131104 | tf_op jit(solution)/shard_map/ppermute | solution.py:593
  48.8 0.9 %shard_map.41 = bf16[128,2048]{1,0:T(8,128)(2,1)} custom-call(bf16[128,512]{1,0:T(8,128)(2,1)S(1)} %collective-permute-done.14.refs_0_, bf16[128,512]{1,0:T(8,128)(2,1)S(1)} %collective-permute-done.15.refs_1_, bf16[128,512]{1,0:T(8,128)(2,1)S(1)} %collective-permute-done.16.refs_2_, bf16[128,512]{1,0:T(8,128)(2,1)S(1)} %collective-permute-done.17.refs_3_), custom_call_target="tpu_custom_call" | custom-call | tf_op jit(solution)/shard_map/pallas_call | solution.py:596
  (13 shorter events, 0.2 us)
Async XLA Ops:
  1.6 1.7 %collective-permute-start.1 = (bf16[4,256,128]{2,1,0:T(8,128)(2,1)S(1)}, bf16[4,256,128]{2,1,0:T(8,128)(2,1)S(1)}, u32[]{:S(2)}, u32[]{:S(2)}) collective-permute-start(bf16[4,256,128]{2,1,0:T(8,128)(2,1)S(1)} %get-tuple-element.29), channel_id=1, source_target_pairs={{0,1},{1,0},{2,3},{3,2},{4,5},{5,4},{6,7},{7,6},{8,9},{9,8},{10,11... | collective-permute-start | bytes 786440 | tf_op jit(solution)/shard_map/ppermute | solution.py:545
  2.2 1.6 %collective-permute-start = (bf16[4,272,128]{2,1,0:T(8,128)(2,1)S(1)}, bf16[4,272,128]{2,1,0:T(8,128)(2,1)S(1)}, u32[]{:S(2)}, u32[]{:S(2)}) collective-permute-start(bf16[4,272,128]{2,1,0:T(8,128)(2,1)S(1)} %get-tuple-element.27), channel_id=1, source_target_pairs={{0,1},{1,0},{2,3},{3,2},{4,5},{5,4},{6,7},{7,6},{8,9},{9,8},{10,11... | collective-permute-start | bytes 835592 | tf_op jit(solution)/shard_map/ppermute | solution.py:545
  3.8 7.0 %collective-permute-start.2 = (bf16[2,272,128]{2,1,0:T(8,128)(2,1)S(1)}, bf16[2,272,128]{2,1,0:T(8,128)(2,1)S(1)}, u32[]{:S(2)}, u32[]{:S(2)}) collective-permute-start(bf16[2,272,128]{2,1,0:T(8,128)(2,1)S(1)} %pad_maximum_fusion), channel_id=1, source_target_pairs={{0,2},{1,3},{2,0},{3,1},{4,6},{5,7},{6,4},{7,5},{8,10},{9,11},{10,... | collective-permute-start | bytes 417800 | tf_op jit(solution)/shard_map/ppermute | solution.py:554
  6.7 8.7 %collective-permute-start.3 = (bf16[2,272,128]{2,1,0:T(8,128)(2,1)S(1)}, bf16[2,272,128]{2,1,0:T(8,128)(2,1)S(1)}, u32[]{:S(2)}, u32[]{:S(2)}) collective-permute-start(bf16[2,272,128]{2,1,0:T(8,128)(2,1)S(1)} %pad_maximum_fusion.1), channel_id=1, source_target_pairs={{0,4},{1,5},{2,6},{3,7},{4,0},{5,1},{6,2},{7,3},{8,12},{9,13},{10,... | collective-permute-start | bytes 417800 | tf_op jit(solution)/shard_map/ppermute | solution.py:554
  8.3 7.6 %collective-permute-start.4 = (bf16[2,272,128]{2,1,0:T(8,128)(2,1)S(1)}, bf16[2,272,128]{2,1,0:T(8,128)(2,1)S(1)}, u32[]{:S(2)}, u32[]{:S(2)}) collective-permute-start(bf16[2,272,128]{2,1,0:T(8,128)(2,1)S(1)} %pad_maximum_fusion.2), channel_id=1, source_target_pairs={{0,6},{1,7},{2,4},{3,5},{4,2},{5,3},{6,0},{7,1},{8,14},{9,15},{10,... | collective-permute-start | bytes 417800 | tf_op jit(solution)/shard_map/ppermute | solution.py:554
  8.4 6.3 %copy-start = (f32[1,5,2048]{2,0,1:T(1,128)S(1)}, f32[1,5,2048]{2,0,1:T(1,128)}, u32[]{:S(2)}) copy-start(f32[1,5,2048]{2,0,1:T(1,128)} %param.5) | copy-start | bytes 122884
  10.8 9.6 %collective-permute-start.5 = (bf16[2,256,128]{2,1,0:T(8,128)(2,1)S(1)}, bf16[2,256,128]{2,1,0:T(8,128)(2,1)S(1)}, u32[]{:S(2)}, u32[]{:S(2)}) collective-permute-start(bf16[2,256,128]{2,1,0:T(8,128)(2,1)S(1)} %get-tuple-element.32), channel_id=1, source_target_pairs={{0,2},{1,3},{2,0},{3,1},{4,6},{5,7},{6,4},{7,5},{8,10},{9,11},{10,... | collective-permute-start | bytes 393224 | tf_op jit(solution)/shard_map/ppermute | solution.py:554
  13.2 7.7 %collective-permute-start.6 = (bf16[2,256,128]{2,1,0:T(8,128)(2,1)S(1)}, bf16[2,256,128]{2,1,0:T(8,128)(2,1)S(1)}, u32[]{:S(2)}, u32[]{:S(2)}) collective-permute-start(bf16[2,256,128]{2,1,0:T(8,128)(2,1)S(1)} %get-tuple-element.33), channel_id=1, source_target_pairs={{0,4},{1,5},{2,6},{3,7},{4,0},{5,1},{6,2},{7,3},{8,12},{9,13},{10,... | collective-permute-start | bytes 393224 | tf_op jit(solution)/shard_map/ppermute | solution.py:554
  14.7 6.2 %collective-permute-start.7 = (bf16[2,256,128]{2,1,0:T(8,128)(2,1)S(1)}, bf16[2,256,128]{2,1,0:T(8,128)(2,1)S(1)}, u32[]{:S(2)}, u32[]{:S(2)}) collective-permute-start(bf16[2,256,128]{2,1,0:T(8,128)(2,1)S(1)} %pad_maximum_fusion.5), channel_id=1, source_target_pairs={{0,6},{1,7},{2,4},{3,5},{4,2},{5,3},{6,0},{7,1},{8,14},{9,15},{10,... | collective-permute-start | bytes 393224 | tf_op jit(solution)/shard_map/ppermute | solution.py:554
  25.4 1.2 %collective-permute-start.8 = (f32[4,128]{1,0:T(4,128)S(1)}, f32[4,128]{1,0:T(4,128)S(1)}, u32[]{:S(2)}, u32[]{:S(2)}) collective-permute-start(f32[4,128]{1,0:T(4,128)S(1)} %slice.55), channel_id=1, source_target_pairs={{0,1},{1,0},{2,3},{3,2},{4,5},{5,4},{6,7},{7,6},{8,9},{9,8},{10,11... | collective-permute-start | bytes 6152 | tf_op jit(solution)/shard_map/ppermute | solution.py:582
  26.7 6.6 %collective-permute-start.9 = (f32[2,512,128]{2,1,0:T(8,128)S(1)}, f32[2,512,128]{2,1,0:T(8,128)S(1)}, u32[]{:S(2)}, u32[]{:S(2)}) collective-permute-start(f32[2,512,128]{2,1,0:T(8,128)S(1)} %get-tuple-element.40), channel_id=1, source_target_pairs={{0,1},{1,0},{2,3},{3,2},{4,5},{5,4},{6,7},{7,6},{8,9},{9,8},{10,11... | collective-permute-start | bytes 1572872 | tf_op jit(solution)/shard_map/ppermute | solution.py:584
  26.8 6.4 %collective-permute-start.10 = (f32[2,512,128]{2,1,0:T(8,128)S(1)}, f32[2,512,128]{2,1,0:T(8,128)S(1)}, u32[]{:S(2)}, u32[]{:S(2)}) collective-permute-start(f32[2,512,128]{2,1,0:T(8,128)S(1)} %get-tuple-element.41), channel_id=1, source_target_pairs={{0,1},{1,0},{2,3},{3,2},{4,5},{5,4},{6,7},{7,6},{8,9},{9,8},{10,11... | collective-permute-start | bytes 1572872 | tf_op jit(solution)/shard_map/ppermute | solution.py:584
  27.2 4.5 %collective-permute-start.13 = (f32[4,128]{1,0:T(4,128)S(1)}, f32[4,128]{1,0:T(4,128)S(1)}, u32[]{:S(2)}, u32[]{:S(2)}) collective-permute-start(f32[4,128]{1,0:T(4,128)S(1)} %slice_add_fusion.refs_4_), channel_id=1, source_target_pairs={{0,6},{1,7},{2,4},{3,5},{4,2},{5,3},{6,0},{7,1},{8,14},{9,15},{10,... | collective-permute-start | bytes 6152 | tf_op jit(solution)/shard_map/ppermute | solution.py:587
  28.5 3.6 %collective-permute-start.12 = (f32[4,128]{1,0:T(4,128)S(1)}, f32[4,128]{1,0:T(4,128)S(1)}, u32[]{:S(2)}, u32[]{:S(2)}) collective-permute-start(f32[4,128]{1,0:T(4,128)S(1)} %slice_add_fusion.refs_4_), channel_id=1, source_target_pairs={{0,4},{1,5},{2,6},{3,7},{4,0},{5,1},{6,2},{7,3},{8,12},{9,13},{10,... | collective-permute-start | bytes 6152 | tf_op jit(solution)/shard_map/ppermute | solution.py:587
  29.7 3.6 %collective-permute-start.11 = (f32[4,128]{1,0:T(4,128)S(1)}, f32[4,128]{1,0:T(4,128)S(1)}, u32[]{:S(2)}, u32[]{:S(2)}) collective-permute-start(f32[4,128]{1,0:T(4,128)S(1)} %slice_add_fusion.refs_4_), channel_id=1, source_target_pairs={{0,2},{1,3},{2,0},{3,1},{4,6},{5,7},{6,4},{7,5},{8,10},{9,11},{10,... | collective-permute-start | bytes 6152 | tf_op jit(solution)/shard_map/ppermute | solution.py:587
  33.5 7.6 %collective-permute-start.14 = (bf16[128,512]{1,0:T(8,128)(2,1)S(1)}, bf16[128,512]{1,0:T(8,128)(2,1)S(1)}, u32[]{:S(2)}, u32[]{:S(2)}) collective-permute-start(bf16[128,512]{1,0:T(8,128)(2,1)S(1)} %get-tuple-element.43), channel_id=1, source_target_pairs={{0,24},{1,25},{2,26},{3,27},{4,28},{5,29},{6,30},{7,31},{8,0},{9,1... | collective-permute-start | bytes 393224 | tf_op jit(solution)/shard_map/ppermute | solution.py:593
  37.2 7.3 %collective-permute-start.15 = (bf16[128,512]{1,0:T(8,128)(2,1)S(1)}, bf16[128,512]{1,0:T(8,128)(2,1)S(1)}, u32[]{:S(2)}, u32[]{:S(2)}) collective-permute-start(bf16[128,512]{1,0:T(8,128)(2,1)S(1)} %get-tuple-element.44), channel_id=1, source_target_pairs={{0,26},{1,27},{2,24},{3,25},{4,30},{5,31},{6,28},{7,29},{8,2},{9,3... | collective-permute-start | bytes 393224 | tf_op jit(solution)/shard_map/ppermute | solution.py:593
  38.0 9.1 %collective-permute-start.16 = (bf16[128,512]{1,0:T(8,128)(2,1)S(1)}, bf16[128,512]{1,0:T(8,128)(2,1)S(1)}, u32[]{:S(2)}, u32[]{:S(2)}) collective-permute-start(bf16[128,512]{1,0:T(8,128)(2,1)S(1)} %get-tuple-element.45), channel_id=1, source_target_pairs={{0,28},{1,29},{2,30},{3,31},{4,24},{5,25},{6,26},{7,27},{8,4},{9,5... | collective-permute-start | bytes 393224 | tf_op jit(solution)/shard_map/ppermute | solution.py:593
  39.3 9.4 %collective-permute-start.17 = (bf16[128,512]{1,0:T(8,128)(2,1)S(1)}, bf16[128,512]{1,0:T(8,128)(2,1)S(1)}, u32[]{:S(2)}, u32[]{:S(2)}) collective-permute-start(bf16[128,512]{1,0:T(8,128)(2,1)S(1)} %get-tuple-element.46), channel_id=1, source_target_pairs={{0,30},{1,31},{2,28},{3,29},{4,26},{5,27},{6,24},{7,25},{8,6},{9,7... | collective-permute-start | bytes 393224 | tf_op jit(solution)/shard_map/ppermute | solution.py:593
where the time goes:
time: 49.8 us; the launch traced here: 49.6 us
  starting transfers between devices  20 us (40%)
  waiting for transfers between devices  17.6 us (35%)
  Pallas kernels  11.7 us (23%)
    pallas_call x2, Pallas kernels, split_heads_per_device(): local_call(functools.partial(attention_kernel, rows, heads, head), [part,...  8.96 us
    ppermute x6, starting transfers between devices, split_heads_per_device(): lax.ppermute(packets[step - 1], plane, crossing(sizes, step, 0))  8.54 us
    ppermute x4, waiting for transfers between devices, split_heads_per_device(): lax.ppermute(grads[step], ('pipe',) + plane, crossing_back((pipes, rows,...  8.45 us
    ppermute x4, starting transfers between devices, split_heads_per_device(): lax.ppermute(grads[step], ('pipe',) + plane, crossing_back((pipes, rows,...  6.8 us
    ppermute x6, waiting for transfers between devices, split_heads_per_device(): lax.ppermute(packets[step - 1], plane, crossing(sizes, step, 0))  4.05 us
    ppermute x3, starting transfers between devices, split_heads_per_device(): totals.append(lax.ppermute(own, plane, crossing(sizes, step, 0)))  3.49 us
    ppermute x3, waiting for transfers between devices, split_heads_per_device(): totals.append(lax.ppermute(own, plane, crossing(sizes, step, 0)))  2.57 us
    pallas_call x1, Pallas kernels, split_heads_per_device(): local_call(functools.partial(pack_kernel, rows, heads), packets, staged,...  1.63 us
  transfers between devices with their start and end apart: 18, of which 14 were waited for; matrix products, arithmetic and copies ran while one was open for 0% of the time, Pallas kernels for 9%

commit v1 on v0

--- a/solution.py
+++ b/solution.py
@@ -233,6 +233,10 @@
 PIECES = 16
 
 
+EXTRA = 8
+SCALES = [2.0 ** (12 * power) for power in range(-8, 11)]
+
+
 def crossing(sizes, row_step, col_step):
     rows, cols = sizes
     return [
@@ -262,6 +266,29 @@
 def inverse_columns(pieces):
     pieces = pieces.astype(jnp.float32)
     return row_to_column(pieces[0:1] + pieces[1:2] + pieces[2:3])
+
+
+def scale_number(size):
+    return sum((size >= scale).astype(jnp.float32) for scale in SCALES[1:])
+
+
+def scale_value(number):
+    value = jnp.full(number.shape, SCALES[0], jnp.float32)
+    for index, scale in enumerate(SCALES[1:]):
+        value = jnp.where(number > index + 0.5, scale, value)
+    return value
+
+
+def inverse_row(x_ref, ready=lambda lane: None):
+    tokens, channels = x_ref.shape
+    squares = None
+    for lane in range(0, channels, HEAD_DIM):
+        ready(lane)
+        part = x_ref[:, lane : lane + HEAD_DIM].astype(jnp.float32)
+        part = part * part
+        squares = part if squares is None else squares + part
+    total = jnp.sum(squares.T, axis=0, keepdims=True)
+    return lax.rsqrt(total / channels + EPSILON)
 
 
 def pack_kernel(rows, heads, x_hbm, c_hbm, *refs):
@@ -281,17 +308,14 @@
     fetches += [fetch(c_hbm, c_ref, c_sem, part) for part in range(parts)]
     for copy in fetches:
         copy.start()
-    squares = None
-    for lane in range(0, channels, HEAD_DIM):
+
+    def ready(lane):
         if lane % wide == 0:
             fetches[lane // wide].wait()
-        part = x_ref[:, lane : lane + HEAD_DIM].astype(jnp.float32)
-        part = part * part
-        squares = part if squares is None else squares + part
+
+    inverse = inverse_row(x_ref, ready)
     for copy in fetches[parts:]:
         copy.wait()
-    total = jnp.sum(squares.T, axis=0, keepdims=True)
-    inverse = lax.rsqrt(total / channels + EPSILON)
     high = inverse.astype(jnp.bfloat16).astype(jnp.float32)
     mid = (inverse - high).astype(jnp.bfloat16).astype(jnp.float32)
     low = inverse - high - mid
@@ -310,12 +334,12 @@
                     out[step, 2 * tokens :, :] = pieces
 
 
-def attention_kernel(rows, heads, head, g_ref, *refs):
+def attend_kernel(rows, heads, head, g_ref, *refs):
     held = rows + 1
     arrays, inverses = refs[0:held], refs[held : 2 * held]
-    before_ref, keep_ref, give_ref, sums_ref = refs[2 * held : 2 * held + 4]
-    q_s, k_s, kt_s, v_s, d_s, p_s, ds_s, s_s, dp_s, dk_s, dv_s, dq_s = refs[2 * held + 4 :]
-    tokens = keep_ref.shape[1] // rows
+    keep_ref, give_ref = refs[2 * held : 2 * held + 2]
+    q_s, k_s, kt_s, v_s, d_s, p_s, ds_s, s_s, dp_s, dk_s, dv_s, dq_s = refs[2 * held + 2 :]
+    tokens = keep_ref.shape[1] - EXTRA
     row = lax.axis_index("row")
     col = lax.axis_index("col")
     lanes = pl.ds(pl.multiple_of(((row * 2 + col) * heads + head) * HEAD_DIM, HEAD_DIM), HEAD_DIM)
@@ -464,52 +488,77 @@
             works += [key_side(at - 1, at)]
         together(*works)
     together(key_side(rows - 1, rows), all_queries())
+    tops, shares = [], []
     for step, slot in blocks:
         here, x, c, inverse = block(step, slot)
         scaled = gn * (dq_s[here, :] * gq + dk_s[here, :] * gk + dv_s[here, :] * gv)
+        value = c + inverse * scaled
+        (keep_ref, give_ref)[slot][step, 0:tokens, :] = value
+        tops.append(jnp.max(jnp.abs(value), axis=0, keepdims=True))
+        shares.append(jnp.sum((x * scaled).T, axis=0, keepdims=True))
+    top = jnp.max(jnp.concatenate(tops, axis=0), axis=1, keepdims=True)
+    number = scale_number(jnp.broadcast_to(top, (len(blocks), tokens)))
+    shrink = 1.0 / scale_value(number)
+    share = jnp.concatenate(shares, axis=0)
+    share_number = scale_number(jnp.abs(share))
+    share = share / scale_value(share_number)
+    high = share.astype(jnp.bfloat16).astype(jnp.float32)
+    mid = (share - high).astype(jnp.bfloat16).astype(jnp.float32)
+    low = share - high - mid
+    place = lax.broadcasted_iota(jnp.int32, (EXTRA, tokens), 0)
+    for index, (step, slot) in enumerate(blocks):
         out = (keep_ref, give_ref)[slot]
-        out[0, step * tokens : (step + 1) * tokens, :] = c + inverse * scaled
-        out[1, step * tokens : (step + 1) * tokens, :] = x * (inverse * inverse * inverse)
-        part = jnp.sum((x * scaled).T, axis=0, keepdims=True)
-        index = slot * rows + step
-        if head > 0:
-            part = part + before_ref[index : index + 1, :]
-        sums_ref[index : index + 1, :] = part
-
-
-def finish_kernel(rows, heads, channels, *refs):
-    parts = refs[0 : 2 * heads]
-    sums = refs[2 * heads : 2 * heads + rows]
-    outs = refs[2 * heads + rows :]
-    tokens = outs[0].shape[0]
+        at = slice(index, index + 1)
+        out[step, 0:tokens, :] = out[step, 0:tokens, :] * shrink[at]
+        extra = jnp.zeros((EXTRA, tokens), jnp.float32)
+        for line, row_of in enumerate((number, share_number, high, mid, low)):
+            extra = jnp.where(place == line, row_of[at], extra)
+        out[step, tokens:, :] = extra
+
+
+def attention_kernel(*operands):
+    @pl.when(lax.axis_index("pipe") > 0)
+    def _():
+        attend_kernel(*operands)
+
+
+def cube_kernel(x_ref, out_ref):
+    inverse = inverse_row(x_ref)
+    out_ref[...] = row_to_column(inverse * inverse * inverse)
+
+
+def collect_kernel(rows, heads, x_ref, cube_ref, *refs):
+    units = refs[:rows]
+    out_hbm, out_ref, sems = refs[rows:]
+    tokens, channels = x_ref.shape
+    row = lax.axis_index("row")
     col = lax.axis_index("col")
+    last = lax.axis_index("pipe") == lax.axis_size("pipe") - 1
+    total, scales = None, {}
     for step in range(rows):
-        total = sums[0][step : step + 1, :]
-        for other in range(1, rows):
-            total = total + sums[other][step ^ other : (step ^ other) + 1, :]
-        mean = row_to_column(total / channels)
-        here = slice(step * tokens, (step + 1) * tokens)
-        for slot in range(2):
-            for head in range(heads):
-                part = parts[slot * heads + head]
-                grad = part[0, here, :] - part[1, here, :] * mean
-                start = pl.multiple_of(((col ^ slot) * heads + head) * HEAD_DIM, HEAD_DIM)
-                outs[step][:, pl.ds(start, HEAD_DIM)] = grad.astype(jnp.bfloat16)
-
-
-def collect_kernel(rows, *refs):
-    out_ref = refs[rows]
-    width = refs[0].shape[1]
-    row = lax.axis_index("row")
-    last = lax.axis_index("pipe") == lax.axis_size("pipe") - 1
+        for slot in range(2 * heads):
+            extra = units[step][slot, tokens : tokens + 8, :]
+            value = scale_value(extra)
+            scales[step, slot] = value[0:1]
+            share = (extra[2:3] + extra[3:4] + extra[4:5]) * value[1:2]
+            total = share if total is None else total + share
+    weight = cube_ref[...] * row_to_column(total / channels)
+    wide = 2 * heads * HEAD_DIM
+    copies = []
     for step in range(rows):
-        start = pl.multiple_of((row ^ step) * width, width)
-        part = refs[step][...]
-        out_ref[:, pl.ds(start, width)] = jnp.where(last, jnp.zeros_like(part), part)
-
-
-def local_call(kernel, out_shape, scratch_shapes=(), in_specs=None):
-    placed = {} if in_specs is None else {"in_specs": in_specs}
+        for slot in range(2 * heads):
+            first = ((row ^ step) * 2 + (col ^ (slot // heads))) * heads + slot % heads
+            lanes = pl.ds(pl.multiple_of(first * HEAD_DIM, HEAD_DIM), HEAD_DIM)
+            grad = units[step][slot, 0:tokens, :] * scales[step, slot] - x_ref[:, lanes].astype(jnp.float32) * weight
+            out_ref[:, lanes] = jnp.where(last, 0.0, grad).astype(jnp.bfloat16)
+        lanes = pl.ds(pl.multiple_of((row ^ step) * wide, wide), wide)
+        copies.append(pltpu.make_async_copy(out_ref.at[:, lanes], out_hbm.at[:, lanes], sems.at[step]))
+        copies[-1].start()
+    for copy in copies:
+        copy.wait()
+
+
+def local_call(kernel, out_shape, scratch_shapes=(), **placed):
     return pl.pallas_call(
         kernel,
         out_shape=out_shape,
@@ -539,7 +588,7 @@
         packets += [pltpu.VMEM((rows, 2 * tokens + (PIECES if head == 0 else 0), HEAD_DIM), bf)] * 2
     far = pl.BlockSpec(memory_space=pltpu.HBM)
     staged = [pltpu.VMEM((tokens, channels), bf)] * 2 + [pltpu.SemaphoreType.DMA((4,))] * 2
-    packed = local_call(functools.partial(pack_kernel, rows, heads), packets, staged, [far, far])(
+    packed = local_call(functools.partial(pack_kernel, rows, heads), packets, staged, in_specs=[far, far])(
         pltpu.with_memory_space_constraint(x, pltpu.HBM), pltpu.with_memory_space_constraint(c, pltpu.HBM)
     )
     passed = [lax.ppermute(packed[2 * head + 1], plane, crossing(sizes, 0, 1)) for head in range(heads)]
@@ -569,33 +618,31 @@
         pltpu.VMEM((count, HEAD_DIM), f32),
         pltpu.VMEM((count, HEAD_DIM), f32),
     ]
-    part = pltpu.VMEM((2, rows * tokens, HEAD_DIM), f32)
-    sums_shape = pltpu.VMEM((2 * rows, tokens), f32)
-    sums = jnp.zeros((2 * rows, tokens), f32)
-    keep, give = [], []
+    behind = [(pipe, (pipe - 1) % pipes) for pipe in range(pipes)]
+    arrays[0][1], free_x = lax.optimization_barrier((arrays[0][1], x))
+    x_ahead = lax.ppermute(free_x, "pipe", behind)
+    part = pltpu.VMEM((rows, tokens + EXTRA, HEAD_DIM), f32)
+    keep, got = [], []
     for head in range(heads):
-        kept, given, sums = local_call(
-            functools.partial(attention_kernel, rows, heads, head), [part, part, sums_shape], scratch
-        )(gains, *near(arrays[head]), *near(arrays[0]), *near([sums]))
-        keep.append(kept)
-        give.append(given)
-    own = sums[0:rows] + lax.ppermute(sums[rows:], plane, crossing(sizes, 0, 1))
-    give, own = lax.optimization_barrier((give, own))
-    got = [lax.ppermute(given, plane, crossing(sizes, 0, 1)) for given in give]
-    totals = [own]
-    for step in range(1, rows):
-        totals.append(lax.ppermute(own, plane, crossing(sizes, step, 0)))
-    piece = pltpu.VMEM((tokens, 2 * heads * HEAD_DIM), bf)
-    grads = local_call(functools.partial(finish_kernel, rows, heads, channels), [piece] * rows)(
-        *near(keep + got + totals)
-    )
-    sent = [
-        lax.ppermute(grads[step], ("pipe",) + plane, crossing_back((pipes, rows, cols), step))
-        for step in range(rows)
-    ]
+        kept, given = local_call(
+            functools.partial(attention_kernel, rows, heads, head), [part, part], scratch
+        )(gains, *near(arrays[head]), *near(arrays[0]))
+        if head == heads - 1:
+            given, x_ahead = lax.optimization_barrier((given, x_ahead))
+        keep.append(kept.astype(jnp.float16))
+        got.append(lax.ppermute(given.astype(jnp.float16), plane, crossing(sizes, 0, 1)))
+    units = []
+    for step in range(rows):
+        sent = jnp.stack([unit[step] for unit in keep + got])
+        sent = lax.ppermute(sent, ("pipe",) + plane, crossing_back((pipes, rows, cols), step))
+        units.append(sent.astype(f32))
+    cube = local_call(cube_kernel, pltpu.VMEM((tokens, HEAD_DIM), f32))(*near([x_ahead]))
     out = local_call(
-        functools.partial(collect_kernel, rows), jax.ShapeDtypeStruct((tokens, channels), bf)
-    )(*near(sent))
+        functools.partial(collect_kernel, rows, heads),
+        jax.ShapeDtypeStruct((tokens, channels), bf),
+        [pltpu.VMEM((tokens, channels), bf), pltpu.SemaphoreType.DMA((rows,))],
+        out_specs=far,
+    )(*near([x_ahead, cube] + units))
     return out.reshape(saved_in.shape)
 
 

time: 49.8 us -> 46.4 us (0.932)
  Pallas kernels: 11.7 us -> 3.12 us
  starting transfers between devices: 20 us -> 23.8 us
  local copies, waits for them, and re-layouts: 0.09 us -> 0.96 us
    pallas_call x2, Pallas kernels: 8.96 us -> 0.01 us  [split_heads_per_device(): local_call(functools.partial(attention_kernel, rows, heads, head), [part,...]
    ppermute x10 -> x7, starting transfers between devices: 10.9 us -> 14.5 us  [the longest x4 10.3 us: split_heads_per_device(): lax.ppermute(sent, ('pipe',) + plane, crossing_back((pipes, rows, cols),...]
    ppermute x6, waiting for transfers between devices: 4.05 us -> 4.97 us  [split_heads_per_device(): lax.ppermute(packets[step - 1], plane, crossing(sizes, step, 0))]
    unnamed x3 -> x5, local copies, waits for them, and re-layouts: 0.02 us -> 0.77 us
    ppermute x2, waiting for transfers between devices: 1.39 us -> 0.64 us  [split_heads_per_device(): lax.ppermute(packed[2 * head + 1], plane, crossing(sizes, 0, 1))]
    ppermute x10 -> x7, waiting for transfers between devices: 12.2 us -> 12 us  [the longest x4 9.38 us: split_heads_per_device(): lax.ppermute(sent, ('pipe',) + plane, crossing_back((pipes, rows, cols),...]
  transfers between devices with their start and end apart: 18 -> 15, of which waited for: 14 -> 9; matrix products, arithmetic and copies ran while one was open for 0% -> 1% of each run, Pallas kernels for 9% -> 1%
where the time goes in v1:
time: 46.4 us; the launch traced here: 46.2 us
  starting transfers between devices  23.8 us (51%)
  waiting for transfers between devices  17.6 us (38%)
  Pallas kernels  3.12 us (7%)
  local copies, waits for them, and re-layouts  0.96 us (2%)
    ppermute x4, starting transfers between devices, split_heads_per_device(): lax.ppermute(sent, ('pipe',) + plane, crossing_back((pipes, rows, cols),...  10.3 us
    ppermute x4, waiting for transfers between devices, split_heads_per_device(): lax.ppermute(sent, ('pipe',) + plane, crossing_back((pipes, rows, cols),...  9.38 us
    ppermute x6, starting transfers between devices, split_heads_per_device(): lax.ppermute(packets[step - 1], plane, crossing(sizes, step, 0))  8.69 us
    ppermute x6, waiting for transfers between devices, split_heads_per_device(): lax.ppermute(packets[step - 1], plane, crossing(sizes, step, 0))  4.97 us
    ppermute x1, starting transfers between devices, split_heads_per_device(): x_ahead = lax.ppermute(free_x, 'pipe', behind)  4.11 us
    pallas_call x1, Pallas kernels, split_heads_per_device(): local_call(functools.partial(pack_kernel, rows, heads), packets, staged,...  1.72 us
    ppermute x2, waiting for transfers between devices, split_heads_per_device(): lax.ppermute(given.astype(jnp.float16), plane, crossing(sizes, 0, 1))  1.3 us
    ppermute x1, waiting for transfers between devices, split_heads_per_device(): x_ahead = lax.ppermute(free_x, 'pipe', behind)  1.3 us
  transfers between devices with their start and end apart: 15, of which 9 were waited for; matrix products, arithmetic and copies ran while one was open for 1% of the time, Pallas kernels for 1%

profile of v1, /device:TPU:0, one launch (start us, length us, event | category | flops | bytes accessed | tf_op | source)
XLA Modules:
  0.0 46.2 jit_solution(15694898489080754297)
XLA Ops:
  0.0 1.7 %shard_map.37 = (bf16[4,272,128]{2,1,0:T(8,128)(2,1)S(1)}, bf16[4,272,128]{2,1,0:T(8,128)(2,1)S(1)}, bf16[4,256,128]{2,1,0:T(8,128)(2,1)S(1)}, bf16[4,256,128]{2,1,0:T(8,128)(2,1)S(1)}) custom-call(bf16[128,2048]{1,0:T(8,128)(2,1)} %bitcast.9, bf16[128,2048]{1,0:T(8,128)(2,1)} %bitcast.8), custom_call_target="tpu_custom_call" | custom-call | tf_op jit(solution)/shard_map/pallas_call | solution.py:591
  1.7 0.5 %collective-permute-start = (bf16[4,256,128]{2,1,0:T(8,128)(2,1)S(1)}, bf16[4,256,128]{2,1,0:T(8,128)(2,1)S(1)}, u32[]{:S(2)}, u32[]{:S(2)}) collective-permute-start(bf16[4,256,128]{2,1,0:T(8,128)(2,1)S(1)} %get-tuple-element.22), channel_id=1, source_target_pairs={{0,1},{1,0},{2,3},{3,2},{4,5},{5,4},{6,7},{7,6},{8,9},{9,8},{10,11... | collective-permute-start | bytes 786440 | tf_op jit(solution)/shard_map/ppermute | solution.py:594
  2.2 0.1 collective-permute-start.1
  2.3 0.0 copy-start.1
  2.4 0.7 %copy-done.1 = f32[1,5,2048]{2,0,1:T(1,128)S(1)} copy-done((f32[1,5,2048]{2,0,1:T(1,128)S(1)}, f32[1,5,2048]{2,0,1:T(1,128)}, u32[]{:S(2)}) %copy-start.1) | copy-done | bytes 40984
  3.1 0.3 collective-permute-done.operands_2_
  3.4 0.4 collective-permute-done.1.operands_7_.operands_2_
  3.8 2.9 %collective-permute-start.2 = (bf16[2,272,128]{2,1,0:T(8,128)(2,1)S(1)}, bf16[2,272,128]{2,1,0:T(8,128)(2,1)S(1)}, u32[]{:S(2)}, u32[]{:S(2)}) collective-permute-start(bf16[2,272,128]{2,1,0:T(8,128)(2,1)S(1)} %pad_maximum_fusion), channel_id=1, source_target_pairs={{0,2},{1,3},{2,0},{3,1},{4,6},{5,7},{6,4},{7,5},{8,10},{9,11},{10,... | collective-permute-start | bytes 417800 | tf_op jit(solution)/shard_map/ppermute | solution.py:603
  6.8 0.0 copy-start
  6.8 1.6 %collective-permute-start.6 = (bf16[2,272,128]{2,1,0:T(8,128)(2,1)S(1)}, bf16[2,272,128]{2,1,0:T(8,128)(2,1)S(1)}, u32[]{:S(2)}, u32[]{:S(2)}) collective-permute-start(bf16[2,272,128]{2,1,0:T(8,128)(2,1)S(1)} %pad_maximum_fusion.1), channel_id=1, source_target_pairs={{0,4},{1,5},{2,6},{3,7},{4,0},{5,1},{6,2},{7,3},{8,12},{9,13},{10,... | collective-permute-start | bytes 417800 | tf_op jit(solution)/shard_map/ppermute | solution.py:603
  8.4 0.1 collective-permute-start.7
  8.5 0.0 copy-done
  8.5 4.1 %collective-permute-start.8 = (bf16[128,2048]{1,0:T(8,128)(2,1)S(1)}, bf16[128,2048]{1,0:T(8,128)(2,1)S(1)}, u32[]{:S(2)}, u32[]{:S(2)}) collective-permute-start(bf16[128,2048]{1,0:T(8,128)(2,1)S(1)} %bitcast.10), channel_id=1, source_target_pairs={{0,24},{8,0},{16,8},{24,16},{1,25},{9,1},{17,9},{25,17},{2,26},{10... | collective-permute-start | bytes 1572872 | tf_op jit(solution)/shard_map/ppermute | solution.py:623
  12.6 0.0 collective-permute-done.2.operands_8_.operands_3_
  12.7 1.6 %collective-permute-start.3 = (bf16[2,256,128]{2,1,0:T(8,128)(2,1)S(1)}, bf16[2,256,128]{2,1,0:T(8,128)(2,1)S(1)}, u32[]{:S(2)}, u32[]{:S(2)}) collective-permute-start(bf16[2,256,128]{2,1,0:T(8,128)(2,1)S(1)} %get-tuple-element.25), channel_id=1, source_target_pairs={{0,2},{1,3},{2,0},{3,1},{4,6},{5,7},{6,4},{7,5},{8,10},{9,11},{10,... | collective-permute-start | bytes 393224 | tf_op jit(solution)/shard_map/ppermute | solution.py:603
  14.2 1.5 %collective-permute-start.4 = (bf16[2,256,128]{2,1,0:T(8,128)(2,1)S(1)}, bf16[2,256,128]{2,1,0:T(8,128)(2,1)S(1)}, u32[]{:S(2)}, u32[]{:S(2)}) collective-permute-start(bf16[2,256,128]{2,1,0:T(8,128)(2,1)S(1)} %get-tuple-element.26), channel_id=1, source_target_pairs={{0,4},{1,5},{2,6},{3,7},{4,0},{5,1},{6,2},{7,3},{8,12},{9,13},{10,... | collective-permute-start | bytes 393224 | tf_op jit(solution)/shard_map/ppermute | solution.py:603
  15.7 0.0 collective-permute-done.6.operands_9_.operands_4_
  15.7 1.0 %collective-permute-start.5 = (bf16[2,256,128]{2,1,0:T(8,128)(2,1)S(1)}, bf16[2,256,128]{2,1,0:T(8,128)(2,1)S(1)}, u32[]{:S(2)}, u32[]{:S(2)}) collective-permute-start(bf16[2,256,128]{2,1,0:T(8,128)(2,1)S(1)} %pad_maximum_fusion.9), channel_id=1, source_target_pairs={{0,6},{1,7},{2,4},{3,5},{4,2},{5,3},{6,0},{7,1},{8,14},{9,15},{10,... | collective-permute-start | bytes 393224 | tf_op jit(solution)/shard_map/ppermute | solution.py:603
  16.8 0.0 collective-permute-done.7.operands_10_.operands_5_
  16.8 0.1 collective-permute-start.9
  16.9 0.7 %collective-permute-done.3.operands_3_ = bf16[2,256,128]{2,1,0:T(8,128)(2,1)S(1)} collective-permute-done((bf16[2,256,128]{2,1,0:T(8,128)(2,1)S(1)}, bf16[2,256,128]{2,1,0:T(8,128)(2,1)S(1)}, u32[]{:S(2)}, u32[]{:S(2)}) %collective-permute-start.3) | collective-permute-done | bytes 131104 | tf_op jit(solution)/shard_map/ppermute | solution.py:603
  17.7 4.2 %collective-permute-done.4.operands_4_ = bf16[2,256,128]{2,1,0:T(8,128)(2,1)S(1)} collective-permute-done((bf16[2,256,128]{2,1,0:T(8,128)(2,1)S(1)}, bf16[2,256,128]{2,1,0:T(8,128)(2,1)S(1)}, u32[]{:S(2)}, u32[]{:S(2)}) %collective-permute-start.4) | collective-permute-done | bytes 131104 | tf_op jit(solution)/shard_map/ppermute | solution.py:603
  21.9 0.0 collective-permute-done.5.operands_5_
  22.0 1.3 %collective-permute-done.8.x_ref = bf16[128,2048]{1,0:T(8,128)(2,1)S(1)} collective-permute-done((bf16[128,2048]{1,0:T(8,128)(2,1)S(1)}, bf16[128,2048]{1,0:T(8,128)(2,1)S(1)}, u32[]{:S(2)}, u32[]{:S(2)}) %collective-permute-start.8) | collective-permute-done | bytes 524320 | tf_op jit(solution)/shard_map/ppermute | solution.py:623
  23.3 0.1 collective-permute-start.10
  23.4 0.0 collective-permute-done.9
  23.4 1.3 %collective-permute-done.10 = f16[4,136,128]{2,1,0:T(8,128)(2,1)S(1)} collective-permute-done((f16[4,136,128]{2,1,0:T(8,128)(2,1)S(1)}, f16[4,136,128]{2,1,0:T(8,128)(2,1)S(1)}, u32[]{:S(2)}, u32[]{:S(2)}) %collective-permute-start.10) | collective-permute-done | bytes 139296 | tf_op jit(solution)/shard_map/ppermute | solution.py:633
  24.8 0.1 pad_maximum_fusion.3
  24.8 6.7 %collective-permute-start.11 = (f16[4,136,128]{2,1,0:T(8,128)(2,1)S(1)}, f16[4,136,128]{2,1,0:T(8,128)(2,1)S(1)}, u32[]{:S(2)}, u32[]{:S(2)}) collective-permute-start(f16[4,136,128]{2,1,0:T(8,128)(2,1)S(1)} %pad_maximum_fusion.3), channel_id=1, source_target_pairs={{0,24},{1,25},{2,26},{3,27},{4,28},{5,29},{6,30},{7,31},{8,0},{9,1... | collective-permute-start | bytes 417800 | tf_op jit(solution)/shard_map/ppermute | solution.py:637
  31.6 0.1 pad_maximum_fusion.4
  31.6 2.1 %collective-permute-start.12 = (f16[4,136,128]{2,1,0:T(8,128)(2,1)S(1)}, f16[4,136,128]{2,1,0:T(8,128)(2,1)S(1)}, u32[]{:S(2)}, u32[]{:S(2)}) collective-permute-start(f16[4,136,128]{2,1,0:T(8,128)(2,1)S(1)} %pad_maximum_fusion.4), channel_id=1, source_target_pairs={{0,26},{1,27},{2,24},{3,25},{4,30},{5,31},{6,28},{7,29},{8,2},{9,3... | collective-permute-start | bytes 417800 | tf_op jit(solution)/shard_map/ppermute | solution.py:637
  33.7 0.1 pad_maximum_fusion.5
  33.7 0.1 collective-permute-start.13
  33.8 0.1 pad_maximum_fusion.6
  33.9 1.4 %collective-permute-start.14 = (f16[4,136,128]{2,1,0:T(8,128)(2,1)S(1)}, f16[4,136,128]{2,1,0:T(8,128)(2,1)S(1)}, u32[]{:S(2)}, u32[]{:S(2)}) collective-permute-start(f16[4,136,128]{2,1,0:T(8,128)(2,1)S(1)} %pad_maximum_fusion.6), channel_id=1, source_target_pairs={{0,30},{1,31},{2,28},{3,29},{4,26},{5,27},{6,24},{7,25},{8,6},{9,7... | collective-permute-start | bytes 417800 | tf_op jit(solution)/shard_map/ppermute | solution.py:637
  35.3 0.3 shard_map.39.cube_ref
  35.6 0.0 collective-permute-done.11
  35.6 3.5 %collective-permute-done.12 = f16[4,136,128]{2,1,0:T(8,128)(2,1)S(1)} collective-permute-done((f16[4,136,128]{2,1,0:T(8,128)(2,1)S(1)}, f16[4,136,128]{2,1,0:T(8,128)(2,1)S(1)}, u32[]{:S(2)}, u32[]{:S(2)}) %collective-permute-start.12) | collective-permute-done | bytes 139296 | tf_op jit(solution)/shard_map/ppermute | solution.py:637
  39.1 2.5 %collective-permute-done.13 = f16[4,136,128]{2,1,0:T(8,128)(2,1)S(1)} collective-permute-done((f16[4,136,128]{2,1,0:T(8,128)(2,1)S(1)}, f16[4,136,128]{2,1,0:T(8,128)(2,1)S(1)}, u32[]{:S(2)}, u32[]{:S(2)}) %collective-permute-start.13) | collective-permute-done | bytes 139296 | tf_op jit(solution)/shard_map/ppermute | solution.py:637
  41.6 3.4 %collective-permute-done.14 = f16[4,136,128]{2,1,0:T(8,128)(2,1)S(1)} collective-permute-done((f16[4,136,128]{2,1,0:T(8,128)(2,1)S(1)}, f16[4,136,128]{2,1,0:T(8,128)(2,1)S(1)}, u32[]{:S(2)}, u32[]{:S(2)}) %collective-permute-start.14) | collective-permute-done | bytes 139296 | tf_op jit(solution)/shard_map/ppermute | solution.py:637
  45.0 1.1 %shard_map.41 = bf16[128,2048]{1,0:T(8,128)(2,1)} custom-call(bf16[128,2048]{1,0:T(8,128)(2,1)S(1)} %collective-permute-done.8.x_ref, f32[128,128]{1,0:T(8,128)S(1)} %shard_map.39.cube_ref, f32[4,136,128]{2,1,0:T(8,128)S(1)} %convert_element_type.28.refs_0_, f32[4,136,128]{2,1,0:T(8,128)S(1)} %convert_element_type.29.refs_1_, ...), custom_call_target="tpu_custom_call" | custom-call | tf_op jit(solution)/shard_map/pallas_call | solution.py:640
  (24 shorter events, 0.5 us)
Async XLA Ops:
  1.7 1.7 %collective-permute-start = (bf16[4,256,128]{2,1,0:T(8,128)(2,1)S(1)}, bf16[4,256,128]{2,1,0:T(8,128)(2,1)S(1)}, u32[]{:S(2)}, u32[]{:S(2)}) collective-permute-start(bf16[4,256,128]{2,1,0:T(8,128)(2,1)S(1)} %get-tuple-element.22), channel_id=1, source_target_pairs={{0,1},{1,0},{2,3},{3,2},{4,5},{5,4},{6,7},{7,6},{8,9},{9,8},{10,11... | collective-permute-start | bytes 786440 | tf_op jit(solution)/shard_map/ppermute | solution.py:594
  2.2 1.6 %collective-permute-start.1 = (bf16[4,272,128]{2,1,0:T(8,128)(2,1)S(1)}, bf16[4,272,128]{2,1,0:T(8,128)(2,1)S(1)}, u32[]{:S(2)}, u32[]{:S(2)}) collective-permute-start(bf16[4,272,128]{2,1,0:T(8,128)(2,1)S(1)} %get-tuple-element.24), channel_id=1, source_target_pairs={{0,1},{1,0},{2,3},{3,2},{4,5},{5,4},{6,7},{7,6},{8,9},{9,8},{10,11... | collective-permute-start | bytes 835592 | tf_op jit(solution)/shard_map/ppermute | solution.py:594
  2.3 0.8 %copy-start.1 = (f32[1,5,2048]{2,0,1:T(1,128)S(1)}, f32[1,5,2048]{2,0,1:T(1,128)}, u32[]{:S(2)}) copy-start(f32[1,5,2048]{2,0,1:T(1,128)} %param.5) | copy-start | bytes 122884
  3.8 8.8 %collective-permute-start.2 = (bf16[2,272,128]{2,1,0:T(8,128)(2,1)S(1)}, bf16[2,272,128]{2,1,0:T(8,128)(2,1)S(1)}, u32[]{:S(2)}, u32[]{:S(2)}) collective-permute-start(bf16[2,272,128]{2,1,0:T(8,128)(2,1)S(1)} %pad_maximum_fusion), channel_id=1, source_target_pairs={{0,2},{1,3},{2,0},{3,1},{4,6},{5,7},{6,4},{7,5},{8,10},{9,11},{10,... | collective-permute-start | bytes 417800 | tf_op jit(solution)/shard_map/ppermute | solution.py:603
  6.8 1.7 %copy-start = (bf16[1,8,16,2048]{3,2,1,0:T(8,128)(2,1)S(1)}, bf16[1,8,16,2048]{3,2,1,0:T(8,128)(2,1)}, u32[]{:S(2)}) copy-start(bf16[1,8,16,2048]{3,2,1,0:T(8,128)(2,1)} %param.3) | copy-start | bytes 1572868
  6.8 8.9 %collective-permute-start.6 = (bf16[2,272,128]{2,1,0:T(8,128)(2,1)S(1)}, bf16[2,272,128]{2,1,0:T(8,128)(2,1)S(1)}, u32[]{:S(2)}, u32[]{:S(2)}) collective-permute-start(bf16[2,272,128]{2,1,0:T(8,128)(2,1)S(1)} %pad_maximum_fusion.1), channel_id=1, source_target_pairs={{0,4},{1,5},{2,6},{3,7},{4,0},{5,1},{6,2},{7,3},{8,12},{9,13},{10,... | collective-permute-start | bytes 417800 | tf_op jit(solution)/shard_map/ppermute | solution.py:603
  8.4 8.4 %collective-permute-start.7 = (bf16[2,272,128]{2,1,0:T(8,128)(2,1)S(1)}, bf16[2,272,128]{2,1,0:T(8,128)(2,1)S(1)}, u32[]{:S(2)}, u32[]{:S(2)}) collective-permute-start(bf16[2,272,128]{2,1,0:T(8,128)(2,1)S(1)} %pad_maximum_fusion.2), channel_id=1, source_target_pairs={{0,6},{1,7},{2,4},{3,5},{4,2},{5,3},{6,0},{7,1},{8,14},{9,15},{10,... | collective-permute-start | bytes 417800 | tf_op jit(solution)/shard_map/ppermute | solution.py:603
  8.5 14.8 %collective-permute-start.8 = (bf16[128,2048]{1,0:T(8,128)(2,1)S(1)}, bf16[128,2048]{1,0:T(8,128)(2,1)S(1)}, u32[]{:S(2)}, u32[]{:S(2)}) collective-permute-start(bf16[128,2048]{1,0:T(8,128)(2,1)S(1)} %bitcast.10), channel_id=1, source_target_pairs={{0,24},{8,0},{16,8},{24,16},{1,25},{9,1},{17,9},{25,17},{2,26},{10... | collective-permute-start | bytes 1572872 | tf_op jit(solution)/shard_map/ppermute | solution.py:623
  12.7 5.0 %collective-permute-start.3 = (bf16[2,256,128]{2,1,0:T(8,128)(2,1)S(1)}, bf16[2,256,128]{2,1,0:T(8,128)(2,1)S(1)}, u32[]{:S(2)}, u32[]{:S(2)}) collective-permute-start(bf16[2,256,128]{2,1,0:T(8,128)(2,1)S(1)} %get-tuple-element.25), channel_id=1, source_target_pairs={{0,2},{1,3},{2,0},{3,1},{4,6},{5,7},{6,4},{7,5},{8,10},{9,11},{10,... | collective-permute-start | bytes 393224 | tf_op jit(solution)/shard_map/ppermute | solution.py:603
  14.2 7.7 %collective-permute-start.4 = (bf16[2,256,128]{2,1,0:T(8,128)(2,1)S(1)}, bf16[2,256,128]{2,1,0:T(8,128)(2,1)S(1)}, u32[]{:S(2)}, u32[]{:S(2)}) collective-permute-start(bf16[2,256,128]{2,1,0:T(8,128)(2,1)S(1)} %get-tuple-element.26), channel_id=1, source_target_pairs={{0,4},{1,5},{2,6},{3,7},{4,0},{5,1},{6,2},{7,3},{8,12},{9,13},{10,... | collective-permute-start | bytes 393224 | tf_op jit(solution)/shard_map/ppermute | solution.py:603
  15.7 6.2 %collective-permute-start.5 = (bf16[2,256,128]{2,1,0:T(8,128)(2,1)S(1)}, bf16[2,256,128]{2,1,0:T(8,128)(2,1)S(1)}, u32[]{:S(2)}, u32[]{:S(2)}) collective-permute-start(bf16[2,256,128]{2,1,0:T(8,128)(2,1)S(1)} %pad_maximum_fusion.9), channel_id=1, source_target_pairs={{0,6},{1,7},{2,4},{3,5},{4,2},{5,3},{6,0},{7,1},{8,14},{9,15},{10,... | collective-permute-start | bytes 393224 | tf_op jit(solution)/shard_map/ppermute | solution.py:603
  16.8 6.6 %collective-permute-start.9 = (f16[4,136,128]{2,1,0:T(8,128)(2,1)S(1)}, f16[4,136,128]{2,1,0:T(8,128)(2,1)S(1)}, u32[]{:S(2)}, u32[]{:S(2)}) collective-permute-start(f16[4,136,128]{2,1,0:T(8,128)(2,1)S(1)} %convert_element_type.26), channel_id=1, source_target_pairs={{0,1},{1,0},{2,3},{3,2},{4,5},{5,4},{6,7},{7,6},{8,9},{9,8},{10,11... | collective-permute-start | bytes 417800 | tf_op jit(solution)/shard_map/ppermute | solution.py:633
  23.3 1.4 %collective-permute-start.10 = (f16[4,136,128]{2,1,0:T(8,128)(2,1)S(1)}, f16[4,136,128]{2,1,0:T(8,128)(2,1)S(1)}, u32[]{:S(2)}, u32[]{:S(2)}) collective-permute-start(f16[4,136,128]{2,1,0:T(8,128)(2,1)S(1)} %convert_element_type.27), channel_id=1, source_target_pairs={{0,1},{1,0},{2,3},{3,2},{4,5},{5,4},{6,7},{7,6},{8,9},{9,8},{10,11... | collective-permute-start | bytes 417800 | tf_op jit(solution)/shard_map/ppermute | solution.py:633
  24.8 10.8 %collective-permute-start.11 = (f16[4,136,128]{2,1,0:T(8,128)(2,1)S(1)}, f16[4,136,128]{2,1,0:T(8,128)(2,1)S(1)}, u32[]{:S(2)}, u32[]{:S(2)}) collective-permute-start(f16[4,136,128]{2,1,0:T(8,128)(2,1)S(1)} %pad_maximum_fusion.3), channel_id=1, source_target_pairs={{0,24},{1,25},{2,26},{3,27},{4,28},{5,29},{6,30},{7,31},{8,0},{9,1... | collective-permute-start | bytes 417800 | tf_op jit(solution)/shard_map/ppermute | solution.py:637
  31.6 7.5 %collective-permute-start.12 = (f16[4,136,128]{2,1,0:T(8,128)(2,1)S(1)}, f16[4,136,128]{2,1,0:T(8,128)(2,1)S(1)}, u32[]{:S(2)}, u32[]{:S(2)}) collective-permute-start(f16[4,136,128]{2,1,0:T(8,128)(2,1)S(1)} %pad_maximum_fusion.4), channel_id=1, source_target_pairs={{0,26},{1,27},{2,24},{3,25},{4,30},{5,31},{6,28},{7,29},{8,2},{9,3... | collective-permute-start | bytes 417800 | tf_op jit(solution)/shard_map/ppermute | solution.py:637
  33.7 7.9 %collective-permute-start.13 = (f16[4,136,128]{2,1,0:T(8,128)(2,1)S(1)}, f16[4,136,128]{2,1,0:T(8,128)(2,1)S(1)}, u32[]{:S(2)}, u32[]{:S(2)}) collective-permute-start(f16[4,136,128]{2,1,0:T(8,128)(2,1)S(1)} %pad_maximum_fusion.5), channel_id=1, source_target_pairs={{0,28},{1,29},{2,30},{3,31},{4,24},{5,25},{6,26},{7,27},{8,4},{9,5... | collective-permute-start | bytes 417800 | tf_op jit(solution)/shard_map/ppermute | solution.py:637
  33.9 11.1 %collective-permute-start.14 = (f16[4,136,128]{2,1,0:T(8,128)(2,1)S(1)}, f16[4,136,128]{2,1,0:T(8,128)(2,1)S(1)}, u32[]{:S(2)}, u32[]{:S(2)}) collective-permute-start(f16[4,136,128]{2,1,0:T(8,128)(2,1)S(1)} %pad_maximum_fusion.6), channel_id=1, source_target_pairs={{0,30},{1,31},{2,28},{3,29},{4,26},{5,27},{6,24},{7,25},{8,6},{9,7... | collective-permute-start | bytes 417800 | tf_op jit(solution)/shard_map/ppermute | solution.py:637

commit v2 on v1

--- a/solution.py
+++ b/solution.py
@@ -279,11 +279,10 @@
     return value
 
 
-def inverse_row(x_ref, ready=lambda lane: None):
+def inverse_row(x_ref):
     tokens, channels = x_ref.shape
     squares = None
     for lane in range(0, channels, HEAD_DIM):
-        ready(lane)
         part = x_ref[:, lane : lane + HEAD_DIM].astype(jnp.float32)
         part = part * part
         squares = part if squares is None else squares + part
@@ -298,40 +297,38 @@
     row = lax.axis_index("row")
     col = lax.axis_index("col")
     parts = x_sem.shape[0]
-    wide = channels // parts
+    high_rows = tokens // parts
 
     def fetch(source, target, sems, part):
-        lanes = pl.ds(part * wide, wide)
-        return pltpu.make_async_copy(source.at[:, lanes], target.at[:, lanes], sems.at[part])
+        here = pl.ds(part * high_rows, high_rows)
+        return pltpu.make_async_copy(source.at[here, :], target.at[here, :], sems.at[part])
 
     fetches = [fetch(x_hbm, x_ref, x_sem, part) for part in range(parts)]
     fetches += [fetch(c_hbm, c_ref, c_sem, part) for part in range(parts)]
     for copy in fetches:
         copy.start()
-
-    def ready(lane):
-        if lane % wide == 0:
-            fetches[lane // wide].wait()
-
-    inverse = inverse_row(x_ref, ready)
-    for copy in fetches[parts:]:
+    for copy in fetches[:parts]:
         copy.wait()
+    inverse = inverse_row(x_ref)
     high = inverse.astype(jnp.bfloat16).astype(jnp.float32)
     mid = (inverse - high).astype(jnp.bfloat16).astype(jnp.float32)
     low = inverse - high - mid
     place = lax.broadcasted_iota(jnp.int32, (PIECES, tokens), 0)
     pieces = jnp.where(place == 0, high, jnp.where(place == 1, mid, jnp.where(place == 2, low, 0.0)))
     pieces = pieces.astype(jnp.bfloat16)
-    for head in range(heads):
-        for step in range(rows):
-            for slot in range(2):
-                first = ((row ^ step) * 2 + (col ^ slot)) * heads + head
-                lanes = pl.ds(pl.multiple_of(first * HEAD_DIM, HEAD_DIM), HEAD_DIM)
-                out = outs[head * 2 + slot]
-                out[step, 0:tokens, :] = x_ref[:, lanes]
-                out[step, tokens : 2 * tokens, :] = c_ref[:, lanes]
-                if head == 0:
-                    out[step, 2 * tokens :, :] = pieces
+    for source, low in ((x_ref, 0), (c_ref, tokens)):
+        if low > 0:
+            for copy in fetches[parts:]:
+                copy.wait()
+        for head in range(heads):
+            for step in range(rows):
+                for slot in range(2):
+                    first = ((row ^ step) * 2 + (col ^ slot)) * heads + head
+                    lanes = pl.ds(pl.multiple_of(first * HEAD_DIM, HEAD_DIM), HEAD_DIM)
+                    out = outs[head * 2 + slot]
+                    out[step, low : low + tokens, :] = source[:, lanes]
+                    if head == 0 and low == 0:
+                        out[step, 2 * tokens :, :] = pieces
 
 
 def attend_kernel(rows, heads, head, g_ref, *refs):
@@ -587,16 +584,26 @@
     for head in range(heads):
         packets += [pltpu.VMEM((rows, 2 * tokens + (PIECES if head == 0 else 0), HEAD_DIM), bf)] * 2
     far = pl.BlockSpec(memory_space=pltpu.HBM)
-    staged = [pltpu.VMEM((tokens, channels), bf)] * 2 + [pltpu.SemaphoreType.DMA((4,))] * 2
+    staged = [pltpu.VMEM((tokens, channels), bf)] * 2 + [pltpu.SemaphoreType.DMA((1,))] * 2
     packed = local_call(functools.partial(pack_kernel, rows, heads), packets, staged, in_specs=[far, far])(
         pltpu.with_memory_space_constraint(x, pltpu.HBM), pltpu.with_memory_space_constraint(c, pltpu.HBM)
     )
-    passed = [lax.ppermute(packed[2 * head + 1], plane, crossing(sizes, 0, 1)) for head in range(heads)]
+
+    def swap(array):
+        return lax.ppermute(array, plane, crossing(sizes, 0, 1))
+
+    passed = [[swap(packed[1][1:2]), swap(packed[1][2:]), swap(packed[1][0:1])]]
+    passed += [swap(packed[2 * head + 1]) for head in range(1, heads)]
     arrays = []
     for head in range(heads):
         own, other = packed[2 * head], passed[head]
-        held = [own, other]
-        packets = [jnp.stack([own[step], other[step]]) for step in range(1, rows)]
+        if head == 0:
+            held = [own, other[2]]
+            packets = [jnp.concatenate([own[1:2], other[0]])]
+            packets += [jnp.stack([own[step], other[1][step - 2]]) for step in range(2, rows)]
+        else:
+            held = [own, other]
+            packets = [jnp.stack([own[step], other[step]]) for step in range(1, rows)]
         if head > 0:
             packets, arrays[head - 1][2] = lax.optimization_barrier((packets, arrays[head - 1][2]))
         for step in range(1, rows):
@@ -619,7 +626,7 @@
         pltpu.VMEM((count, HEAD_DIM), f32),
     ]
     behind = [(pipe, (pipe - 1) % pipes) for pipe in range(pipes)]
-    arrays[0][1], free_x = lax.optimization_barrier((arrays[0][1], x))
+    arrays[0][2], free_x = lax.optimization_barrier((arrays[0][2], x))
     x_ahead = lax.ppermute(free_x, "pipe", behind)
     part = pltpu.VMEM((rows, tokens + EXTRA, HEAD_DIM), f32)
     keep, got = [], []

time: 46.4 us -> 45.8 us (0.987)
  waiting for transfers between devices: 17.6 us -> 20.1 us
  starting transfers between devices: 23.8 us -> 21.8 us
  local copies, waits for them, and re-layouts: 0.96 us -> 0.24 us
    ppermute x6, waiting for transfers between devices: 4.97 us -> 7.67 us  [split_heads_per_device(): lax.ppermute(packets[step - 1], plane, crossing(sizes, step, 0))]
    ppermute x4, starting transfers between devices: 10.3 us -> 8.04 us  [split_heads_per_device(): lax.ppermute(sent, ('pipe',) + plane, crossing_back((pipes, rows, cols),...]
    unnamed x5, local copies, waits for them, and re-layouts: 0.77 us -> 0.03 us
    ppermute x2 -> x4, starting transfers between devices: 0.6 us -> 1.17 us  [swap(): return lax.ppermute(array, plane, crossing(sizes, 0, 1))]
  transfers between devices with their start and end apart: 15 -> 17, of which waited for: 9 -> 10; matrix products, arithmetic and copies ran while one was open for 1% -> 1% of each run, Pallas kernels for 1% -> 1%
where the time goes in v2:
time: 45.8 us; the launch traced here: 45.6 us
  starting transfers between devices  21.8 us (48%)
  waiting for transfers between devices  20.1 us (44%)
  Pallas kernels  2.89 us (6%)
  other arithmetic  0.47 us (1%)
    ppermute x4, waiting for transfers between devices, split_heads_per_device(): lax.ppermute(sent, ('pipe',) + plane, crossing_back((pipes, rows, cols),...  9.39 us
    ppermute x6, starting transfers between devices, split_heads_per_device(): lax.ppermute(packets[step - 1], plane, crossing(sizes, step, 0))  8.3 us
    ppermute x4, starting transfers between devices, split_heads_per_device(): lax.ppermute(sent, ('pipe',) + plane, crossing_back((pipes, rows, cols),...  8.04 us
    ppermute x6, waiting for transfers between devices, split_heads_per_device(): lax.ppermute(packets[step - 1], plane, crossing(sizes, step, 0))  7.67 us
    ppermute x1, starting transfers between devices, split_heads_per_device(): x_ahead = lax.ppermute(free_x, 'pipe', behind)  4.1 us
    pallas_call x1, Pallas kernels, split_heads_per_device(): local_call(functools.partial(pack_kernel, rows, heads), packets, staged,...  1.49 us
    ppermute x2, waiting for transfers between devices, split_heads_per_device(): lax.ppermute(given.astype(jnp.float16), plane, crossing(sizes, 0, 1))  1.3 us
    ppermute x4, starting transfers between devices, swap(): return lax.ppermute(array, plane, crossing(sizes, 0, 1))  1.17 us
  transfers between devices with their start and end apart: 17, of which 10 were waited for; matrix products, arithmetic and copies ran while one was open for 1% of the time, Pallas kernels for 1%

profile of v2, /device:TPU:0, one launch (start us, length us, event | category | flops | bytes accessed | tf_op | source)
XLA Modules:
  0.0 45.6 jit_solution(10587567266688047751)
XLA Ops:
  0.0 1.5 %shard_map.37 = (bf16[4,272,128]{2,1,0:T(8,128)(2,1)S(1)}, bf16[4,272,128]{2,1,0:T(8,128)(2,1)S(1)}, bf16[4,256,128]{2,1,0:T(8,128)(2,1)S(1)}, bf16[4,256,128]{2,1,0:T(8,128)(2,1)S(1)}) custom-call(bf16[128,2048]{1,0:T(8,128)(2,1)} %bitcast.9, bf16[128,2048]{1,0:T(8,128)(2,1)} %bitcast.8), custom_call_target="tpu_custom_call" | custom-call | tf_op jit(solution)/shard_map/pallas_call | solution.py:588
  1.5 0.5 %collective-permute-start.6 = (bf16[1,272,128]{2,1,0:T(8,128)(2,1)S(1)}, bf16[1,272,128]{2,1,0:T(8,128)(2,1)S(1)}, u32[]{:S(2)}, u32[]{:S(2)}) collective-permute-start(bf16[1,272,128]{2,1,0:T(8,128)(2,1)S(1)} %get-tuple-element.40), channel_id=1, source_target_pairs={{0,1},{1,0},{2,3},{3,2},{4,5},{5,4},{6,7},{7,6},{8,9},{9,8},{10,11... | collective-permute-start | bytes 208904 | tf_op jit(solution)/shard_map/ppermute | solution.py:593
  2.0 0.1 collective-permute-start.1
  2.1 0.5 %collective-permute-start.7 = (bf16[2,272,128]{2,1,0:T(8,128)(2,1)S(1)}, bf16[2,272,128]{2,1,0:T(8,128)(2,1)S(1)}, u32[]{:S(2)}, u32[]{:S(2)}) collective-permute-start(bf16[2,272,128]{2,1,0:T(8,128)(2,1)S(1)} %slice.100), channel_id=1, source_target_pairs={{0,1},{1,0},{2,3},{3,2},{4,5},{5,4},{6,7},{7,6},{8,9},{9,8},{10,11... | collective-permute-start | bytes 417800 | tf_op jit(solution)/shard_map/ppermute | solution.py:593
  2.6 0.1 collective-permute-start
  2.7 0.6 %collective-permute-done.1 = bf16[1,272,128]{2,1,0:T(8,128)(2,1)S(1)} collective-permute-done((bf16[1,272,128]{2,1,0:T(8,128)(2,1)S(1)}, bf16[1,272,128]{2,1,0:T(8,128)(2,1)S(1)}, u32[]{:S(2)}, u32[]{:S(2)}) %collective-permute-start.1) | collective-permute-done | bytes 69664 | tf_op jit(solution)/shard_map/ppermute | solution.py:593
  3.3 2.7 %collective-permute-start.2 = (bf16[2,272,128]{2,1,0:T(8,128)(2,1)S(1)}, bf16[2,272,128]{2,1,0:T(8,128)(2,1)S(1)}, u32[]{:S(2)}, u32[]{:S(2)}) collective-permute-start(bf16[2,272,128]{2,1,0:T(8,128)(2,1)S(1)} %pad_maximum_fusion), channel_id=1, source_target_pairs={{0,2},{1,3},{2,0},{3,1},{4,6},{5,7},{6,4},{7,5},{8,10},{9,11},{10,... | collective-permute-start | bytes 417800 | tf_op jit(solution)/shard_map/ppermute | solution.py:610
  6.0 0.0 collective-permute-done.7
  6.1 1.6 %collective-permute-start.8 = (bf16[2,272,128]{2,1,0:T(8,128)(2,1)S(1)}, bf16[2,272,128]{2,1,0:T(8,128)(2,1)S(1)}, u32[]{:S(2)}, u32[]{:S(2)}) collective-permute-start(bf16[2,272,128]{2,1,0:T(8,128)(2,1)S(1)} %pad_maximum_fusion.1), channel_id=1, source_target_pairs={{0,4},{1,5},{2,6},{3,7},{4,0},{5,1},{6,2},{7,3},{8,12},{9,13},{10,... | collective-permute-start | bytes 417800 | tf_op jit(solution)/shard_map/ppermute | solution.py:610
  7.7 0.0 copy-start
  7.7 0.5 collective-permute-start.9
  8.1 0.0 collective-permute-done.operands_2_
  8.2 0.0 copy-start.1
  8.2 2.1 %collective-permute-done.2.operands_8_.operands_3_ = bf16[2,272,128]{2,1,0:T(8,128)(2,1)S(1)} collective-permute-done((bf16[2,272,128]{2,1,0:T(8,128)(2,1)S(1)}, bf16[2,272,128]{2,1,0:T(8,128)(2,1)S(1)}, u32[]{:S(2)}, u32[]{:S(2)}) %collective-permute-start.2) | collective-permute-done | bytes 139296 | tf_op jit(solution)/shard_map/ppermute | solution.py:610
  10.3 0.0 copy-done
  10.3 4.1 %collective-permute-start.10 = (bf16[128,2048]{1,0:T(8,128)(2,1)S(1)}, bf16[128,2048]{1,0:T(8,128)(2,1)S(1)}, u32[]{:S(2)}, u32[]{:S(2)}) collective-permute-start(bf16[128,2048]{1,0:T(8,128)(2,1)S(1)} %bitcast.10), channel_id=1, source_target_pairs={{0,24},{8,0},{16,8},{24,16},{1,25},{9,1},{17,9},{25,17},{2,26},{10... | collective-permute-start | bytes 1572872 | tf_op jit(solution)/shard_map/ppermute | solution.py:630
  14.4 0.0 copy-done.1
  14.4 1.8 %collective-permute-start.3 = (bf16[2,256,128]{2,1,0:T(8,128)(2,1)S(1)}, bf16[2,256,128]{2,1,0:T(8,128)(2,1)S(1)}, u32[]{:S(2)}, u32[]{:S(2)}) collective-permute-start(bf16[2,256,128]{2,1,0:T(8,128)(2,1)S(1)} %get-tuple-element.25), channel_id=1, source_target_pairs={{0,2},{1,3},{2,0},{3,1},{4,6},{5,7},{6,4},{7,5},{8,10},{9,11},{10,... | collective-permute-start | bytes 393224 | tf_op jit(solution)/shard_map/ppermute | solution.py:610
  16.2 0.0 collective-permute-done.6.operands_7_.operands_2_
  16.2 1.5 %collective-permute-start.4 = (bf16[2,256,128]{2,1,0:T(8,128)(2,1)S(1)}, bf16[2,256,128]{2,1,0:T(8,128)(2,1)S(1)}, u32[]{:S(2)}, u32[]{:S(2)}) collective-permute-start(bf16[2,256,128]{2,1,0:T(8,128)(2,1)S(1)} %get-tuple-element.26), channel_id=1, source_target_pairs={{0,4},{1,5},{2,6},{3,7},{4,0},{5,1},{6,2},{7,3},{8,12},{9,13},{10,... | collective-permute-start | bytes 393224 | tf_op jit(solution)/shard_map/ppermute | solution.py:610
  17.7 0.0 collective-permute-done.8.operands_9_.operands_4_
  17.7 0.2 collective-permute-start.5
  18.0 0.0 collective-permute-done.9.operands_10_.operands_5_
  18.0 0.1 collective-permute-start.11
  18.1 2.4 %collective-permute-done.3.operands_3_ = bf16[2,256,128]{2,1,0:T(8,128)(2,1)S(1)} collective-permute-done((bf16[2,256,128]{2,1,0:T(8,128)(2,1)S(1)}, bf16[2,256,128]{2,1,0:T(8,128)(2,1)S(1)}, u32[]{:S(2)}, u32[]{:S(2)}) %collective-permute-start.3) | collective-permute-done | bytes 131104 | tf_op jit(solution)/shard_map/ppermute | solution.py:610
  20.5 3.2 %collective-permute-done.4.operands_4_ = bf16[2,256,128]{2,1,0:T(8,128)(2,1)S(1)} collective-permute-done((bf16[2,256,128]{2,1,0:T(8,128)(2,1)S(1)}, bf16[2,256,128]{2,1,0:T(8,128)(2,1)S(1)}, u32[]{:S(2)}, u32[]{:S(2)}) %collective-permute-start.4) | collective-permute-done | bytes 131104 | tf_op jit(solution)/shard_map/ppermute | solution.py:610
  23.7 0.0 collective-permute-done.5.operands_5_
  23.8 1.1 %collective-permute-done.10.x_ref = bf16[128,2048]{1,0:T(8,128)(2,1)S(1)} collective-permute-done((bf16[128,2048]{1,0:T(8,128)(2,1)S(1)}, bf16[128,2048]{1,0:T(8,128)(2,1)S(1)}, u32[]{:S(2)}, u32[]{:S(2)}) %collective-permute-start.10) | collective-permute-done | bytes 524320 | tf_op jit(solution)/shard_map/ppermute | solution.py:630
  25.0 0.1 collective-permute-start.12
  25.1 0.0 collective-permute-done.11
  25.1 1.3 %collective-permute-done.12 = f16[4,136,128]{2,1,0:T(8,128)(2,1)S(1)} collective-permute-done((f16[4,136,128]{2,1,0:T(8,128)(2,1)S(1)}, f16[4,136,128]{2,1,0:T(8,128)(2,1)S(1)}, u32[]{:S(2)}, u32[]{:S(2)}) %collective-permute-start.12) | collective-permute-done | bytes 139296 | tf_op jit(solution)/shard_map/ppermute | solution.py:640
  26.4 0.1 pad_maximum_fusion.3
  26.5 4.7 %collective-permute-start.13 = (f16[4,136,128]{2,1,0:T(8,128)(2,1)S(1)}, f16[4,136,128]{2,1,0:T(8,128)(2,1)S(1)}, u32[]{:S(2)}, u32[]{:S(2)}) collective-permute-start(f16[4,136,128]{2,1,0:T(8,128)(2,1)S(1)} %pad_maximum_fusion.3), channel_id=1, source_target_pairs={{0,24},{1,25},{2,26},{3,27},{4,28},{5,29},{6,30},{7,31},{8,0},{9,1... | collective-permute-start | bytes 417800 | tf_op jit(solution)/shard_map/ppermute | solution.py:644
  31.2 0.1 pad_maximum_fusion.4
  31.3 1.9 %collective-permute-start.14 = (f16[4,136,128]{2,1,0:T(8,128)(2,1)S(1)}, f16[4,136,128]{2,1,0:T(8,128)(2,1)S(1)}, u32[]{:S(2)}, u32[]{:S(2)}) collective-permute-start(f16[4,136,128]{2,1,0:T(8,128)(2,1)S(1)} %pad_maximum_fusion.4), channel_id=1, source_target_pairs={{0,26},{1,27},{2,24},{3,25},{4,30},{5,31},{6,28},{7,29},{8,2},{9,3... | collective-permute-start | bytes 417800 | tf_op jit(solution)/shard_map/ppermute | solution.py:644
  33.2 0.1 pad_maximum_fusion.5
  33.2 0.1 collective-permute-start.15
  33.3 0.1 pad_maximum_fusion.6
  33.3 1.4 %collective-permute-start.16 = (f16[4,136,128]{2,1,0:T(8,128)(2,1)S(1)}, f16[4,136,128]{2,1,0:T(8,128)(2,1)S(1)}, u32[]{:S(2)}, u32[]{:S(2)}) collective-permute-start(f16[4,136,128]{2,1,0:T(8,128)(2,1)S(1)} %pad_maximum_fusion.6), channel_id=1, source_target_pairs={{0,30},{1,31},{2,28},{3,29},{4,26},{5,27},{6,24},{7,25},{8,6},{9,7... | collective-permute-start | bytes 417800 | tf_op jit(solution)/shard_map/ppermute | solution.py:644
  34.7 0.3 shard_map.39.cube_ref
  35.0 0.2 collective-permute-done.13
  35.3 3.5 %collective-permute-done.14 = f16[4,136,128]{2,1,0:T(8,128)(2,1)S(1)} collective-permute-done((f16[4,136,128]{2,1,0:T(8,128)(2,1)S(1)}, f16[4,136,128]{2,1,0:T(8,128)(2,1)S(1)}, u32[]{:S(2)}, u32[]{:S(2)}) %collective-permute-start.14) | collective-permute-done | bytes 139296 | tf_op jit(solution)/shard_map/ppermute | solution.py:644
  38.8 3.6 %collective-permute-done.15 = f16[4,136,128]{2,1,0:T(8,128)(2,1)S(1)} collective-permute-done((f16[4,136,128]{2,1,0:T(8,128)(2,1)S(1)}, f16[4,136,128]{2,1,0:T(8,128)(2,1)S(1)}, u32[]{:S(2)}, u32[]{:S(2)}) %collective-permute-start.15) | collective-permute-done | bytes 139296 | tf_op jit(solution)/shard_map/ppermute | solution.py:644
  42.4 2.1 %collective-permute-done.16 = f16[4,136,128]{2,1,0:T(8,128)(2,1)S(1)} collective-permute-done((f16[4,136,128]{2,1,0:T(8,128)(2,1)S(1)}, f16[4,136,128]{2,1,0:T(8,128)(2,1)S(1)}, u32[]{:S(2)}, u32[]{:S(2)}) %collective-permute-start.16) | collective-permute-done | bytes 139296 | tf_op jit(solution)/shard_map/ppermute | solution.py:644
  44.5 1.1 %shard_map.41 = bf16[128,2048]{1,0:T(8,128)(2,1)} custom-call(bf16[128,2048]{1,0:T(8,128)(2,1)S(1)} %collective-permute-done.10.x_ref, f32[128,128]{1,0:T(8,128)S(1)} %shard_map.39.cube_ref, f32[4,136,128]{2,1,0:T(8,128)S(1)} %convert_element_type.28.refs_0_, f32[4,136,128]{2,1,0:T(8,128)S(1)} %convert_element_type.29.refs_1_, ...), custom_call_target="tpu_custom_call" | custom-call | tf_op jit(solution)/shard_map/pallas_call | solution.py:647
  (26 shorter events, 0.5 us)
Async XLA Ops:
  1.5 14.7 %collective-permute-start.6 = (bf16[1,272,128]{2,1,0:T(8,128)(2,1)S(1)}, bf16[1,272,128]{2,1,0:T(8,128)(2,1)S(1)}, u32[]{:S(2)}, u32[]{:S(2)}) collective-permute-start(bf16[1,272,128]{2,1,0:T(8,128)(2,1)S(1)} %get-tuple-element.40), channel_id=1, source_target_pairs={{0,1},{1,0},{2,3},{3,2},{4,5},{5,4},{6,7},{7,6},{8,9},{9,8},{10,11... | collective-permute-start | bytes 208904 | tf_op jit(solution)/shard_map/ppermute | solution.py:593
  2.0 1.3 %collective-permute-start.1 = (bf16[1,272,128]{2,1,0:T(8,128)(2,1)S(1)}, bf16[1,272,128]{2,1,0:T(8,128)(2,1)S(1)}, u32[]{:S(2)}, u32[]{:S(2)}) collective-permute-start(bf16[1,272,128]{2,1,0:T(8,128)(2,1)S(1)} %get-tuple-element.41), channel_id=1, source_target_pairs={{0,1},{1,0},{2,3},{3,2},{4,5},{5,4},{6,7},{7,6},{8,9},{9,8},{10,11... | collective-permute-start | bytes 208904 | tf_op jit(solution)/shard_map/ppermute | solution.py:593
  2.1 3.9 %collective-permute-start.7 = (bf16[2,272,128]{2,1,0:T(8,128)(2,1)S(1)}, bf16[2,272,128]{2,1,0:T(8,128)(2,1)S(1)}, u32[]{:S(2)}, u32[]{:S(2)}) collective-permute-start(bf16[2,272,128]{2,1,0:T(8,128)(2,1)S(1)} %slice.100), channel_id=1, source_target_pairs={{0,1},{1,0},{2,3},{3,2},{4,5},{5,4},{6,7},{7,6},{8,9},{9,8},{10,11... | collective-permute-start | bytes 417800 | tf_op jit(solution)/shard_map/ppermute | solution.py:593
  2.6 5.5 %collective-permute-start = (bf16[4,256,128]{2,1,0:T(8,128)(2,1)S(1)}, bf16[4,256,128]{2,1,0:T(8,128)(2,1)S(1)}, u32[]{:S(2)}, u32[]{:S(2)}) collective-permute-start(bf16[4,256,128]{2,1,0:T(8,128)(2,1)S(1)} %get-tuple-element.22), channel_id=1, source_target_pairs={{0,1},{1,0},{2,3},{3,2},{4,5},{5,4},{6,7},{7,6},{8,9},{9,8},{10,11... | collective-permute-start | bytes 786440 | tf_op jit(solution)/shard_map/ppermute | solution.py:593
  3.3 7.0 %collective-permute-start.2 = (bf16[2,272,128]{2,1,0:T(8,128)(2,1)S(1)}, bf16[2,272,128]{2,1,0:T(8,128)(2,1)S(1)}, u32[]{:S(2)}, u32[]{:S(2)}) collective-permute-start(bf16[2,272,128]{2,1,0:T(8,128)(2,1)S(1)} %pad_maximum_fusion), channel_id=1, source_target_pairs={{0,2},{1,3},{2,0},{3,1},{4,6},{5,7},{6,4},{7,5},{8,10},{9,11},{10,... | collective-permute-start | bytes 417800 | tf_op jit(solution)/shard_map/ppermute | solution.py:610
  6.1 11.7 %collective-permute-start.8 = (bf16[2,272,128]{2,1,0:T(8,128)(2,1)S(1)}, bf16[2,272,128]{2,1,0:T(8,128)(2,1)S(1)}, u32[]{:S(2)}, u32[]{:S(2)}) collective-permute-start(bf16[2,272,128]{2,1,0:T(8,128)(2,1)S(1)} %pad_maximum_fusion.1), channel_id=1, source_target_pairs={{0,4},{1,5},{2,6},{3,7},{4,0},{5,1},{6,2},{7,3},{8,12},{9,13},{10,... | collective-permute-start | bytes 417800 | tf_op jit(solution)/shard_map/ppermute | solution.py:610
  7.7 2.6 %copy-start = (bf16[1,8,16,2048]{3,2,1,0:T(8,128)(2,1)S(1)}, bf16[1,8,16,2048]{3,2,1,0:T(8,128)(2,1)}, u32[]{:S(2)}) copy-start(bf16[1,8,16,2048]{3,2,1,0:T(8,128)(2,1)} %param.3) | copy-start | bytes 1572868
  7.7 10.3 %collective-permute-start.9 = (bf16[2,272,128]{2,1,0:T(8,128)(2,1)S(1)}, bf16[2,272,128]{2,1,0:T(8,128)(2,1)S(1)}, u32[]{:S(2)}, u32[]{:S(2)}) collective-permute-start(bf16[2,272,128]{2,1,0:T(8,128)(2,1)S(1)} %pad_maximum_fusion.2), channel_id=1, source_target_pairs={{0,6},{1,7},{2,4},{3,5},{4,2},{5,3},{6,0},{7,1},{8,14},{9,15},{10,... | collective-permute-start | bytes 417800 | tf_op jit(solution)/shard_map/ppermute | solution.py:610
  8.2 6.2 %copy-start.1 = (f32[1,5,2048]{2,0,1:T(1,128)S(1)}, f32[1,5,2048]{2,0,1:T(1,128)}, u32[]{:S(2)}) copy-start(f32[1,5,2048]{2,0,1:T(1,128)} %param.5) | copy-start | bytes 122884
  10.3 14.7 %collective-permute-start.10 = (bf16[128,2048]{1,0:T(8,128)(2,1)S(1)}, bf16[128,2048]{1,0:T(8,128)(2,1)S(1)}, u32[]{:S(2)}, u32[]{:S(2)}) collective-permute-start(bf16[128,2048]{1,0:T(8,128)(2,1)S(1)} %bitcast.10), channel_id=1, source_target_pairs={{0,24},{8,0},{16,8},{24,16},{1,25},{9,1},{17,9},{25,17},{2,26},{10... | collective-permute-start | bytes 1572872 | tf_op jit(solution)/shard_map/ppermute | solution.py:630
  14.4 6.1 %collective-permute-start.3 = (bf16[2,256,128]{2,1,0:T(8,128)(2,1)S(1)}, bf16[2,256,128]{2,1,0:T(8,128)(2,1)S(1)}, u32[]{:S(2)}, u32[]{:S(2)}) collective-permute-start(bf16[2,256,128]{2,1,0:T(8,128)(2,1)S(1)} %get-tuple-element.25), channel_id=1, source_target_pairs={{0,2},{1,3},{2,0},{3,1},{4,6},{5,7},{6,4},{7,5},{8,10},{9,11},{10,... | collective-permute-start | bytes 393224 | tf_op jit(solution)/shard_map/ppermute | solution.py:610
  16.2 7.5 %collective-permute-start.4 = (bf16[2,256,128]{2,1,0:T(8,128)(2,1)S(1)}, bf16[2,256,128]{2,1,0:T(8,128)(2,1)S(1)}, u32[]{:S(2)}, u32[]{:S(2)}) collective-permute-start(bf16[2,256,128]{2,1,0:T(8,128)(2,1)S(1)} %get-tuple-element.26), channel_id=1, source_target_pairs={{0,4},{1,5},{2,6},{3,7},{4,0},{5,1},{6,2},{7,3},{8,12},{9,13},{10,... | collective-permute-start | bytes 393224 | tf_op jit(solution)/shard_map/ppermute | solution.py:610
  17.7 6.0 %collective-permute-start.5 = (bf16[2,256,128]{2,1,0:T(8,128)(2,1)S(1)}, bf16[2,256,128]{2,1,0:T(8,128)(2,1)S(1)}, u32[]{:S(2)}, u32[]{:S(2)}) collective-permute-start(bf16[2,256,128]{2,1,0:T(8,128)(2,1)S(1)} %pad_maximum_fusion.9), channel_id=1, source_target_pairs={{0,6},{1,7},{2,4},{3,5},{4,2},{5,3},{6,0},{7,1},{8,14},{9,15},{10,... | collective-permute-start | bytes 393224 | tf_op jit(solution)/shard_map/ppermute | solution.py:610
  18.0 7.0 %collective-permute-start.11 = (f16[4,136,128]{2,1,0:T(8,128)(2,1)S(1)}, f16[4,136,128]{2,1,0:T(8,128)(2,1)S(1)}, u32[]{:S(2)}, u32[]{:S(2)}) collective-permute-start(f16[4,136,128]{2,1,0:T(8,128)(2,1)S(1)} %convert_element_type.26), channel_id=1, source_target_pairs={{0,1},{1,0},{2,3},{3,2},{4,5},{5,4},{6,7},{7,6},{8,9},{9,8},{10,11... | collective-permute-start | bytes 417800 | tf_op jit(solution)/shard_map/ppermute | solution.py:640
  25.0 1.4 %collective-permute-start.12 = (f16[4,136,128]{2,1,0:T(8,128)(2,1)S(1)}, f16[4,136,128]{2,1,0:T(8,128)(2,1)S(1)}, u32[]{:S(2)}, u32[]{:S(2)}) collective-permute-start(f16[4,136,128]{2,1,0:T(8,128)(2,1)S(1)} %convert_element_type.27), channel_id=1, source_target_pairs={{0,1},{1,0},{2,3},{3,2},{4,5},{5,4},{6,7},{7,6},{8,9},{9,8},{10,11... | collective-permute-start | bytes 417800 | tf_op jit(solution)/shard_map/ppermute | solution.py:640
  26.5 8.7 %collective-permute-start.13 = (f16[4,136,128]{2,1,0:T(8,128)(2,1)S(1)}, f16[4,136,128]{2,1,0:T(8,128)(2,1)S(1)}, u32[]{:S(2)}, u32[]{:S(2)}) collective-permute-start(f16[4,136,128]{2,1,0:T(8,128)(2,1)S(1)} %pad_maximum_fusion.3), channel_id=1, source_target_pairs={{0,24},{1,25},{2,26},{3,27},{4,28},{5,29},{6,30},{7,31},{8,0},{9,1... | collective-permute-start | bytes 417800 | tf_op jit(solution)/shard_map/ppermute | solution.py:644
  31.3 7.5 %collective-permute-start.14 = (f16[4,136,128]{2,1,0:T(8,128)(2,1)S(1)}, f16[4,136,128]{2,1,0:T(8,128)(2,1)S(1)}, u32[]{:S(2)}, u32[]{:S(2)}) collective-permute-start(f16[4,136,128]{2,1,0:T(8,128)(2,1)S(1)} %pad_maximum_fusion.4), channel_id=1, source_target_pairs={{0,26},{1,27},{2,24},{3,25},{4,30},{5,31},{6,28},{7,29},{8,2},{9,3... | collective-permute-start | bytes 417800 | tf_op jit(solution)/shard_map/ppermute | solution.py:644
  33.2 9.2 %collective-permute-start.15 = (f16[4,136,128]{2,1,0:T(8,128)(2,1)S(1)}, f16[4,136,128]{2,1,0:T(8,128)(2,1)S(1)}, u32[]{:S(2)}, u32[]{:S(2)}) collective-permute-start(f16[4,136,128]{2,1,0:T(8,128)(2,1)S(1)} %pad_maximum_fusion.5), channel_id=1, source_target_pairs={{0,28},{1,29},{2,30},{3,31},{4,24},{5,25},{6,26},{7,27},{8,4},{9,5... | collective-permute-start | bytes 417800 | tf_op jit(solution)/shard_map/ppermute | solution.py:644
  33.3 11.1 %collective-permute-start.16 = (f16[4,136,128]{2,1,0:T(8,128)(2,1)S(1)}, f16[4,136,128]{2,1,0:T(8,128)(2,1)S(1)}, u32[]{:S(2)}, u32[]{:S(2)}) collective-permute-start(f16[4,136,128]{2,1,0:T(8,128)(2,1)S(1)} %pad_maximum_fusion.6), channel_id=1, source_target_pairs={{0,30},{1,31},{2,28},{3,29},{4,26},{5,27},{6,24},{7,25},{8,6},{9,7... | collective-permute-start | bytes 417800 | tf_op jit(solution)/shard_map/ppermute | solution.py:644

commit v3 on v2

--- a/solution.py
+++ b/solution.py
@@ -333,10 +333,13 @@
 
 def attend_kernel(rows, heads, head, g_ref, *refs):
     held = rows + 1
-    arrays, inverses = refs[0:held], refs[held : 2 * held]
-    keep_ref, give_ref = refs[2 * held : 2 * held + 2]
-    q_s, k_s, kt_s, v_s, d_s, p_s, ds_s, s_s, dp_s, dk_s, dv_s, dq_s = refs[2 * held + 2 :]
-    tokens = keep_ref.shape[1] - EXTRA
+    arrays, refs = refs[:held], list(refs[held:])
+    columns_ref = refs.pop(0)
+    before_ref = refs.pop(0) if head > 0 else None
+    after_ref = refs.pop(0) if head < heads - 1 else None
+    keep_ref, give_ref = refs[:2]
+    q_s, k_s, kt_s, v_s, d_s, p_s, ds_s, s_s, dp_s, dk_s, dv_s, dq_s = refs[-12:]
+    tokens = columns_ref.shape[0] // (2 * rows)
     row = lax.axis_index("row")
     col = lax.axis_index("col")
     lanes = pl.ds(pl.multiple_of(((row * 2 + col) * heads + head) * HEAD_DIM, HEAD_DIM), HEAD_DIM)
@@ -353,18 +356,21 @@
     def capped(s, cap):
         return jnp.minimum(s.reshape(pattern), cap[None]).reshape(tokens, tokens)
 
-    def block(step, slot):
+    def block(step, slot, fresh=False):
         number, index = (slot, 0) if step == 0 else (step + 1, slot)
         ref = arrays[number]
         place = pl.multiple_of(((row ^ step) * 2 + (col ^ slot)) * tokens, tokens)
         x = ref[index, 0:tokens, :].astype(jnp.float32)
         c = ref[index, tokens : 2 * tokens, :].astype(jnp.float32)
-        inverse = inverse_columns(inverses[number][index, 2 * tokens :, :])
-        return pl.ds(place, tokens), x, c, inverse
+        here = pl.ds(place, tokens)
+        return here, x, c, ref[index, 2 * tokens :, :] if fresh else columns_ref[here, :]
 
     blocks = [(step, slot) for step in range(rows) for slot in range(2)]
     for step, slot in blocks:
-        here, x, c, inverse = block(step, slot)
+        here, x, c, inverse = block(step, slot, head == 0)
+        if head == 0:
+            inverse = inverse_columns(inverse)
+            columns_ref[here, :] = inverse
         normed = (x * inverse * gn).astype(jnp.bfloat16).astype(jnp.float32)
         q_s[here, :] = (normed * gq).astype(jnp.bfloat16)
         key = (normed * gk).astype(jnp.bfloat16)
@@ -497,20 +503,29 @@
     number = scale_number(jnp.broadcast_to(top, (len(blocks), tokens)))
     shrink = 1.0 / scale_value(number)
     share = jnp.concatenate(shares, axis=0)
-    share_number = scale_number(jnp.abs(share))
-    share = share / scale_value(share_number)
-    high = share.astype(jnp.bfloat16).astype(jnp.float32)
-    mid = (share - high).astype(jnp.bfloat16).astype(jnp.float32)
-    low = share - high - mid
-    place = lax.broadcasted_iota(jnp.int32, (EXTRA, tokens), 0)
+    numbers = [before_ref[earlier + 1] for earlier in range(head)] + [number]
+    if head > 0:
+        share = share + before_ref[0]
+    if head < heads - 1:
+        after_ref[0] = share
+        for index, value in enumerate(numbers):
+            after_ref[index + 1] = value
+    else:
+        share_number = scale_number(jnp.abs(share))
+        share = share / scale_value(share_number)
+        high = share.astype(jnp.bfloat16).astype(jnp.float32)
+        mid = (share - high).astype(jnp.bfloat16).astype(jnp.float32)
+        low = share - high - mid
+        place = lax.broadcasted_iota(jnp.int32, (EXTRA, tokens), 0)
     for index, (step, slot) in enumerate(blocks):
         out = (keep_ref, give_ref)[slot]
         at = slice(index, index + 1)
         out[step, 0:tokens, :] = out[step, 0:tokens, :] * shrink[at]
-        extra = jnp.zeros((EXTRA, tokens), jnp.float32)
-        for line, row_of in enumerate((number, share_number, high, mid, low)):
-            extra = jnp.where(place == line, row_of[at], extra)
-        out[step, tokens:, :] = extra
+        if head == heads - 1:
+            extra = jnp.zeros((EXTRA, tokens), jnp.float32)
+            for line, value in enumerate([share_number, high, mid, low] + numbers):
+                extra = jnp.where(place == line, value[at], extra)
+            out[step, tokens:, :] = extra
 
 
 def attention_kernel(*operands):
@@ -531,13 +546,15 @@
     row = lax.axis_index("row")
     col = lax.axis_index("col")
     last = lax.axis_index("pipe") == lax.axis_size("pipe") - 1
+    side = heads * tokens + EXTRA
     total, scales = None, {}
     for step in range(rows):
-        for slot in range(2 * heads):
-            extra = units[step][slot, tokens : tokens + 8, :]
+        for half in range(2):
+            extra = units[step][half * side + heads * tokens : (half + 1) * side, :]
             value = scale_value(extra)
-            scales[step, slot] = value[0:1]
-            share = (extra[2:3] + extra[3:4] + extra[4:5]) * value[1:2]
+            for head in range(heads):
+                scales[step, half * heads + head] = value[4 + head : 5 + head]
+            share = (extra[1:2] + extra[2:3] + extra[3:4]) * value[0:1]
             total = share if total is None else total + share
     weight = cube_ref[...] * row_to_column(total / channels)
     wide = 2 * heads * HEAD_DIM
@@ -546,7 +563,9 @@
         for slot in range(2 * heads):
             first = ((row ^ step) * 2 + (col ^ (slot // heads))) * heads + slot % heads
             lanes = pl.ds(pl.multiple_of(first * HEAD_DIM, HEAD_DIM), HEAD_DIM)
-            grad = units[step][slot, 0:tokens, :] * scales[step, slot] - x_ref[:, lanes].astype(jnp.float32) * weight
+            top = slot // heads * side + slot % heads * tokens
+            part = units[step][top : top + tokens, :] * scales[step, slot]
+            grad = part - x_ref[:, lanes].astype(jnp.float32) * weight
             out_ref[:, lanes] = jnp.where(last, 0.0, grad).astype(jnp.bfloat16)
         lanes = pl.ds(pl.multiple_of((row ^ step) * wide, wide), wide)
         copies.append(pltpu.make_async_copy(out_ref.at[:, lanes], out_hbm.at[:, lanes], sems.at[step]))
@@ -628,19 +647,27 @@
     behind = [(pipe, (pipe - 1) % pipes) for pipe in range(pipes)]
     arrays[0][2], free_x = lax.optimization_barrier((arrays[0][2], x))
     x_ahead = lax.ppermute(free_x, "pipe", behind)
-    part = pltpu.VMEM((rows, tokens + EXTRA, HEAD_DIM), f32)
+    carried = pltpu.VMEM((heads, 2 * rows, tokens), f32)
+    columns = [pltpu.VMEM((count, HEAD_DIM), f32)]
+    handed = []
     keep, got = [], []
     for head in range(heads):
-        kept, given = local_call(
-            functools.partial(attention_kernel, rows, heads, head), [part, part], scratch
-        )(gains, *near(arrays[head]), *near(arrays[0]))
+        results = columns if head == 0 else []
+        results = results + ([carried] if head < heads - 1 else [])
+        height = tokens + (EXTRA if head == heads - 1 else 0)
+        results = results + [pltpu.VMEM((rows, height, HEAD_DIM), f32)] * 2
+        operands = arrays[head] + ([] if head == 0 else columns + handed)
+        call = local_call(functools.partial(attention_kernel, rows, heads, head), results, scratch)
+        *others, kept, given = call(gains, *near(operands))
+        columns = others[:1] if head == 0 else columns
+        handed = others[-1:]
         if head == heads - 1:
             given, x_ahead = lax.optimization_barrier((given, x_ahead))
         keep.append(kept.astype(jnp.float16))
         got.append(lax.ppermute(given.astype(jnp.float16), plane, crossing(sizes, 0, 1)))
     units = []
     for step in range(rows):
-        sent = jnp.stack([unit[step] for unit in keep + got])
+        sent = jnp.concatenate([unit[step] for unit in keep + got])
         sent = lax.ppermute(sent, ("pipe",) + plane, crossing_back((pipes, rows, cols), step))
         units.append(sent.astype(f32))
     cube = local_call(cube_kernel, pltpu.VMEM((tokens, HEAD_DIM), f32))(*near([x_ahead]))

time: 45.8 us -> 45.5 us (level)
  no operation moved by 1% of the time
where the time goes in v3:
time: 45.5 us; the launch traced here: 45.3 us
  starting transfers between devices  21.6 us (47%)
  waiting for transfers between devices  20 us (44%)
  Pallas kernels  2.84 us (6%)
  other arithmetic  0.46 us (1%)
    ppermute x4, waiting for transfers between devices, split_heads_per_device(): lax.ppermute(sent, ('pipe',) + plane, crossing_back((pipes, rows, cols),...  9.32 us
    ppermute x6, starting transfers between devices, split_heads_per_device(): lax.ppermute(packets[step - 1], plane, crossing(sizes, step, 0))  8.3 us
    ppermute x4, starting transfers between devices, split_heads_per_device(): lax.ppermute(sent, ('pipe',) + plane, crossing_back((pipes, rows, cols),...  7.86 us
    ppermute x6, waiting for transfers between devices, split_heads_per_device(): lax.ppermute(packets[step - 1], plane, crossing(sizes, step, 0))  7.67 us
    ppermute x1, starting transfers between devices, split_heads_per_device(): x_ahead = lax.ppermute(free_x, 'pipe', behind)  4.1 us
    pallas_call x1, Pallas kernels, split_heads_per_device(): local_call(functools.partial(pack_kernel, rows, heads), packets, staged,...  1.49 us
    ppermute x2, waiting for transfers between devices, split_heads_per_device(): lax.ppermute(given.astype(jnp.float16), plane, crossing(sizes, 0, 1))  1.3 us
    ppermute x4, starting transfers between devices, swap(): return lax.ppermute(array, plane, crossing(sizes, 0, 1))  1.17 us
  transfers between devices with their start and end apart: 17, of which 10 were waited for; matrix products, arithmetic and copies ran while one was open for 1% of the time, Pallas kernels for 1%

profile of v3, /device:TPU:0, one launch (start us, length us, event | category | flops | bytes accessed | tf_op | source)
XLA Modules:
  0.0 45.3 jit_solution(17417293893863849156)
XLA Ops:
  0.0 1.5 %shard_map.37 = (bf16[4,272,128]{2,1,0:T(8,128)(2,1)S(1)}, bf16[4,272,128]{2,1,0:T(8,128)(2,1)S(1)}, bf16[4,256,128]{2,1,0:T(8,128)(2,1)S(1)}, bf16[4,256,128]{2,1,0:T(8,128)(2,1)S(1)}) custom-call(bf16[128,2048]{1,0:T(8,128)(2,1)} %bitcast.41, bf16[128,2048]{1,0:T(8,128)(2,1)} %bitcast.40), custom_call_target="tpu_custom_call" | custom-call | tf_op jit(solution)/shard_map/pallas_call | solution.py:607
  1.5 0.5 %collective-permute-start.6 = (bf16[1,272,128]{2,1,0:T(8,128)(2,1)S(1)}, bf16[1,272,128]{2,1,0:T(8,128)(2,1)S(1)}, u32[]{:S(2)}, u32[]{:S(2)}) collective-permute-start(bf16[1,272,128]{2,1,0:T(8,128)(2,1)S(1)} %get-tuple-element.44), channel_id=1, source_target_pairs={{0,1},{1,0},{2,3},{3,2},{4,5},{5,4},{6,7},{7,6},{8,9},{9,8},{10,11... | collective-permute-start | bytes 208904 | tf_op jit(solution)/shard_map/ppermute | solution.py:612
  2.0 0.1 collective-permute-start.1
  2.1 0.5 %collective-permute-start.7 = (bf16[2,272,128]{2,1,0:T(8,128)(2,1)S(1)}, bf16[2,272,128]{2,1,0:T(8,128)(2,1)S(1)}, u32[]{:S(2)}, u32[]{:S(2)}) collective-permute-start(bf16[2,272,128]{2,1,0:T(8,128)(2,1)S(1)} %slice.100), channel_id=1, source_target_pairs={{0,1},{1,0},{2,3},{3,2},{4,5},{5,4},{6,7},{7,6},{8,9},{9,8},{10,11... | collective-permute-start | bytes 417800 | tf_op jit(solution)/shard_map/ppermute | solution.py:612
  2.6 0.1 collective-permute-start
  2.7 0.6 %collective-permute-done.1 = bf16[1,272,128]{2,1,0:T(8,128)(2,1)S(1)} collective-permute-done((bf16[1,272,128]{2,1,0:T(8,128)(2,1)S(1)}, bf16[1,272,128]{2,1,0:T(8,128)(2,1)S(1)}, u32[]{:S(2)}, u32[]{:S(2)}) %collective-permute-start.1) | collective-permute-done | bytes 69664 | tf_op jit(solution)/shard_map/ppermute | solution.py:612
  3.3 2.7 %collective-permute-start.2 = (bf16[2,272,128]{2,1,0:T(8,128)(2,1)S(1)}, bf16[2,272,128]{2,1,0:T(8,128)(2,1)S(1)}, u32[]{:S(2)}, u32[]{:S(2)}) collective-permute-start(bf16[2,272,128]{2,1,0:T(8,128)(2,1)S(1)} %pad_maximum_fusion), channel_id=1, source_target_pairs={{0,2},{1,3},{2,0},{3,1},{4,6},{5,7},{6,4},{7,5},{8,10},{9,11},{10,... | collective-permute-start | bytes 417800 | tf_op jit(solution)/shard_map/ppermute | solution.py:629
  6.0 0.0 collective-permute-done.7
  6.1 1.6 %collective-permute-start.8 = (bf16[2,272,128]{2,1,0:T(8,128)(2,1)S(1)}, bf16[2,272,128]{2,1,0:T(8,128)(2,1)S(1)}, u32[]{:S(2)}, u32[]{:S(2)}) collective-permute-start(bf16[2,272,128]{2,1,0:T(8,128)(2,1)S(1)} %pad_maximum_fusion.1), channel_id=1, source_target_pairs={{0,4},{1,5},{2,6},{3,7},{4,0},{5,1},{6,2},{7,3},{8,12},{9,13},{10,... | collective-permute-start | bytes 417800 | tf_op jit(solution)/shard_map/ppermute | solution.py:629
  7.7 0.0 copy-start
  7.7 0.5 collective-permute-start.9
  8.1 0.0 collective-permute-done.operands_2_
  8.2 0.0 copy-start.1
  8.2 2.1 %collective-permute-done.2.operands_3_ = bf16[2,272,128]{2,1,0:T(8,128)(2,1)S(1)} collective-permute-done((bf16[2,272,128]{2,1,0:T(8,128)(2,1)S(1)}, bf16[2,272,128]{2,1,0:T(8,128)(2,1)S(1)}, u32[]{:S(2)}, u32[]{:S(2)}) %collective-permute-start.2) | collective-permute-done | bytes 139296 | tf_op jit(solution)/shard_map/ppermute | solution.py:629
  10.3 0.0 copy-done
  10.3 4.1 %collective-permute-start.10 = (bf16[128,2048]{1,0:T(8,128)(2,1)S(1)}, bf16[128,2048]{1,0:T(8,128)(2,1)S(1)}, u32[]{:S(2)}, u32[]{:S(2)}) collective-permute-start(bf16[128,2048]{1,0:T(8,128)(2,1)S(1)} %bitcast.42), channel_id=1, source_target_pairs={{0,24},{8,0},{16,8},{24,16},{1,25},{9,1},{17,9},{25,17},{2,26},{10... | collective-permute-start | bytes 1572872 | tf_op jit(solution)/shard_map/ppermute | solution.py:649
  14.4 0.0 copy-done.1
  14.4 1.8 %collective-permute-start.3 = (bf16[2,256,128]{2,1,0:T(8,128)(2,1)S(1)}, bf16[2,256,128]{2,1,0:T(8,128)(2,1)S(1)}, u32[]{:S(2)}, u32[]{:S(2)}) collective-permute-start(bf16[2,256,128]{2,1,0:T(8,128)(2,1)S(1)} %get-tuple-element.27), channel_id=1, source_target_pairs={{0,2},{1,3},{2,0},{3,1},{4,6},{5,7},{6,4},{7,5},{8,10},{9,11},{10,... | collective-permute-start | bytes 393224 | tf_op jit(solution)/shard_map/ppermute | solution.py:629
  16.2 0.0 collective-permute-done.6.operands_2_
  16.2 1.5 %collective-permute-start.4 = (bf16[2,256,128]{2,1,0:T(8,128)(2,1)S(1)}, bf16[2,256,128]{2,1,0:T(8,128)(2,1)S(1)}, u32[]{:S(2)}, u32[]{:S(2)}) collective-permute-start(bf16[2,256,128]{2,1,0:T(8,128)(2,1)S(1)} %get-tuple-element.28), channel_id=1, source_target_pairs={{0,4},{1,5},{2,6},{3,7},{4,0},{5,1},{6,2},{7,3},{8,12},{9,13},{10,... | collective-permute-start | bytes 393224 | tf_op jit(solution)/shard_map/ppermute | solution.py:629
  17.7 0.0 collective-permute-done.8.operands_4_
  17.7 0.2 collective-permute-start.5
  18.0 0.0 collective-permute-done.9.operands_5_
  18.0 0.1 collective-permute-start.11
  18.1 2.4 %collective-permute-done.3.operands_3_ = bf16[2,256,128]{2,1,0:T(8,128)(2,1)S(1)} collective-permute-done((bf16[2,256,128]{2,1,0:T(8,128)(2,1)S(1)}, bf16[2,256,128]{2,1,0:T(8,128)(2,1)S(1)}, u32[]{:S(2)}, u32[]{:S(2)}) %collective-permute-start.3) | collective-permute-done | bytes 131104 | tf_op jit(solution)/shard_map/ppermute | solution.py:629
  20.5 3.2 %collective-permute-done.4.operands_4_ = bf16[2,256,128]{2,1,0:T(8,128)(2,1)S(1)} collective-permute-done((bf16[2,256,128]{2,1,0:T(8,128)(2,1)S(1)}, bf16[2,256,128]{2,1,0:T(8,128)(2,1)S(1)}, u32[]{:S(2)}, u32[]{:S(2)}) %collective-permute-start.4) | collective-permute-done | bytes 131104 | tf_op jit(solution)/shard_map/ppermute | solution.py:629
  23.7 0.0 collective-permute-done.5.operands_5_
  23.8 1.1 %collective-permute-done.10.x_ref = bf16[128,2048]{1,0:T(8,128)(2,1)S(1)} collective-permute-done((bf16[128,2048]{1,0:T(8,128)(2,1)S(1)}, bf16[128,2048]{1,0:T(8,128)(2,1)S(1)}, u32[]{:S(2)}, u32[]{:S(2)}) %collective-permute-start.10) | collective-permute-done | bytes 524320 | tf_op jit(solution)/shard_map/ppermute | solution.py:649
  25.0 0.1 collective-permute-start.12
  25.1 0.0 collective-permute-done.11
  25.1 1.3 %collective-permute-done.12 = f16[4,136,128]{2,1,0:T(8,128)(2,1)S(1)} collective-permute-done((f16[4,136,128]{2,1,0:T(8,128)(2,1)S(1)}, f16[4,136,128]{2,1,0:T(8,128)(2,1)S(1)}, u32[]{:S(2)}, u32[]{:S(2)}) %collective-permute-start.12) | collective-permute-done | bytes 139296 | tf_op jit(solution)/shard_map/ppermute | solution.py:667
  26.4 0.1 pad_maximum_fusion.3
  26.5 4.5 %collective-permute-start.13 = (f16[528,128]{1,0:T(8,128)(2,1)S(1)}, f16[528,128]{1,0:T(8,128)(2,1)S(1)}, u32[]{:S(2)}, u32[]{:S(2)}) collective-permute-start(f16[528,128]{1,0:T(8,128)(2,1)S(1)} %pad_maximum_fusion.3), channel_id=1, source_target_pairs={{0,24},{1,25},{2,26},{3,27},{4,28},{5,29},{6,30},{7,31},{8,0},{9,1... | collective-permute-start | bytes 405512 | tf_op jit(solution)/shard_map/ppermute | solution.py:671
  31.0 0.1 pad_maximum_fusion.4
  31.1 1.9 %collective-permute-start.14 = (f16[528,128]{1,0:T(8,128)(2,1)S(1)}, f16[528,128]{1,0:T(8,128)(2,1)S(1)}, u32[]{:S(2)}, u32[]{:S(2)}) collective-permute-start(f16[528,128]{1,0:T(8,128)(2,1)S(1)} %pad_maximum_fusion.4), channel_id=1, source_target_pairs={{0,26},{1,27},{2,24},{3,25},{4,30},{5,31},{6,28},{7,29},{8,2},{9,3... | collective-permute-start | bytes 405512 | tf_op jit(solution)/shard_map/ppermute | solution.py:671
  33.0 0.1 pad_maximum_fusion.5
  33.0 0.1 collective-permute-start.15
  33.1 0.1 pad_maximum_fusion.6
  33.1 1.4 %collective-permute-start.16 = (f16[528,128]{1,0:T(8,128)(2,1)S(1)}, f16[528,128]{1,0:T(8,128)(2,1)S(1)}, u32[]{:S(2)}, u32[]{:S(2)}) collective-permute-start(f16[528,128]{1,0:T(8,128)(2,1)S(1)} %pad_maximum_fusion.6), channel_id=1, source_target_pairs={{0,30},{1,31},{2,28},{3,29},{4,26},{5,27},{6,24},{7,25},{8,6},{9,7... | collective-permute-start | bytes 405512 | tf_op jit(solution)/shard_map/ppermute | solution.py:671
  34.5 0.3 shard_map.40.cube_ref
  34.8 0.1 collective-permute-done.13
  35.0 3.5 %collective-permute-done.14 = f16[528,128]{1,0:T(8,128)(2,1)S(1)} collective-permute-done((f16[528,128]{1,0:T(8,128)(2,1)S(1)}, f16[528,128]{1,0:T(8,128)(2,1)S(1)}, u32[]{:S(2)}, u32[]{:S(2)}) %collective-permute-start.14) | collective-permute-done | bytes 135200 | tf_op jit(solution)/shard_map/ppermute | solution.py:671
  38.5 3.7 %collective-permute-done.15 = f16[528,128]{1,0:T(8,128)(2,1)S(1)} collective-permute-done((f16[528,128]{1,0:T(8,128)(2,1)S(1)}, f16[528,128]{1,0:T(8,128)(2,1)S(1)}, u32[]{:S(2)}, u32[]{:S(2)}) %collective-permute-start.15) | collective-permute-done | bytes 135200 | tf_op jit(solution)/shard_map/ppermute | solution.py:671
  42.2 2.0 %collective-permute-done.16 = f16[528,128]{1,0:T(8,128)(2,1)S(1)} collective-permute-done((f16[528,128]{1,0:T(8,128)(2,1)S(1)}, f16[528,128]{1,0:T(8,128)(2,1)S(1)}, u32[]{:S(2)}, u32[]{:S(2)}) %collective-permute-start.16) | collective-permute-done | bytes 135200 | tf_op jit(solution)/shard_map/ppermute | solution.py:671
  44.2 1.1 %shard_map.41 = bf16[128,2048]{1,0:T(8,128)(2,1)} custom-call(bf16[128,2048]{1,0:T(8,128)(2,1)S(1)} %collective-permute-done.10.x_ref, f32[128,128]{1,0:T(8,128)S(1)} %shard_map.40.cube_ref, f32[528,128]{1,0:T(8,128)S(1)} %convert_element_type.28.refs_0_, f32[528,128]{1,0:T(8,128)S(1)} %convert_element_type.29.refs_1_, ...), custom_call_target="tpu_custom_call" | custom-call | tf_op jit(solution)/shard_map/pallas_call | solution.py:674
  (26 shorter events, 0.5 us)
Async XLA Ops:
  1.5 14.7 %collective-permute-start.6 = (bf16[1,272,128]{2,1,0:T(8,128)(2,1)S(1)}, bf16[1,272,128]{2,1,0:T(8,128)(2,1)S(1)}, u32[]{:S(2)}, u32[]{:S(2)}) collective-permute-start(bf16[1,272,128]{2,1,0:T(8,128)(2,1)S(1)} %get-tuple-element.44), channel_id=1, source_target_pairs={{0,1},{1,0},{2,3},{3,2},{4,5},{5,4},{6,7},{7,6},{8,9},{9,8},{10,11... | collective-permute-start | bytes 208904 | tf_op jit(solution)/shard_map/ppermute | solution.py:612
  2.0 1.3 %collective-permute-start.1 = (bf16[1,272,128]{2,1,0:T(8,128)(2,1)S(1)}, bf16[1,272,128]{2,1,0:T(8,128)(2,1)S(1)}, u32[]{:S(2)}, u32[]{:S(2)}) collective-permute-start(bf16[1,272,128]{2,1,0:T(8,128)(2,1)S(1)} %get-tuple-element.45), channel_id=1, source_target_pairs={{0,1},{1,0},{2,3},{3,2},{4,5},{5,4},{6,7},{7,6},{8,9},{9,8},{10,11... | collective-permute-start | bytes 208904 | tf_op jit(solution)/shard_map/ppermute | solution.py:612
  2.1 3.9 %collective-permute-start.7 = (bf16[2,272,128]{2,1,0:T(8,128)(2,1)S(1)}, bf16[2,272,128]{2,1,0:T(8,128)(2,1)S(1)}, u32[]{:S(2)}, u32[]{:S(2)}) collective-permute-start(bf16[2,272,128]{2,1,0:T(8,128)(2,1)S(1)} %slice.100), channel_id=1, source_target_pairs={{0,1},{1,0},{2,3},{3,2},{4,5},{5,4},{6,7},{7,6},{8,9},{9,8},{10,11... | collective-permute-start | bytes 417800 | tf_op jit(solution)/shard_map/ppermute | solution.py:612
  2.6 5.5 %collective-permute-start = (bf16[4,256,128]{2,1,0:T(8,128)(2,1)S(1)}, bf16[4,256,128]{2,1,0:T(8,128)(2,1)S(1)}, u32[]{:S(2)}, u32[]{:S(2)}) collective-permute-start(bf16[4,256,128]{2,1,0:T(8,128)(2,1)S(1)} %get-tuple-element.24), channel_id=1, source_target_pairs={{0,1},{1,0},{2,3},{3,2},{4,5},{5,4},{6,7},{7,6},{8,9},{9,8},{10,11... | collective-permute-start | bytes 786440 | tf_op jit(solution)/shard_map/ppermute | solution.py:612
  3.3 7.0 %collective-permute-start.2 = (bf16[2,272,128]{2,1,0:T(8,128)(2,1)S(1)}, bf16[2,272,128]{2,1,0:T(8,128)(2,1)S(1)}, u32[]{:S(2)}, u32[]{:S(2)}) collective-permute-start(bf16[2,272,128]{2,1,0:T(8,128)(2,1)S(1)} %pad_maximum_fusion), channel_id=1, source_target_pairs={{0,2},{1,3},{2,0},{3,1},{4,6},{5,7},{6,4},{7,5},{8,10},{9,11},{10,... | collective-permute-start | bytes 417800 | tf_op jit(solution)/shard_map/ppermute | solution.py:629
  6.1 11.7 %collective-permute-start.8 = (bf16[2,272,128]{2,1,0:T(8,128)(2,1)S(1)}, bf16[2,272,128]{2,1,0:T(8,128)(2,1)S(1)}, u32[]{:S(2)}, u32[]{:S(2)}) collective-permute-start(bf16[2,272,128]{2,1,0:T(8,128)(2,1)S(1)} %pad_maximum_fusion.1), channel_id=1, source_target_pairs={{0,4},{1,5},{2,6},{3,7},{4,0},{5,1},{6,2},{7,3},{8,12},{9,13},{10,... | collective-permute-start | bytes 417800 | tf_op jit(solution)/shard_map/ppermute | solution.py:629
  7.7 2.6 %copy-start = (bf16[1,8,16,2048]{3,2,1,0:T(8,128)(2,1)S(1)}, bf16[1,8,16,2048]{3,2,1,0:T(8,128)(2,1)}, u32[]{:S(2)}) copy-start(bf16[1,8,16,2048]{3,2,1,0:T(8,128)(2,1)} %param.3) | copy-start | bytes 1572868
  7.7 10.3 %collective-permute-start.9 = (bf16[2,272,128]{2,1,0:T(8,128)(2,1)S(1)}, bf16[2,272,128]{2,1,0:T(8,128)(2,1)S(1)}, u32[]{:S(2)}, u32[]{:S(2)}) collective-permute-start(bf16[2,272,128]{2,1,0:T(8,128)(2,1)S(1)} %pad_maximum_fusion.2), channel_id=1, source_target_pairs={{0,6},{1,7},{2,4},{3,5},{4,2},{5,3},{6,0},{7,1},{8,14},{9,15},{10,... | collective-permute-start | bytes 417800 | tf_op jit(solution)/shard_map/ppermute | solution.py:629
  8.2 6.2 %copy-start.1 = (f32[1,5,2048]{2,0,1:T(1,128)S(1)}, f32[1,5,2048]{2,0,1:T(1,128)}, u32[]{:S(2)}) copy-start(f32[1,5,2048]{2,0,1:T(1,128)} %param.5) | copy-start | bytes 122884
  10.3 14.7 %collective-permute-start.10 = (bf16[128,2048]{1,0:T(8,128)(2,1)S(1)}, bf16[128,2048]{1,0:T(8,128)(2,1)S(1)}, u32[]{:S(2)}, u32[]{:S(2)}) collective-permute-start(bf16[128,2048]{1,0:T(8,128)(2,1)S(1)} %bitcast.42), channel_id=1, source_target_pairs={{0,24},{8,0},{16,8},{24,16},{1,25},{9,1},{17,9},{25,17},{2,26},{10... | collective-permute-start | bytes 1572872 | tf_op jit(solution)/shard_map/ppermute | solution.py:649
  14.4 6.1 %collective-permute-start.3 = (bf16[2,256,128]{2,1,0:T(8,128)(2,1)S(1)}, bf16[2,256,128]{2,1,0:T(8,128)(2,1)S(1)}, u32[]{:S(2)}, u32[]{:S(2)}) collective-permute-start(bf16[2,256,128]{2,1,0:T(8,128)(2,1)S(1)} %get-tuple-element.27), channel_id=1, source_target_pairs={{0,2},{1,3},{2,0},{3,1},{4,6},{5,7},{6,4},{7,5},{8,10},{9,11},{10,... | collective-permute-start | bytes 393224 | tf_op jit(solution)/shard_map/ppermute | solution.py:629
  16.2 7.5 %collective-permute-start.4 = (bf16[2,256,128]{2,1,0:T(8,128)(2,1)S(1)}, bf16[2,256,128]{2,1,0:T(8,128)(2,1)S(1)}, u32[]{:S(2)}, u32[]{:S(2)}) collective-permute-start(bf16[2,256,128]{2,1,0:T(8,128)(2,1)S(1)} %get-tuple-element.28), channel_id=1, source_target_pairs={{0,4},{1,5},{2,6},{3,7},{4,0},{5,1},{6,2},{7,3},{8,12},{9,13},{10,... | collective-permute-start | bytes 393224 | tf_op jit(solution)/shard_map/ppermute | solution.py:629
  17.7 6.0 %collective-permute-start.5 = (bf16[2,256,128]{2,1,0:T(8,128)(2,1)S(1)}, bf16[2,256,128]{2,1,0:T(8,128)(2,1)S(1)}, u32[]{:S(2)}, u32[]{:S(2)}) collective-permute-start(bf16[2,256,128]{2,1,0:T(8,128)(2,1)S(1)} %pad_maximum_fusion.9), channel_id=1, source_target_pairs={{0,6},{1,7},{2,4},{3,5},{4,2},{5,3},{6,0},{7,1},{8,14},{9,15},{10,... | collective-permute-start | bytes 393224 | tf_op jit(solution)/shard_map/ppermute | solution.py:629
  18.0 7.0 %collective-permute-start.11 = (f16[4,128,128]{2,1,0:T(8,128)(2,1)S(1)}, f16[4,128,128]{2,1,0:T(8,128)(2,1)S(1)}, u32[]{:S(2)}, u32[]{:S(2)}) collective-permute-start(f16[4,128,128]{2,1,0:T(8,128)(2,1)S(1)} %convert_element_type.26), channel_id=1, source_target_pairs={{0,1},{1,0},{2,3},{3,2},{4,5},{5,4},{6,7},{7,6},{8,9},{9,8},{10,11... | collective-permute-start | bytes 393224 | tf_op jit(solution)/shard_map/ppermute | solution.py:667
  25.0 1.4 %collective-permute-start.12 = (f16[4,136,128]{2,1,0:T(8,128)(2,1)S(1)}, f16[4,136,128]{2,1,0:T(8,128)(2,1)S(1)}, u32[]{:S(2)}, u32[]{:S(2)}) collective-permute-start(f16[4,136,128]{2,1,0:T(8,128)(2,1)S(1)} %convert_element_type.27), channel_id=1, source_target_pairs={{0,1},{1,0},{2,3},{3,2},{4,5},{5,4},{6,7},{7,6},{8,9},{9,8},{10,11... | collective-permute-start | bytes 417800 | tf_op jit(solution)/shard_map/ppermute | solution.py:667
  26.5 8.4 %collective-permute-start.13 = (f16[528,128]{1,0:T(8,128)(2,1)S(1)}, f16[528,128]{1,0:T(8,128)(2,1)S(1)}, u32[]{:S(2)}, u32[]{:S(2)}) collective-permute-start(f16[528,128]{1,0:T(8,128)(2,1)S(1)} %pad_maximum_fusion.3), channel_id=1, source_target_pairs={{0,24},{1,25},{2,26},{3,27},{4,28},{5,29},{6,30},{7,31},{8,0},{9,1... | collective-permute-start | bytes 405512 | tf_op jit(solution)/shard_map/ppermute | solution.py:671
  31.1 7.4 %collective-permute-start.14 = (f16[528,128]{1,0:T(8,128)(2,1)S(1)}, f16[528,128]{1,0:T(8,128)(2,1)S(1)}, u32[]{:S(2)}, u32[]{:S(2)}) collective-permute-start(f16[528,128]{1,0:T(8,128)(2,1)S(1)} %pad_maximum_fusion.4), channel_id=1, source_target_pairs={{0,26},{1,27},{2,24},{3,25},{4,30},{5,31},{6,28},{7,29},{8,2},{9,3... | collective-permute-start | bytes 405512 | tf_op jit(solution)/shard_map/ppermute | solution.py:671
  33.0 9.2 %collective-permute-start.15 = (f16[528,128]{1,0:T(8,128)(2,1)S(1)}, f16[528,128]{1,0:T(8,128)(2,1)S(1)}, u32[]{:S(2)}, u32[]{:S(2)}) collective-permute-start(f16[528,128]{1,0:T(8,128)(2,1)S(1)} %pad_maximum_fusion.5), channel_id=1, source_target_pairs={{0,28},{1,29},{2,30},{3,31},{4,24},{5,25},{6,26},{7,27},{8,4},{9,5... | collective-permute-start | bytes 405512 | tf_op jit(solution)/shard_map/ppermute | solution.py:671
  33.1 11.1 %collective-permute-start.16 = (f16[528,128]{1,0:T(8,128)(2,1)S(1)}, f16[528,128]{1,0:T(8,128)(2,1)S(1)}, u32[]{:S(2)}, u32[]{:S(2)}) collective-permute-start(f16[528,128]{1,0:T(8,128)(2,1)S(1)} %pad_maximum_fusion.6), channel_id=1, source_target_pairs={{0,30},{1,31},{2,28},{3,29},{4,26},{5,27},{6,24},{7,25},{8,6},{9,7... | collective-permute-start | bytes 405512 | tf_op jit(solution)/shard_map/ppermute | solution.py:671

commit v4 on v3

--- a/solution.py
+++ b/solution.py
@@ -536,10 +536,13 @@
 
 def cube_kernel(x_ref, out_ref):
     inverse = inverse_row(x_ref)
-    out_ref[...] = row_to_column(inverse * inverse * inverse)
-
-
-def collect_kernel(rows, heads, x_ref, cube_ref, *refs):
+    cube = row_to_column(inverse * inverse * inverse)
+    for lane in range(0, x_ref.shape[1], HEAD_DIM):
+        lanes = slice(lane, lane + HEAD_DIM)
+        out_ref[:, lanes] = x_ref[:, lanes].astype(jnp.float32) * cube
+
+
+def collect_kernel(rows, heads, x_ref, *refs):
     units = refs[:rows]
     out_hbm, out_ref, sems = refs[rows:]
     tokens, channels = x_ref.shape
@@ -556,7 +559,7 @@
                 scales[step, half * heads + head] = value[4 + head : 5 + head]
             share = (extra[1:2] + extra[2:3] + extra[3:4]) * value[0:1]
             total = share if total is None else total + share
-    weight = cube_ref[...] * row_to_column(total / channels)
+    mean = row_to_column(total / channels)
     wide = 2 * heads * HEAD_DIM
     copies = []
     for step in range(rows):
@@ -565,7 +568,7 @@
             lanes = pl.ds(pl.multiple_of(first * HEAD_DIM, HEAD_DIM), HEAD_DIM)
             top = slot // heads * side + slot % heads * tokens
             part = units[step][top : top + tokens, :] * scales[step, slot]
-            grad = part - x_ref[:, lanes].astype(jnp.float32) * weight
+            grad = part - x_ref[:, lanes] * mean
             out_ref[:, lanes] = jnp.where(last, 0.0, grad).astype(jnp.bfloat16)
         lanes = pl.ds(pl.multiple_of((row ^ step) * wide, wide), wide)
         copies.append(pltpu.make_async_copy(out_ref.at[:, lanes], out_hbm.at[:, lanes], sems.at[step]))
@@ -670,13 +673,13 @@
         sent = jnp.concatenate([unit[step] for unit in keep + got])
         sent = lax.ppermute(sent, ("pipe",) + plane, crossing_back((pipes, rows, cols), step))
         units.append(sent.astype(f32))
-    cube = local_call(cube_kernel, pltpu.VMEM((tokens, HEAD_DIM), f32))(*near([x_ahead]))
+    cubed = local_call(cube_kernel, pltpu.VMEM((tokens, channels), f32))(*near([x_ahead]))
     out = local_call(
         functools.partial(collect_kernel, rows, heads),
         jax.ShapeDtypeStruct((tokens, channels), bf),
         [pltpu.VMEM((tokens, channels), bf), pltpu.SemaphoreType.DMA((rows,))],
         out_specs=far,
-    )(*near([x_ahead, cube] + units))
+    )(*near([cubed] + units))
     return out.reshape(saved_in.shape)
 
 

time: 45.5 us -> 45.5 us (level)
  no operation moved by 1% of the time
where the time goes in v4:
time: 45.5 us; the launch traced here: 45.3 us
  starting transfers between devices  21.6 us (47%)
  waiting for transfers between devices  19.9 us (44%)
  Pallas kernels  2.87 us (6%)
  other arithmetic  0.46 us (1%)
    ppermute x4, waiting for transfers between devices, split_heads_per_device(): lax.ppermute(sent, ('pipe',) + plane, crossing_back((pipes, rows, cols),...  9.26 us
    ppermute x6, starting transfers between devices, split_heads_per_device(): lax.ppermute(packets[step - 1], plane, crossing(sizes, step, 0))  8.3 us
    ppermute x4, starting transfers between devices, split_heads_per_device(): lax.ppermute(sent, ('pipe',) + plane, crossing_back((pipes, rows, cols),...  7.88 us
    ppermute x6, waiting for transfers between devices, split_heads_per_device(): lax.ppermute(packets[step - 1], plane, crossing(sizes, step, 0))  7.67 us
    ppermute x1, starting transfers between devices, split_heads_per_device(): x_ahead = lax.ppermute(free_x, 'pipe', behind)  4.1 us
    pallas_call x1, Pallas kernels, split_heads_per_device(): local_call(functools.partial(pack_kernel, rows, heads), packets, staged,...  1.49 us
    ppermute x2, waiting for transfers between devices, split_heads_per_device(): lax.ppermute(given.astype(jnp.float16), plane, crossing(sizes, 0, 1))  1.3 us
    ppermute x4, starting transfers between devices, swap(): return lax.ppermute(array, plane, crossing(sizes, 0, 1))  1.17 us
  transfers between devices with their start and end apart: 17, of which 10 were waited for; matrix products, arithmetic and copies ran while one was open for 1% of the time, Pallas kernels for 1%

profile of v4, /device:TPU:0, one launch (start us, length us, event | category | flops | bytes accessed | tf_op | source)
XLA Modules:
  0.0 45.3 jit_solution(4285412396333960309)
XLA Ops:
  0.0 1.5 %shard_map.37 = (bf16[4,272,128]{2,1,0:T(8,128)(2,1)S(1)}, bf16[4,272,128]{2,1,0:T(8,128)(2,1)S(1)}, bf16[4,256,128]{2,1,0:T(8,128)(2,1)S(1)}, bf16[4,256,128]{2,1,0:T(8,128)(2,1)S(1)}) custom-call(bf16[128,2048]{1,0:T(8,128)(2,1)} %bitcast.41, bf16[128,2048]{1,0:T(8,128)(2,1)} %bitcast.40), custom_call_target="tpu_custom_call" | custom-call | tf_op jit(solution)/shard_map/pallas_call | solution.py:610
  1.5 0.5 %collective-permute-start.6 = (bf16[1,272,128]{2,1,0:T(8,128)(2,1)S(1)}, bf16[1,272,128]{2,1,0:T(8,128)(2,1)S(1)}, u32[]{:S(2)}, u32[]{:S(2)}) collective-permute-start(bf16[1,272,128]{2,1,0:T(8,128)(2,1)S(1)} %get-tuple-element.44), channel_id=1, source_target_pairs={{0,1},{1,0},{2,3},{3,2},{4,5},{5,4},{6,7},{7,6},{8,9},{9,8},{10,11... | collective-permute-start | bytes 208904 | tf_op jit(solution)/shard_map/ppermute | solution.py:615
  2.0 0.1 collective-permute-start.1
  2.1 0.5 %collective-permute-start.7 = (bf16[2,272,128]{2,1,0:T(8,128)(2,1)S(1)}, bf16[2,272,128]{2,1,0:T(8,128)(2,1)S(1)}, u32[]{:S(2)}, u32[]{:S(2)}) collective-permute-start(bf16[2,272,128]{2,1,0:T(8,128)(2,1)S(1)} %slice.100), channel_id=1, source_target_pairs={{0,1},{1,0},{2,3},{3,2},{4,5},{5,4},{6,7},{7,6},{8,9},{9,8},{10,11... | collective-permute-start | bytes 417800 | tf_op jit(solution)/shard_map/ppermute | solution.py:615
  2.6 0.1 collective-permute-start
  2.7 0.6 %collective-permute-done.1 = bf16[1,272,128]{2,1,0:T(8,128)(2,1)S(1)} collective-permute-done((bf16[1,272,128]{2,1,0:T(8,128)(2,1)S(1)}, bf16[1,272,128]{2,1,0:T(8,128)(2,1)S(1)}, u32[]{:S(2)}, u32[]{:S(2)}) %collective-permute-start.1) | collective-permute-done | bytes 69664 | tf_op jit(solution)/shard_map/ppermute | solution.py:615
  3.3 2.7 %collective-permute-start.2 = (bf16[2,272,128]{2,1,0:T(8,128)(2,1)S(1)}, bf16[2,272,128]{2,1,0:T(8,128)(2,1)S(1)}, u32[]{:S(2)}, u32[]{:S(2)}) collective-permute-start(bf16[2,272,128]{2,1,0:T(8,128)(2,1)S(1)} %pad_maximum_fusion), channel_id=1, source_target_pairs={{0,2},{1,3},{2,0},{3,1},{4,6},{5,7},{6,4},{7,5},{8,10},{9,11},{10,... | collective-permute-start | bytes 417800 | tf_op jit(solution)/shard_map/ppermute | solution.py:632
  6.0 0.0 collective-permute-done.7
  6.1 1.6 %collective-permute-start.8 = (bf16[2,272,128]{2,1,0:T(8,128)(2,1)S(1)}, bf16[2,272,128]{2,1,0:T(8,128)(2,1)S(1)}, u32[]{:S(2)}, u32[]{:S(2)}) collective-permute-start(bf16[2,272,128]{2,1,0:T(8,128)(2,1)S(1)} %pad_maximum_fusion.1), channel_id=1, source_target_pairs={{0,4},{1,5},{2,6},{3,7},{4,0},{5,1},{6,2},{7,3},{8,12},{9,13},{10,... | collective-permute-start | bytes 417800 | tf_op jit(solution)/shard_map/ppermute | solution.py:632
  7.7 0.0 copy-start
  7.7 0.5 collective-permute-start.9
  8.1 0.0 collective-permute-done.operands_2_
  8.2 0.0 copy-start.1
  8.2 2.1 %collective-permute-done.2.operands_3_ = bf16[2,272,128]{2,1,0:T(8,128)(2,1)S(1)} collective-permute-done((bf16[2,272,128]{2,1,0:T(8,128)(2,1)S(1)}, bf16[2,272,128]{2,1,0:T(8,128)(2,1)S(1)}, u32[]{:S(2)}, u32[]{:S(2)}) %collective-permute-start.2) | collective-permute-done | bytes 139296 | tf_op jit(solution)/shard_map/ppermute | solution.py:632
  10.3 0.0 copy-done
  10.3 4.1 %collective-permute-start.10 = (bf16[128,2048]{1,0:T(8,128)(2,1)S(1)}, bf16[128,2048]{1,0:T(8,128)(2,1)S(1)}, u32[]{:S(2)}, u32[]{:S(2)}) collective-permute-start(bf16[128,2048]{1,0:T(8,128)(2,1)S(1)} %bitcast.42), channel_id=1, source_target_pairs={{0,24},{8,0},{16,8},{24,16},{1,25},{9,1},{17,9},{25,17},{2,26},{10... | collective-permute-start | bytes 1572872 | tf_op jit(solution)/shard_map/ppermute | solution.py:652
  14.4 0.0 copy-done.1
  14.4 1.8 %collective-permute-start.3 = (bf16[2,256,128]{2,1,0:T(8,128)(2,1)S(1)}, bf16[2,256,128]{2,1,0:T(8,128)(2,1)S(1)}, u32[]{:S(2)}, u32[]{:S(2)}) collective-permute-start(bf16[2,256,128]{2,1,0:T(8,128)(2,1)S(1)} %get-tuple-element.27), channel_id=1, source_target_pairs={{0,2},{1,3},{2,0},{3,1},{4,6},{5,7},{6,4},{7,5},{8,10},{9,11},{10,... | collective-permute-start | bytes 393224 | tf_op jit(solution)/shard_map/ppermute | solution.py:632
  16.2 0.0 collective-permute-done.6.operands_2_
  16.2 1.5 %collective-permute-start.4 = (bf16[2,256,128]{2,1,0:T(8,128)(2,1)S(1)}, bf16[2,256,128]{2,1,0:T(8,128)(2,1)S(1)}, u32[]{:S(2)}, u32[]{:S(2)}) collective-permute-start(bf16[2,256,128]{2,1,0:T(8,128)(2,1)S(1)} %get-tuple-element.28), channel_id=1, source_target_pairs={{0,4},{1,5},{2,6},{3,7},{4,0},{5,1},{6,2},{7,3},{8,12},{9,13},{10,... | collective-permute-start | bytes 393224 | tf_op jit(solution)/shard_map/ppermute | solution.py:632
  17.7 0.0 collective-permute-done.8.operands_4_
  17.7 0.2 collective-permute-start.5
  18.0 0.0 collective-permute-done.9.operands_5_
  18.0 0.1 collective-permute-start.11
  18.1 2.4 %collective-permute-done.3.operands_3_ = bf16[2,256,128]{2,1,0:T(8,128)(2,1)S(1)} collective-permute-done((bf16[2,256,128]{2,1,0:T(8,128)(2,1)S(1)}, bf16[2,256,128]{2,1,0:T(8,128)(2,1)S(1)}, u32[]{:S(2)}, u32[]{:S(2)}) %collective-permute-start.3) | collective-permute-done | bytes 131104 | tf_op jit(solution)/shard_map/ppermute | solution.py:632
  20.5 3.2 %collective-permute-done.4.operands_4_ = bf16[2,256,128]{2,1,0:T(8,128)(2,1)S(1)} collective-permute-done((bf16[2,256,128]{2,1,0:T(8,128)(2,1)S(1)}, bf16[2,256,128]{2,1,0:T(8,128)(2,1)S(1)}, u32[]{:S(2)}, u32[]{:S(2)}) %collective-permute-start.4) | collective-permute-done | bytes 131104 | tf_op jit(solution)/shard_map/ppermute | solution.py:632
  23.7 0.0 collective-permute-done.5.operands_5_
  23.8 1.1 %collective-permute-done.10.x_ref = bf16[128,2048]{1,0:T(8,128)(2,1)S(1)} collective-permute-done((bf16[128,2048]{1,0:T(8,128)(2,1)S(1)}, bf16[128,2048]{1,0:T(8,128)(2,1)S(1)}, u32[]{:S(2)}, u32[]{:S(2)}) %collective-permute-start.10) | collective-permute-done | bytes 524320 | tf_op jit(solution)/shard_map/ppermute | solution.py:652
  25.0 0.1 collective-permute-start.12
  25.1 0.0 collective-permute-done.11
  25.1 1.3 %collective-permute-done.12 = f16[4,136,128]{2,1,0:T(8,128)(2,1)S(1)} collective-permute-done((f16[4,136,128]{2,1,0:T(8,128)(2,1)S(1)}, f16[4,136,128]{2,1,0:T(8,128)(2,1)S(1)}, u32[]{:S(2)}, u32[]{:S(2)}) %collective-permute-start.12) | collective-permute-done | bytes 139296 | tf_op jit(solution)/shard_map/ppermute | solution.py:670
  26.4 0.1 pad_maximum_fusion.3
  26.5 4.5 %collective-permute-start.13 = (f16[528,128]{1,0:T(8,128)(2,1)S(1)}, f16[528,128]{1,0:T(8,128)(2,1)S(1)}, u32[]{:S(2)}, u32[]{:S(2)}) collective-permute-start(f16[528,128]{1,0:T(8,128)(2,1)S(1)} %pad_maximum_fusion.3), channel_id=1, source_target_pairs={{0,24},{1,25},{2,26},{3,27},{4,28},{5,29},{6,30},{7,31},{8,0},{9,1... | collective-permute-start | bytes 405512 | tf_op jit(solution)/shard_map/ppermute | solution.py:674
  31.1 0.1 pad_maximum_fusion.4
  31.1 1.9 %collective-permute-start.14 = (f16[528,128]{1,0:T(8,128)(2,1)S(1)}, f16[528,128]{1,0:T(8,128)(2,1)S(1)}, u32[]{:S(2)}, u32[]{:S(2)}) collective-permute-start(f16[528,128]{1,0:T(8,128)(2,1)S(1)} %pad_maximum_fusion.4), channel_id=1, source_target_pairs={{0,26},{1,27},{2,24},{3,25},{4,30},{5,31},{6,28},{7,29},{8,2},{9,3... | collective-permute-start | bytes 405512 | tf_op jit(solution)/shard_map/ppermute | solution.py:674
  33.0 0.1 pad_maximum_fusion.5
  33.0 0.1 collective-permute-start.15
  33.1 0.1 pad_maximum_fusion.6
  33.2 1.4 %collective-permute-start.16 = (f16[528,128]{1,0:T(8,128)(2,1)S(1)}, f16[528,128]{1,0:T(8,128)(2,1)S(1)}, u32[]{:S(2)}, u32[]{:S(2)}) collective-permute-start(f16[528,128]{1,0:T(8,128)(2,1)S(1)} %pad_maximum_fusion.6), channel_id=1, source_target_pairs={{0,30},{1,31},{2,28},{3,29},{4,26},{5,27},{6,24},{7,25},{8,6},{9,7... | collective-permute-start | bytes 405512 | tf_op jit(solution)/shard_map/ppermute | solution.py:674
  34.6 0.3 shard_map.40.x_ref
  34.9 0.1 collective-permute-done.13
  35.0 3.5 %collective-permute-done.14 = f16[528,128]{1,0:T(8,128)(2,1)S(1)} collective-permute-done((f16[528,128]{1,0:T(8,128)(2,1)S(1)}, f16[528,128]{1,0:T(8,128)(2,1)S(1)}, u32[]{:S(2)}, u32[]{:S(2)}) %collective-permute-start.14) | collective-permute-done | bytes 135200 | tf_op jit(solution)/shard_map/ppermute | solution.py:674
  38.5 3.7 %collective-permute-done.15 = f16[528,128]{1,0:T(8,128)(2,1)S(1)} collective-permute-done((f16[528,128]{1,0:T(8,128)(2,1)S(1)}, f16[528,128]{1,0:T(8,128)(2,1)S(1)}, u32[]{:S(2)}, u32[]{:S(2)}) %collective-permute-start.15) | collective-permute-done | bytes 135200 | tf_op jit(solution)/shard_map/ppermute | solution.py:674
  42.2 2.0 %collective-permute-done.16 = f16[528,128]{1,0:T(8,128)(2,1)S(1)} collective-permute-done((f16[528,128]{1,0:T(8,128)(2,1)S(1)}, f16[528,128]{1,0:T(8,128)(2,1)S(1)}, u32[]{:S(2)}, u32[]{:S(2)}) %collective-permute-start.16) | collective-permute-done | bytes 135200 | tf_op jit(solution)/shard_map/ppermute | solution.py:674
  44.3 1.1 %shard_map.41 = bf16[128,2048]{1,0:T(8,128)(2,1)} custom-call(f32[128,2048]{1,0:T(8,128)S(1)} %shard_map.40.x_ref, f32[528,128]{1,0:T(8,128)S(1)} %convert_element_type.28.refs_0_, f32[528,128]{1,0:T(8,128)S(1)} %convert_element_type.29.refs_1_, f32[528,128]{1,0:T(8,128)S(1)} %convert_element_type.30.refs_2_, f32[528,128]{1,0:T(8,128)S(1)} %convert_element_type.31.refs_3_), custom_call_target="tpu_custom_call" | custom-call | tf_op jit(solution)/shard_map/pallas_call | solution.py:677
  (26 shorter events, 0.5 us)
Async XLA Ops:
  1.5 14.7 %collective-permute-start.6 = (bf16[1,272,128]{2,1,0:T(8,128)(2,1)S(1)}, bf16[1,272,128]{2,1,0:T(8,128)(2,1)S(1)}, u32[]{:S(2)}, u32[]{:S(2)}) collective-permute-start(bf16[1,272,128]{2,1,0:T(8,128)(2,1)S(1)} %get-tuple-element.44), channel_id=1, source_target_pairs={{0,1},{1,0},{2,3},{3,2},{4,5},{5,4},{6,7},{7,6},{8,9},{9,8},{10,11... | collective-permute-start | bytes 208904 | tf_op jit(solution)/shard_map/ppermute | solution.py:615
  2.0 1.3 %collective-permute-start.1 = (bf16[1,272,128]{2,1,0:T(8,128)(2,1)S(1)}, bf16[1,272,128]{2,1,0:T(8,128)(2,1)S(1)}, u32[]{:S(2)}, u32[]{:S(2)}) collective-permute-start(bf16[1,272,128]{2,1,0:T(8,128)(2,1)S(1)} %get-tuple-element.45), channel_id=1, source_target_pairs={{0,1},{1,0},{2,3},{3,2},{4,5},{5,4},{6,7},{7,6},{8,9},{9,8},{10,11... | collective-permute-start | bytes 208904 | tf_op jit(solution)/shard_map/ppermute | solution.py:615
  2.1 3.9 %collective-permute-start.7 = (bf16[2,272,128]{2,1,0:T(8,128)(2,1)S(1)}, bf16[2,272,128]{2,1,0:T(8,128)(2,1)S(1)}, u32[]{:S(2)}, u32[]{:S(2)}) collective-permute-start(bf16[2,272,128]{2,1,0:T(8,128)(2,1)S(1)} %slice.100), channel_id=1, source_target_pairs={{0,1},{1,0},{2,3},{3,2},{4,5},{5,4},{6,7},{7,6},{8,9},{9,8},{10,11... | collective-permute-start | bytes 417800 | tf_op jit(solution)/shard_map/ppermute | solution.py:615
  2.6 5.5 %collective-permute-start = (bf16[4,256,128]{2,1,0:T(8,128)(2,1)S(1)}, bf16[4,256,128]{2,1,0:T(8,128)(2,1)S(1)}, u32[]{:S(2)}, u32[]{:S(2)}) collective-permute-start(bf16[4,256,128]{2,1,0:T(8,128)(2,1)S(1)} %get-tuple-element.24), channel_id=1, source_target_pairs={{0,1},{1,0},{2,3},{3,2},{4,5},{5,4},{6,7},{7,6},{8,9},{9,8},{10,11... | collective-permute-start | bytes 786440 | tf_op jit(solution)/shard_map/ppermute | solution.py:615
  3.3 7.0 %collective-permute-start.2 = (bf16[2,272,128]{2,1,0:T(8,128)(2,1)S(1)}, bf16[2,272,128]{2,1,0:T(8,128)(2,1)S(1)}, u32[]{:S(2)}, u32[]{:S(2)}) collective-permute-start(bf16[2,272,128]{2,1,0:T(8,128)(2,1)S(1)} %pad_maximum_fusion), channel_id=1, source_target_pairs={{0,2},{1,3},{2,0},{3,1},{4,6},{5,7},{6,4},{7,5},{8,10},{9,11},{10,... | collective-permute-start | bytes 417800 | tf_op jit(solution)/shard_map/ppermute | solution.py:632
  6.1 11.7 %collective-permute-start.8 = (bf16[2,272,128]{2,1,0:T(8,128)(2,1)S(1)}, bf16[2,272,128]{2,1,0:T(8,128)(2,1)S(1)}, u32[]{:S(2)}, u32[]{:S(2)}) collective-permute-start(bf16[2,272,128]{2,1,0:T(8,128)(2,1)S(1)} %pad_maximum_fusion.1), channel_id=1, source_target_pairs={{0,4},{1,5},{2,6},{3,7},{4,0},{5,1},{6,2},{7,3},{8,12},{9,13},{10,... | collective-permute-start | bytes 417800 | tf_op jit(solution)/shard_map/ppermute | solution.py:632
  7.7 2.6 %copy-start = (bf16[1,8,16,2048]{3,2,1,0:T(8,128)(2,1)S(1)}, bf16[1,8,16,2048]{3,2,1,0:T(8,128)(2,1)}, u32[]{:S(2)}) copy-start(bf16[1,8,16,2048]{3,2,1,0:T(8,128)(2,1)} %param.3) | copy-start | bytes 1572868
  7.7 10.3 %collective-permute-start.9 = (bf16[2,272,128]{2,1,0:T(8,128)(2,1)S(1)}, bf16[2,272,128]{2,1,0:T(8,128)(2,1)S(1)}, u32[]{:S(2)}, u32[]{:S(2)}) collective-permute-start(bf16[2,272,128]{2,1,0:T(8,128)(2,1)S(1)} %pad_maximum_fusion.2), channel_id=1, source_target_pairs={{0,6},{1,7},{2,4},{3,5},{4,2},{5,3},{6,0},{7,1},{8,14},{9,15},{10,... | collective-permute-start | bytes 417800 | tf_op jit(solution)/shard_map/ppermute | solution.py:632
  8.2 6.2 %copy-start.1 = (f32[1,5,2048]{2,0,1:T(1,128)S(1)}, f32[1,5,2048]{2,0,1:T(1,128)}, u32[]{:S(2)}) copy-start(f32[1,5,2048]{2,0,1:T(1,128)} %param.5) | copy-start | bytes 122884
  10.3 14.7 %collective-permute-start.10 = (bf16[128,2048]{1,0:T(8,128)(2,1)S(1)}, bf16[128,2048]{1,0:T(8,128)(2,1)S(1)}, u32[]{:S(2)}, u32[]{:S(2)}) collective-permute-start(bf16[128,2048]{1,0:T(8,128)(2,1)S(1)} %bitcast.42), channel_id=1, source_target_pairs={{0,24},{8,0},{16,8},{24,16},{1,25},{9,1},{17,9},{25,17},{2,26},{10... | collective-permute-start | bytes 1572872 | tf_op jit(solution)/shard_map/ppermute | solution.py:652
  14.4 6.1 %collective-permute-start.3 = (bf16[2,256,128]{2,1,0:T(8,128)(2,1)S(1)}, bf16[2,256,128]{2,1,0:T(8,128)(2,1)S(1)}, u32[]{:S(2)}, u32[]{:S(2)}) collective-permute-start(bf16[2,256,128]{2,1,0:T(8,128)(2,1)S(1)} %get-tuple-element.27), channel_id=1, source_target_pairs={{0,2},{1,3},{2,0},{3,1},{4,6},{5,7},{6,4},{7,5},{8,10},{9,11},{10,... | collective-permute-start | bytes 393224 | tf_op jit(solution)/shard_map/ppermute | solution.py:632
  16.2 7.5 %collective-permute-start.4 = (bf16[2,256,128]{2,1,0:T(8,128)(2,1)S(1)}, bf16[2,256,128]{2,1,0:T(8,128)(2,1)S(1)}, u32[]{:S(2)}, u32[]{:S(2)}) collective-permute-start(bf16[2,256,128]{2,1,0:T(8,128)(2,1)S(1)} %get-tuple-element.28), channel_id=1, source_target_pairs={{0,4},{1,5},{2,6},{3,7},{4,0},{5,1},{6,2},{7,3},{8,12},{9,13},{10,... | collective-permute-start | bytes 393224 | tf_op jit(solution)/shard_map/ppermute | solution.py:632
  17.7 6.0 %collective-permute-start.5 = (bf16[2,256,128]{2,1,0:T(8,128)(2,1)S(1)}, bf16[2,256,128]{2,1,0:T(8,128)(2,1)S(1)}, u32[]{:S(2)}, u32[]{:S(2)}) collective-permute-start(bf16[2,256,128]{2,1,0:T(8,128)(2,1)S(1)} %pad_maximum_fusion.9), channel_id=1, source_target_pairs={{0,6},{1,7},{2,4},{3,5},{4,2},{5,3},{6,0},{7,1},{8,14},{9,15},{10,... | collective-permute-start | bytes 393224 | tf_op jit(solution)/shard_map/ppermute | solution.py:632
  18.0 7.0 %collective-permute-start.11 = (f16[4,128,128]{2,1,0:T(8,128)(2,1)S(1)}, f16[4,128,128]{2,1,0:T(8,128)(2,1)S(1)}, u32[]{:S(2)}, u32[]{:S(2)}) collective-permute-start(f16[4,128,128]{2,1,0:T(8,128)(2,1)S(1)} %convert_element_type.26), channel_id=1, source_target_pairs={{0,1},{1,0},{2,3},{3,2},{4,5},{5,4},{6,7},{7,6},{8,9},{9,8},{10,11... | collective-permute-start | bytes 393224 | tf_op jit(solution)/shard_map/ppermute | solution.py:670
  25.0 1.4 %collective-permute-start.12 = (f16[4,136,128]{2,1,0:T(8,128)(2,1)S(1)}, f16[4,136,128]{2,1,0:T(8,128)(2,1)S(1)}, u32[]{:S(2)}, u32[]{:S(2)}) collective-permute-start(f16[4,136,128]{2,1,0:T(8,128)(2,1)S(1)} %convert_element_type.27), channel_id=1, source_target_pairs={{0,1},{1,0},{2,3},{3,2},{4,5},{5,4},{6,7},{7,6},{8,9},{9,8},{10,11... | collective-permute-start | bytes 417800 | tf_op jit(solution)/shard_map/ppermute | solution.py:670
  26.5 8.5 %collective-permute-start.13 = (f16[528,128]{1,0:T(8,128)(2,1)S(1)}, f16[528,128]{1,0:T(8,128)(2,1)S(1)}, u32[]{:S(2)}, u32[]{:S(2)}) collective-permute-start(f16[528,128]{1,0:T(8,128)(2,1)S(1)} %pad_maximum_fusion.3), channel_id=1, source_target_pairs={{0,24},{1,25},{2,26},{3,27},{4,28},{5,29},{6,30},{7,31},{8,0},{9,1... | collective-permute-start | bytes 405512 | tf_op jit(solution)/shard_map/ppermute | solution.py:674
  31.1 7.4 %collective-permute-start.14 = (f16[528,128]{1,0:T(8,128)(2,1)S(1)}, f16[528,128]{1,0:T(8,128)(2,1)S(1)}, u32[]{:S(2)}, u32[]{:S(2)}) collective-permute-start(f16[528,128]{1,0:T(8,128)(2,1)S(1)} %pad_maximum_fusion.4), channel_id=1, source_target_pairs={{0,26},{1,27},{2,24},{3,25},{4,30},{5,31},{6,28},{7,29},{8,2},{9,3... | collective-permute-start | bytes 405512 | tf_op jit(solution)/shard_map/ppermute | solution.py:674
  33.0 9.2 %collective-permute-start.15 = (f16[528,128]{1,0:T(8,128)(2,1)S(1)}, f16[528,128]{1,0:T(8,128)(2,1)S(1)}, u32[]{:S(2)}, u32[]{:S(2)}) collective-permute-start(f16[528,128]{1,0:T(8,128)(2,1)S(1)} %pad_maximum_fusion.5), channel_id=1, source_target_pairs={{0,28},{1,29},{2,30},{3,31},{4,24},{5,25},{6,26},{7,27},{8,4},{9,5... | collective-permute-start | bytes 405512 | tf_op jit(solution)/shard_map/ppermute | solution.py:674
  33.2 11.1 %collective-permute-start.16 = (f16[528,128]{1,0:T(8,128)(2,1)S(1)}, f16[528,128]{1,0:T(8,128)(2,1)S(1)}, u32[]{:S(2)}, u32[]{:S(2)}) collective-permute-start(f16[528,128]{1,0:T(8,128)(2,1)S(1)} %pad_maximum_fusion.6), channel_id=1, source_target_pairs={{0,30},{1,31},{2,28},{3,29},{4,26},{5,27},{6,24},{7,25},{8,6},{9,7... | collective-permute-start | bytes 405512 | tf_op jit(solution)/shard_map/ppermute | solution.py:674

commit v5 on v4

--- a/solution.py
+++ b/solution.py
@@ -490,7 +490,7 @@
         if at > 0:
             works += [key_side(at - 1, at)]
         together(*works)
-    together(key_side(rows - 1, rows), all_queries())
+    together(all_queries(), key_side(rows - 1, rows))
     tops, shares = [], []
     for step, slot in blocks:
         here, x, c, inverse = block(step, slot)

time: 45.5 us -> 45.5 us (level)
  no operation moved by 1% of the time
where the time goes in v5:
time: 45.5 us; the launch traced here: 45.3 us
  starting transfers between devices  21.6 us (47%)
  waiting for transfers between devices  20 us (44%)
  Pallas kernels  2.87 us (6%)
  other arithmetic  0.46 us (1%)
    ppermute x4, waiting for transfers between devices, split_heads_per_device(): lax.ppermute(sent, ('pipe',) + plane, crossing_back((pipes, rows, cols),...  9.3 us
    ppermute x6, starting transfers between devices, split_heads_per_device(): lax.ppermute(packets[step - 1], plane, crossing(sizes, step, 0))  8.3 us
    ppermute x4, starting transfers between devices, split_heads_per_device(): lax.ppermute(sent, ('pipe',) + plane, crossing_back((pipes, rows, cols),...  7.86 us
    ppermute x6, waiting for transfers between devices, split_heads_per_device(): lax.ppermute(packets[step - 1], plane, crossing(sizes, step, 0))  7.67 us
    ppermute x1, starting transfers between devices, split_heads_per_device(): x_ahead = lax.ppermute(free_x, 'pipe', behind)  4.1 us
    pallas_call x1, Pallas kernels, split_heads_per_device(): local_call(functools.partial(pack_kernel, rows, heads), packets, staged,...  1.49 us
    ppermute x2, waiting for transfers between devices, split_heads_per_device(): lax.ppermute(given.astype(jnp.float16), plane, crossing(sizes, 0, 1))  1.3 us
    ppermute x4, starting transfers between devices, swap(): return lax.ppermute(array, plane, crossing(sizes, 0, 1))  1.17 us
  transfers between devices with their start and end apart: 17, of which 10 were waited for; matrix products, arithmetic and copies ran while one was open for 1% of the time, Pallas kernels for 1%

profile of v5, /device:TPU:0, one launch (start us, length us, event | category | flops | bytes accessed | tf_op | source)
XLA Modules:
  0.0 45.3 jit_solution(16414519264164329092)
XLA Ops:
  0.0 1.5 %shard_map.37 = (bf16[4,272,128]{2,1,0:T(8,128)(2,1)S(1)}, bf16[4,272,128]{2,1,0:T(8,128)(2,1)S(1)}, bf16[4,256,128]{2,1,0:T(8,128)(2,1)S(1)}, bf16[4,256,128]{2,1,0:T(8,128)(2,1)S(1)}) custom-call(bf16[128,2048]{1,0:T(8,128)(2,1)} %bitcast.41, bf16[128,2048]{1,0:T(8,128)(2,1)} %bitcast.40), custom_call_target="tpu_custom_call" | custom-call | tf_op jit(solution)/shard_map/pallas_call | solution.py:610
  1.5 0.5 %collective-permute-start.6 = (bf16[1,272,128]{2,1,0:T(8,128)(2,1)S(1)}, bf16[1,272,128]{2,1,0:T(8,128)(2,1)S(1)}, u32[]{:S(2)}, u32[]{:S(2)}) collective-permute-start(bf16[1,272,128]{2,1,0:T(8,128)(2,1)S(1)} %get-tuple-element.44), channel_id=1, source_target_pairs={{0,1},{1,0},{2,3},{3,2},{4,5},{5,4},{6,7},{7,6},{8,9},{9,8},{10,11... | collective-permute-start | bytes 208904 | tf_op jit(solution)/shard_map/ppermute | solution.py:615
  2.0 0.1 collective-permute-start.1
  2.1 0.5 %collective-permute-start.7 = (bf16[2,272,128]{2,1,0:T(8,128)(2,1)S(1)}, bf16[2,272,128]{2,1,0:T(8,128)(2,1)S(1)}, u32[]{:S(2)}, u32[]{:S(2)}) collective-permute-start(bf16[2,272,128]{2,1,0:T(8,128)(2,1)S(1)} %slice.100), channel_id=1, source_target_pairs={{0,1},{1,0},{2,3},{3,2},{4,5},{5,4},{6,7},{7,6},{8,9},{9,8},{10,11... | collective-permute-start | bytes 417800 | tf_op jit(solution)/shard_map/ppermute | solution.py:615
  2.6 0.1 collective-permute-start
  2.7 0.6 %collective-permute-done.1 = bf16[1,272,128]{2,1,0:T(8,128)(2,1)S(1)} collective-permute-done((bf16[1,272,128]{2,1,0:T(8,128)(2,1)S(1)}, bf16[1,272,128]{2,1,0:T(8,128)(2,1)S(1)}, u32[]{:S(2)}, u32[]{:S(2)}) %collective-permute-start.1) | collective-permute-done | bytes 69664 | tf_op jit(solution)/shard_map/ppermute | solution.py:615
  3.3 2.7 %collective-permute-start.2 = (bf16[2,272,128]{2,1,0:T(8,128)(2,1)S(1)}, bf16[2,272,128]{2,1,0:T(8,128)(2,1)S(1)}, u32[]{:S(2)}, u32[]{:S(2)}) collective-permute-start(bf16[2,272,128]{2,1,0:T(8,128)(2,1)S(1)} %pad_maximum_fusion), channel_id=1, source_target_pairs={{0,2},{1,3},{2,0},{3,1},{4,6},{5,7},{6,4},{7,5},{8,10},{9,11},{10,... | collective-permute-start | bytes 417800 | tf_op jit(solution)/shard_map/ppermute | solution.py:632
  6.0 0.0 collective-permute-done.7
  6.1 1.6 %collective-permute-start.8 = (bf16[2,272,128]{2,1,0:T(8,128)(2,1)S(1)}, bf16[2,272,128]{2,1,0:T(8,128)(2,1)S(1)}, u32[]{:S(2)}, u32[]{:S(2)}) collective-permute-start(bf16[2,272,128]{2,1,0:T(8,128)(2,1)S(1)} %pad_maximum_fusion.1), channel_id=1, source_target_pairs={{0,4},{1,5},{2,6},{3,7},{4,0},{5,1},{6,2},{7,3},{8,12},{9,13},{10,... | collective-permute-start | bytes 417800 | tf_op jit(solution)/shard_map/ppermute | solution.py:632
  7.7 0.0 copy-start
  7.7 0.5 collective-permute-start.9
  8.1 0.0 collective-permute-done.operands_2_
  8.2 0.0 copy-start.1
  8.2 2.1 %collective-permute-done.2.operands_3_ = bf16[2,272,128]{2,1,0:T(8,128)(2,1)S(1)} collective-permute-done((bf16[2,272,128]{2,1,0:T(8,128)(2,1)S(1)}, bf16[2,272,128]{2,1,0:T(8,128)(2,1)S(1)}, u32[]{:S(2)}, u32[]{:S(2)}) %collective-permute-start.2) | collective-permute-done | bytes 139296 | tf_op jit(solution)/shard_map/ppermute | solution.py:632
  10.3 0.0 copy-done
  10.3 4.1 %collective-permute-start.10 = (bf16[128,2048]{1,0:T(8,128)(2,1)S(1)}, bf16[128,2048]{1,0:T(8,128)(2,1)S(1)}, u32[]{:S(2)}, u32[]{:S(2)}) collective-permute-start(bf16[128,2048]{1,0:T(8,128)(2,1)S(1)} %bitcast.42), channel_id=1, source_target_pairs={{0,24},{8,0},{16,8},{24,16},{1,25},{9,1},{17,9},{25,17},{2,26},{10... | collective-permute-start | bytes 1572872 | tf_op jit(solution)/shard_map/ppermute | solution.py:652
  14.4 0.0 copy-done.1
  14.4 1.8 %collective-permute-start.3 = (bf16[2,256,128]{2,1,0:T(8,128)(2,1)S(1)}, bf16[2,256,128]{2,1,0:T(8,128)(2,1)S(1)}, u32[]{:S(2)}, u32[]{:S(2)}) collective-permute-start(bf16[2,256,128]{2,1,0:T(8,128)(2,1)S(1)} %get-tuple-element.27), channel_id=1, source_target_pairs={{0,2},{1,3},{2,0},{3,1},{4,6},{5,7},{6,4},{7,5},{8,10},{9,11},{10,... | collective-permute-start | bytes 393224 | tf_op jit(solution)/shard_map/ppermute | solution.py:632
  16.2 0.0 collective-permute-done.6.operands_2_
  16.2 1.5 %collective-permute-start.4 = (bf16[2,256,128]{2,1,0:T(8,128)(2,1)S(1)}, bf16[2,256,128]{2,1,0:T(8,128)(2,1)S(1)}, u32[]{:S(2)}, u32[]{:S(2)}) collective-permute-start(bf16[2,256,128]{2,1,0:T(8,128)(2,1)S(1)} %get-tuple-element.28), channel_id=1, source_target_pairs={{0,4},{1,5},{2,6},{3,7},{4,0},{5,1},{6,2},{7,3},{8,12},{9,13},{10,... | collective-permute-start | bytes 393224 | tf_op jit(solution)/shard_map/ppermute | solution.py:632
  17.7 0.0 collective-permute-done.8.operands_4_
  17.7 0.2 collective-permute-start.5
  18.0 0.0 collective-permute-done.9.operands_5_
  18.0 0.1 collective-permute-start.11
  18.1 2.4 %collective-permute-done.3.operands_3_ = bf16[2,256,128]{2,1,0:T(8,128)(2,1)S(1)} collective-permute-done((bf16[2,256,128]{2,1,0:T(8,128)(2,1)S(1)}, bf16[2,256,128]{2,1,0:T(8,128)(2,1)S(1)}, u32[]{:S(2)}, u32[]{:S(2)}) %collective-permute-start.3) | collective-permute-done | bytes 131104 | tf_op jit(solution)/shard_map/ppermute | solution.py:632
  20.5 3.2 %collective-permute-done.4.operands_4_ = bf16[2,256,128]{2,1,0:T(8,128)(2,1)S(1)} collective-permute-done((bf16[2,256,128]{2,1,0:T(8,128)(2,1)S(1)}, bf16[2,256,128]{2,1,0:T(8,128)(2,1)S(1)}, u32[]{:S(2)}, u32[]{:S(2)}) %collective-permute-start.4) | collective-permute-done | bytes 131104 | tf_op jit(solution)/shard_map/ppermute | solution.py:632
  23.7 0.0 collective-permute-done.5.operands_5_
  23.8 1.1 %collective-permute-done.10.x_ref = bf16[128,2048]{1,0:T(8,128)(2,1)S(1)} collective-permute-done((bf16[128,2048]{1,0:T(8,128)(2,1)S(1)}, bf16[128,2048]{1,0:T(8,128)(2,1)S(1)}, u32[]{:S(2)}, u32[]{:S(2)}) %collective-permute-start.10) | collective-permute-done | bytes 524320 | tf_op jit(solution)/shard_map/ppermute | solution.py:652
  25.0 0.1 collective-permute-start.12
  25.1 0.0 collective-permute-done.11
  25.1 1.3 %collective-permute-done.12 = f16[4,136,128]{2,1,0:T(8,128)(2,1)S(1)} collective-permute-done((f16[4,136,128]{2,1,0:T(8,128)(2,1)S(1)}, f16[4,136,128]{2,1,0:T(8,128)(2,1)S(1)}, u32[]{:S(2)}, u32[]{:S(2)}) %collective-permute-start.12) | collective-permute-done | bytes 139296 | tf_op jit(solution)/shard_map/ppermute | solution.py:670
  26.4 0.1 pad_maximum_fusion.3
  26.5 4.5 %collective-permute-start.13 = (f16[528,128]{1,0:T(8,128)(2,1)S(1)}, f16[528,128]{1,0:T(8,128)(2,1)S(1)}, u32[]{:S(2)}, u32[]{:S(2)}) collective-permute-start(f16[528,128]{1,0:T(8,128)(2,1)S(1)} %pad_maximum_fusion.3), channel_id=1, source_target_pairs={{0,24},{1,25},{2,26},{3,27},{4,28},{5,29},{6,30},{7,31},{8,0},{9,1... | collective-permute-start | bytes 405512 | tf_op jit(solution)/shard_map/ppermute | solution.py:674
  31.0 0.1 pad_maximum_fusion.4
  31.1 1.9 %collective-permute-start.14 = (f16[528,128]{1,0:T(8,128)(2,1)S(1)}, f16[528,128]{1,0:T(8,128)(2,1)S(1)}, u32[]{:S(2)}, u32[]{:S(2)}) collective-permute-start(f16[528,128]{1,0:T(8,128)(2,1)S(1)} %pad_maximum_fusion.4), channel_id=1, source_target_pairs={{0,26},{1,27},{2,24},{3,25},{4,30},{5,31},{6,28},{7,29},{8,2},{9,3... | collective-permute-start | bytes 405512 | tf_op jit(solution)/shard_map/ppermute | solution.py:674
  33.0 0.1 pad_maximum_fusion.5
  33.0 0.1 collective-permute-start.15
  33.1 0.1 pad_maximum_fusion.6
  33.1 1.4 %collective-permute-start.16 = (f16[528,128]{1,0:T(8,128)(2,1)S(1)}, f16[528,128]{1,0:T(8,128)(2,1)S(1)}, u32[]{:S(2)}, u32[]{:S(2)}) collective-permute-start(f16[528,128]{1,0:T(8,128)(2,1)S(1)} %pad_maximum_fusion.6), channel_id=1, source_target_pairs={{0,30},{1,31},{2,28},{3,29},{4,26},{5,27},{6,24},{7,25},{8,6},{9,7... | collective-permute-start | bytes 405512 | tf_op jit(solution)/shard_map/ppermute | solution.py:674
  34.5 0.3 shard_map.40.x_ref
  34.9 0.1 collective-permute-done.13
  35.0 3.5 %collective-permute-done.14 = f16[528,128]{1,0:T(8,128)(2,1)S(1)} collective-permute-done((f16[528,128]{1,0:T(8,128)(2,1)S(1)}, f16[528,128]{1,0:T(8,128)(2,1)S(1)}, u32[]{:S(2)}, u32[]{:S(2)}) %collective-permute-start.14) | collective-permute-done | bytes 135200 | tf_op jit(solution)/shard_map/ppermute | solution.py:674
  38.5 3.7 %collective-permute-done.15 = f16[528,128]{1,0:T(8,128)(2,1)S(1)} collective-permute-done((f16[528,128]{1,0:T(8,128)(2,1)S(1)}, f16[528,128]{1,0:T(8,128)(2,1)S(1)}, u32[]{:S(2)}, u32[]{:S(2)}) %collective-permute-start.15) | collective-permute-done | bytes 135200 | tf_op jit(solution)/shard_map/ppermute | solution.py:674
  42.2 2.0 %collective-permute-done.16 = f16[528,128]{1,0:T(8,128)(2,1)S(1)} collective-permute-done((f16[528,128]{1,0:T(8,128)(2,1)S(1)}, f16[528,128]{1,0:T(8,128)(2,1)S(1)}, u32[]{:S(2)}, u32[]{:S(2)}) %collective-permute-start.16) | collective-permute-done | bytes 135200 | tf_op jit(solution)/shard_map/ppermute | solution.py:674
  44.3 1.1 %shard_map.41 = bf16[128,2048]{1,0:T(8,128)(2,1)} custom-call(f32[128,2048]{1,0:T(8,128)S(1)} %shard_map.40.x_ref, f32[528,128]{1,0:T(8,128)S(1)} %convert_element_type.28.refs_0_, f32[528,128]{1,0:T(8,128)S(1)} %convert_element_type.29.refs_1_, f32[528,128]{1,0:T(8,128)S(1)} %convert_element_type.30.refs_2_, f32[528,128]{1,0:T(8,128)S(1)} %convert_element_type.31.refs_3_), custom_call_target="tpu_custom_call" | custom-call | tf_op jit(solution)/shard_map/pallas_call | solution.py:677
  (26 shorter events, 0.5 us)
Async XLA Ops:
  1.5 14.7 %collective-permute-start.6 = (bf16[1,272,128]{2,1,0:T(8,128)(2,1)S(1)}, bf16[1,272,128]{2,1,0:T(8,128)(2,1)S(1)}, u32[]{:S(2)}, u32[]{:S(2)}) collective-permute-start(bf16[1,272,128]{2,1,0:T(8,128)(2,1)S(1)} %get-tuple-element.44), channel_id=1, source_target_pairs={{0,1},{1,0},{2,3},{3,2},{4,5},{5,4},{6,7},{7,6},{8,9},{9,8},{10,11... | collective-permute-start | bytes 208904 | tf_op jit(solution)/shard_map/ppermute | solution.py:615
  2.0 1.3 %collective-permute-start.1 = (bf16[1,272,128]{2,1,0:T(8,128)(2,1)S(1)}, bf16[1,272,128]{2,1,0:T(8,128)(2,1)S(1)}, u32[]{:S(2)}, u32[]{:S(2)}) collective-permute-start(bf16[1,272,128]{2,1,0:T(8,128)(2,1)S(1)} %get-tuple-element.45), channel_id=1, source_target_pairs={{0,1},{1,0},{2,3},{3,2},{4,5},{5,4},{6,7},{7,6},{8,9},{9,8},{10,11... | collective-permute-start | bytes 208904 | tf_op jit(solution)/shard_map/ppermute | solution.py:615
  2.1 3.9 %collective-permute-start.7 = (bf16[2,272,128]{2,1,0:T(8,128)(2,1)S(1)}, bf16[2,272,128]{2,1,0:T(8,128)(2,1)S(1)}, u32[]{:S(2)}, u32[]{:S(2)}) collective-permute-start(bf16[2,272,128]{2,1,0:T(8,128)(2,1)S(1)} %slice.100), channel_id=1, source_target_pairs={{0,1},{1,0},{2,3},{3,2},{4,5},{5,4},{6,7},{7,6},{8,9},{9,8},{10,11... | collective-permute-start | bytes 417800 | tf_op jit(solution)/shard_map/ppermute | solution.py:615
  2.6 5.5 %collective-permute-start = (bf16[4,256,128]{2,1,0:T(8,128)(2,1)S(1)}, bf16[4,256,128]{2,1,0:T(8,128)(2,1)S(1)}, u32[]{:S(2)}, u32[]{:S(2)}) collective-permute-start(bf16[4,256,128]{2,1,0:T(8,128)(2,1)S(1)} %get-tuple-element.24), channel_id=1, source_target_pairs={{0,1},{1,0},{2,3},{3,2},{4,5},{5,4},{6,7},{7,6},{8,9},{9,8},{10,11... | collective-permute-start | bytes 786440 | tf_op jit(solution)/shard_map/ppermute | solution.py:615
  3.3 7.0 %collective-permute-start.2 = (bf16[2,272,128]{2,1,0:T(8,128)(2,1)S(1)}, bf16[2,272,128]{2,1,0:T(8,128)(2,1)S(1)}, u32[]{:S(2)}, u32[]{:S(2)}) collective-permute-start(bf16[2,272,128]{2,1,0:T(8,128)(2,1)S(1)} %pad_maximum_fusion), channel_id=1, source_target_pairs={{0,2},{1,3},{2,0},{3,1},{4,6},{5,7},{6,4},{7,5},{8,10},{9,11},{10,... | collective-permute-start | bytes 417800 | tf_op jit(solution)/shard_map/ppermute | solution.py:632
  6.1 11.7 %collective-permute-start.8 = (bf16[2,272,128]{2,1,0:T(8,128)(2,1)S(1)}, bf16[2,272,128]{2,1,0:T(8,128)(2,1)S(1)}, u32[]{:S(2)}, u32[]{:S(2)}) collective-permute-start(bf16[2,272,128]{2,1,0:T(8,128)(2,1)S(1)} %pad_maximum_fusion.1), channel_id=1, source_target_pairs={{0,4},{1,5},{2,6},{3,7},{4,0},{5,1},{6,2},{7,3},{8,12},{9,13},{10,... | collective-permute-start | bytes 417800 | tf_op jit(solution)/shard_map/ppermute | solution.py:632
  7.7 2.6 %copy-start = (bf16[1,8,16,2048]{3,2,1,0:T(8,128)(2,1)S(1)}, bf16[1,8,16,2048]{3,2,1,0:T(8,128)(2,1)}, u32[]{:S(2)}) copy-start(bf16[1,8,16,2048]{3,2,1,0:T(8,128)(2,1)} %param.3) | copy-start | bytes 1572868
  7.7 10.3 %collective-permute-start.9 = (bf16[2,272,128]{2,1,0:T(8,128)(2,1)S(1)}, bf16[2,272,128]{2,1,0:T(8,128)(2,1)S(1)}, u32[]{:S(2)}, u32[]{:S(2)}) collective-permute-start(bf16[2,272,128]{2,1,0:T(8,128)(2,1)S(1)} %pad_maximum_fusion.2), channel_id=1, source_target_pairs={{0,6},{1,7},{2,4},{3,5},{4,2},{5,3},{6,0},{7,1},{8,14},{9,15},{10,... | collective-permute-start | bytes 417800 | tf_op jit(solution)/shard_map/ppermute | solution.py:632
  8.2 6.2 %copy-start.1 = (f32[1,5,2048]{2,0,1:T(1,128)S(1)}, f32[1,5,2048]{2,0,1:T(1,128)}, u32[]{:S(2)}) copy-start(f32[1,5,2048]{2,0,1:T(1,128)} %param.5) | copy-start | bytes 122884
  10.3 14.7 %collective-permute-start.10 = (bf16[128,2048]{1,0:T(8,128)(2,1)S(1)}, bf16[128,2048]{1,0:T(8,128)(2,1)S(1)}, u32[]{:S(2)}, u32[]{:S(2)}) collective-permute-start(bf16[128,2048]{1,0:T(8,128)(2,1)S(1)} %bitcast.42), channel_id=1, source_target_pairs={{0,24},{8,0},{16,8},{24,16},{1,25},{9,1},{17,9},{25,17},{2,26},{10... | collective-permute-start | bytes 1572872 | tf_op jit(solution)/shard_map/ppermute | solution.py:652
  14.4 6.1 %collective-permute-start.3 = (bf16[2,256,128]{2,1,0:T(8,128)(2,1)S(1)}, bf16[2,256,128]{2,1,0:T(8,128)(2,1)S(1)}, u32[]{:S(2)}, u32[]{:S(2)}) collective-permute-start(bf16[2,256,128]{2,1,0:T(8,128)(2,1)S(1)} %get-tuple-element.27), channel_id=1, source_target_pairs={{0,2},{1,3},{2,0},{3,1},{4,6},{5,7},{6,4},{7,5},{8,10},{9,11},{10,... | collective-permute-start | bytes 393224 | tf_op jit(solution)/shard_map/ppermute | solution.py:632
  16.2 7.5 %collective-permute-start.4 = (bf16[2,256,128]{2,1,0:T(8,128)(2,1)S(1)}, bf16[2,256,128]{2,1,0:T(8,128)(2,1)S(1)}, u32[]{:S(2)}, u32[]{:S(2)}) collective-permute-start(bf16[2,256,128]{2,1,0:T(8,128)(2,1)S(1)} %get-tuple-element.28), channel_id=1, source_target_pairs={{0,4},{1,5},{2,6},{3,7},{4,0},{5,1},{6,2},{7,3},{8,12},{9,13},{10,... | collective-permute-start | bytes 393224 | tf_op jit(solution)/shard_map/ppermute | solution.py:632
  17.7 6.0 %collective-permute-start.5 = (bf16[2,256,128]{2,1,0:T(8,128)(2,1)S(1)}, bf16[2,256,128]{2,1,0:T(8,128)(2,1)S(1)}, u32[]{:S(2)}, u32[]{:S(2)}) collective-permute-start(bf16[2,256,128]{2,1,0:T(8,128)(2,1)S(1)} %pad_maximum_fusion.9), channel_id=1, source_target_pairs={{0,6},{1,7},{2,4},{3,5},{4,2},{5,3},{6,0},{7,1},{8,14},{9,15},{10,... | collective-permute-start | bytes 393224 | tf_op jit(solution)/shard_map/ppermute | solution.py:632
  18.0 7.0 %collective-permute-start.11 = (f16[4,128,128]{2,1,0:T(8,128)(2,1)S(1)}, f16[4,128,128]{2,1,0:T(8,128)(2,1)S(1)}, u32[]{:S(2)}, u32[]{:S(2)}) collective-permute-start(f16[4,128,128]{2,1,0:T(8,128)(2,1)S(1)} %convert_element_type.26), channel_id=1, source_target_pairs={{0,1},{1,0},{2,3},{3,2},{4,5},{5,4},{6,7},{7,6},{8,9},{9,8},{10,11... | collective-permute-start | bytes 393224 | tf_op jit(solution)/shard_map/ppermute | solution.py:670
  25.0 1.4 %collective-permute-start.12 = (f16[4,136,128]{2,1,0:T(8,128)(2,1)S(1)}, f16[4,136,128]{2,1,0:T(8,128)(2,1)S(1)}, u32[]{:S(2)}, u32[]{:S(2)}) collective-permute-start(f16[4,136,128]{2,1,0:T(8,128)(2,1)S(1)} %convert_element_type.27), channel_id=1, source_target_pairs={{0,1},{1,0},{2,3},{3,2},{4,5},{5,4},{6,7},{7,6},{8,9},{9,8},{10,11... | collective-permute-start | bytes 417800 | tf_op jit(solution)/shard_map/ppermute | solution.py:670
  26.5 8.4 %collective-permute-start.13 = (f16[528,128]{1,0:T(8,128)(2,1)S(1)}, f16[528,128]{1,0:T(8,128)(2,1)S(1)}, u32[]{:S(2)}, u32[]{:S(2)}) collective-permute-start(f16[528,128]{1,0:T(8,128)(2,1)S(1)} %pad_maximum_fusion.3), channel_id=1, source_target_pairs={{0,24},{1,25},{2,26},{3,27},{4,28},{5,29},{6,30},{7,31},{8,0},{9,1... | collective-permute-start | bytes 405512 | tf_op jit(solution)/shard_map/ppermute | solution.py:674
  31.1 7.4 %collective-permute-start.14 = (f16[528,128]{1,0:T(8,128)(2,1)S(1)}, f16[528,128]{1,0:T(8,128)(2,1)S(1)}, u32[]{:S(2)}, u32[]{:S(2)}) collective-permute-start(f16[528,128]{1,0:T(8,128)(2,1)S(1)} %pad_maximum_fusion.4), channel_id=1, source_target_pairs={{0,26},{1,27},{2,24},{3,25},{4,30},{5,31},{6,28},{7,29},{8,2},{9,3... | collective-permute-start | bytes 405512 | tf_op jit(solution)/shard_map/ppermute | solution.py:674
  33.0 9.2 %collective-permute-start.15 = (f16[528,128]{1,0:T(8,128)(2,1)S(1)}, f16[528,128]{1,0:T(8,128)(2,1)S(1)}, u32[]{:S(2)}, u32[]{:S(2)}) collective-permute-start(f16[528,128]{1,0:T(8,128)(2,1)S(1)} %pad_maximum_fusion.5), channel_id=1, source_target_pairs={{0,28},{1,29},{2,30},{3,31},{4,24},{5,25},{6,26},{7,27},{8,4},{9,5... | collective-permute-start | bytes 405512 | tf_op jit(solution)/shard_map/ppermute | solution.py:674
  33.1 11.1 %collective-permute-start.16 = (f16[528,128]{1,0:T(8,128)(2,1)S(1)}, f16[528,128]{1,0:T(8,128)(2,1)S(1)}, u32[]{:S(2)}, u32[]{:S(2)}) collective-permute-start(f16[528,128]{1,0:T(8,128)(2,1)S(1)} %pad_maximum_fusion.6), channel_id=1, source_target_pairs={{0,30},{1,31},{2,28},{3,29},{4,26},{5,27},{6,24},{7,25},{8,6},{9,7... | collective-permute-start | bytes 405512 | tf_op jit(solution)/shard_map/ppermute | solution.py:674
